TPU v7x, 32 devices: a whole 2x2x4 slice. The times are simulated.
32 devices in a mesh: replica: 4 (over z), shard: 8 (over y, x, core).
Axes of the slice: x: 2, y: 2, z: 4, core: 2. Of those that a mesh axis runs over, the one named last changes fastest.
Arguments:
- hidden_in: bfloat16 [6144, 2304], P(('replica', 'shard')), may hold values from -16 to 16
- cotangent: bfloat16 [6144, 2304], P(('replica', 'shard')), may hold values from -6 to 6
- token_segment: int32 [6144], P('replica'), may hold values from 0 to 12, as said below
- token_valid: int32 [6144], P('replica'), may hold values from 0 to 1, as said below
- segment_parent: int32 [4, 13], P('replica'), may hold values from 0 to 4, as said below
- query_weight: bfloat16 [2048, 2304], P('shard'), may hold values from -0.125 to 0.125
- key_weight: bfloat16 [1024, 2304], P('shard'), may hold values from -0.125 to 0.125
- value_weight: bfloat16 [1024, 2304], P('shard'), may hold values from -0.125 to 0.125
- output_weight: bfloat16 [2048, 2304], P('shard'), may hold values from -0.125 to 0.125
- gate_weight: bfloat16 [9216, 2304], P('shard'), may hold values from -0.125 to 0.125
- up_weight: bfloat16 [9216, 2304], P('shard'), may hold values from -0.125 to 0.125
- down_weight: bfloat16 [9216, 2304], P('shard'), may hold values from -0.0625 to 0.0625
- attention_gain: float32 [2304], replicated, may hold values from -1.2 to 1.2
- attention_post_gain: float32 [2304], replicated, may hold values from -1.2 to 1.2
- feedforward_gain: float32 [2304], replicated, may hold values from -1.2 to 1.2
- feedforward_post_gain: float32 [2304], replicated, may hold values from -1.2 to 1.2
Outputs:
- block_out: bfloat16 [6144, 2304], P(('replica', 'shard'))
- input_grad: float32 [6144, 2304], P(('replica', 'shard'))
- query_grad: float32 [2048, 2304], P('shard')
- key_grad: float32 [1024, 2304], P('shard')
- value_grad: float32 [1024, 2304], P('shard')
- output_grad: float32 [2048, 2304], P('shard')
- gate_grad: float32 [9216, 2304], P('shard')
- up_grad: float32 [9216, 2304], P('shard')
- down_grad: float32 [9216, 2304], P('shard')
- attention_gain_grad: float32 [2304], replicated
- attention_post_gain_grad: float32 [2304], replicated
- feedforward_gain_grad: float32 [2304], replicated
- feedforward_post_gain_grad: float32 [2304], replicated
- stream_rms: float32 [4], replicated
Inputs may be any that keep to these rules, and one draw needn't show every extreme that they name: `token_segment`: segment numbers never fall along a tree's 1536 token slots; each segment has one or more valid tokens; tokens with valid 0 stand at the end of their tree, in segment 13 - 1. `token_valid`: each tree ends in one or more padding tokens. `segment_parent`: row b is tree b's table: segment 0 is the trunk and its own parent, segments 1 to 4 are branches with parent 0, and each branch is the parent of exactly two of the leaves 5 to 12.
All inputs are finite; a program needn't handle non-finite values.
Results may differ from a plain program's by a relative error of at most 0.015.
Values may be sent and summed in bfloat16 or wider, within the bound.
A program may use at most 320 MiB of HBM per device.

v0:
```python
import jax
import jax.numpy as jnp
from jax import lax
from jax.sharding import PartitionSpec as P

HEADS = 8
KV_HEADS = 4
HEAD = 256


norm_eps = 1e-06
score_cap = 50.0


def norm_rows(stream, norm_gain):
    factor = lax.rsqrt(jnp.mean(stream * stream, axis=-1, keepdims=True) + norm_eps)
    return stream * factor * (1.0 + norm_gain)


def rotate(values, cos_table, sin_table):
    half_width = values.shape[-1] // 2
    turned = jnp.concatenate([-values[..., half_width:], values[..., :half_width]], axis=-1)
    return values * cos_table + turned * sin_table


def rotate_back(gradient, cos_table, sin_table):
    half_width = gradient.shape[-1] // 2
    shifted = gradient * sin_table
    unturned = jnp.concatenate([shifted[..., half_width:], -shifted[..., :half_width]], axis=-1)
    return gradient * cos_table + unturned


def rope_tables(position, head_size):
    half_width = head_size // 2
    frequency = jnp.power(10000.0, -jnp.arange(half_width, dtype=jnp.float32) * 2.0 / head_size)
    angles = position.astype(jnp.float32)[:, None] * frequency[None, :]
    angles = jnp.concatenate([angles, angles], axis=-1)[:, None, :]
    return (jnp.cos(angles), jnp.sin(angles))


def tree_tables(segment, valid_mask, parent):
    labels = jnp.arange(parent.shape[0], dtype=jnp.int32)
    member = (segment[:, None] == labels[None, :]).astype(jnp.int32)
    lengths = jnp.sum(member * valid_mask[:, None], axis=0)
    starts = jnp.sum((segment[:, None] < labels[None, :]).astype(jnp.int32), axis=0)
    parent_of = (parent[:, None] == labels[None, :]).astype(jnp.int32)
    grandparent = jnp.sum(parent_of * parent[None, :], axis=1)
    parent_len = jnp.sum(parent_of * lengths[None, :], axis=1)
    grand_of = (grandparent[:, None] == labels[None, :]).astype(jnp.int32)
    grand_len = jnp.sum(grand_of * lengths[None, :], axis=1)
    offsets = jnp.where(parent != labels, parent_len, 0) + jnp.where(
        grandparent != parent, grand_len, 0
    )
    token_index = jnp.arange(segment.shape[0], dtype=jnp.int32)
    position = jnp.sum(member * (offsets - starts)[None, :], axis=1) + token_index
    parent_tok = jnp.sum(member * parent[None, :], axis=1)
    grand_tok = jnp.sum(member * grandparent[None, :], axis=1)
    return (position, parent_tok, grand_tok)


def allowed_mask(query_index, query_seg, query_parent, query_grand, key_index, key_seg, key_valid):
    lineage = (
        (key_seg[None, :] == query_seg[:, None])
        | (key_seg[None, :] == query_parent[:, None])
        | (key_seg[None, :] == query_grand[:, None])
    )
    earlier = (key_seg[None, :] != query_seg[:, None]) | (key_index[None, :] < query_index[:, None])
    itself = key_index[None, :] == query_index[:, None]
    return itself | (key_valid[None, :] == 1) & lineage & earlier


def softmax_parts(scores, allowed):
    capped = score_cap * jnp.tanh(scores / score_cap)
    held = jnp.where(allowed, capped, -1000000000.0)
    largest = jnp.max(held, axis=-1, keepdims=True)
    raised = jnp.where(allowed, jnp.exp(held - largest), 0.0)
    total_mass = jnp.sum(raised, axis=-1, keepdims=True)
    return (raised / total_mass, largest + jnp.log(total_mass))


def gated_gelu(gate_lin, up_lin):
    return jax.nn.gelu(gate_lin, approximate=True) * up_lin


def collect_attention(query_weight, key_weight, value_weight, output_weight):
    return (
        lax.all_gather(query_weight, "shard", axis=0, tiled=True),
        lax.all_gather(key_weight, "shard", axis=0, tiled=True),
        lax.all_gather(value_weight, "shard", axis=0, tiled=True),
        lax.all_gather(output_weight, "shard", axis=0, tiled=True),
    )


def group_rows(values):
    return lax.all_gather(values, "shard", axis=0, tiled=True)


def group_sums(values):
    return lax.psum_scatter(values, "shard", scatter_dimension=0, tiled=True)


def shards(
    hidden_in,
    cotangent,
    token_segment,
    token_valid,
    segment_parent,
    query_weight,
    key_weight,
    value_weight,
    output_weight,
    gate_weight,
    up_weight,
    down_weight,
    attention_gain,
    attention_post_gain,
    feedforward_gain,
    feedforward_post_gain,
):
    row_count, model_width = hidden_in.shape
    group_size = HEADS // KV_HEADS
    row_start = lax.axis_index("shard") * row_count
    tree_size = token_segment.shape[0]
    position, parent_tok, grand_tok = tree_tables(token_segment, token_valid, segment_parent[0])
    key_index = jnp.arange(tree_size, dtype=jnp.int32)

    def own_rows(table):
        return lax.dynamic_slice_in_dim(table, row_start, row_count)

    allowed = allowed_mask(
        own_rows(key_index),
        own_rows(token_segment),
        own_rows(parent_tok),
        own_rows(grand_tok),
        key_index,
        token_segment,
        token_valid,
    )
    mask_full = allowed[None, None]
    cos_table, sin_table = rope_tables(own_rows(position), HEAD)
    query_scale = HEAD ** (-0.5)
    valid_rows = own_rows(token_valid).astype(jnp.float32)
    stream = hidden_in.astype(jnp.float32)
    query_all, key_all, value_all, output_all = collect_attention(
        query_weight, key_weight, value_weight, output_weight
    )
    normed_in = norm_rows(stream, attention_gain).astype(jnp.bfloat16)
    query_lin = jnp.einsum("td,qd->tq", normed_in, query_all, preferred_element_type=jnp.float32)
    key_lin = jnp.einsum("td,qd->tq", normed_in, key_all, preferred_element_type=jnp.float32)
    value_lin = jnp.einsum("td,qd->tq", normed_in, value_all, preferred_element_type=jnp.float32)
    queries = (
        rotate(query_lin.reshape(row_count, HEADS, HEAD), cos_table, sin_table) * query_scale
    ).astype(jnp.bfloat16)
    keys_own = (
        rotate(key_lin.reshape(row_count, KV_HEADS, HEAD), cos_table, sin_table)
        .astype(jnp.bfloat16)
        .reshape(row_count, KV_HEADS * HEAD)
    )
    values_own = value_lin.astype(jnp.bfloat16)
    key_tree, value_tree = (
        lax.all_gather(keys_own, "shard", axis=0, tiled=True),
        lax.all_gather(values_own, "shard", axis=0, tiled=True),
    )
    query_groups = queries.reshape(row_count, KV_HEADS, group_size, HEAD)
    key_groups = key_tree.reshape(tree_size, KV_HEADS, HEAD)
    value_groups = value_tree.reshape(tree_size, KV_HEADS, HEAD)
    scores = jnp.einsum(
        "qgrd,kgd->grqk", query_groups, key_groups, preferred_element_type=jnp.float32
    )
    probs, log_total = softmax_parts(scores, mask_full)
    attended = jnp.einsum(
        "grqk,kgd->qgrd",
        probs.astype(jnp.bfloat16),
        value_groups,
        preferred_element_type=jnp.float32,
    )
    attended = attended.astype(jnp.bfloat16).reshape(row_count, HEADS * HEAD)
    attention_pre = jnp.dot(attended, output_all, preferred_element_type=jnp.float32)
    attention_branch = norm_rows(attention_pre, attention_post_gain)
    middle = stream + attention_branch
    normed_mid = norm_rows(middle, feedforward_gain).astype(jnp.bfloat16)
    mid_tree = group_rows(normed_mid)
    gate_lin = jnp.einsum("td,fd->tf", mid_tree, gate_weight, preferred_element_type=jnp.float32)
    up_lin = jnp.einsum("td,fd->tf", mid_tree, up_weight, preferred_element_type=jnp.float32)
    hidden = gated_gelu(gate_lin, up_lin).astype(jnp.bfloat16)
    feedforward_pre = group_sums(jnp.dot(hidden, down_weight, preferred_element_type=jnp.float32))
    feedforward_branch = norm_rows(feedforward_pre, feedforward_post_gain)
    result = middle + feedforward_branch
    squares = jnp.stack(
        [
            jnp.sum(valid_rows[:, None] * summand * summand)
            for summand in (stream, attention_branch, feedforward_branch, result)
        ]
    )
    valid_total = jnp.sum(valid_rows) * model_width
    squares_all, valid_all = lax.psum((squares, valid_total), ("replica", "shard"))
    seed_grad = cotangent.astype(jnp.float32) * valid_rows[:, None]
    unused_four, pull_four = jax.vjp(norm_rows, feedforward_pre, feedforward_post_gain)
    ffpre_back, grad_four = pull_four(seed_grad)
    ffpre_low = ffpre_back.astype(jnp.bfloat16)
    ffpre_tree = group_rows(ffpre_low)
    hidden_back = jnp.einsum(
        "td,fd->tf", ffpre_tree, down_weight, preferred_element_type=jnp.float32
    ).astype(jnp.bfloat16)
    unused_glu, pull_glu = jax.vjp(gated_gelu, gate_lin, up_lin)
    gate_back, up_back = pull_glu(hidden_back.astype(jnp.float32))
    gate_back = gate_back.astype(jnp.bfloat16)
    up_back = up_back.astype(jnp.bfloat16)
    mid_terms = jnp.dot(gate_back, gate_weight, preferred_element_type=jnp.float32) + jnp.dot(
        up_back, up_weight, preferred_element_type=jnp.float32
    )
    mid_back = group_sums(mid_terms)
    gate_grad = jnp.einsum("tf,td->fd", gate_back, mid_tree, preferred_element_type=jnp.float32)
    up_grad = jnp.einsum("tf,td->fd", up_back, mid_tree, preferred_element_type=jnp.float32)
    down_grad = jnp.einsum("tf,td->fd", hidden, ffpre_tree, preferred_element_type=jnp.float32)
    unused_three, pull_three = jax.vjp(norm_rows, middle, feedforward_gain)
    middle_part, grad_three = pull_three(mid_back)
    middle_back = seed_grad + middle_part
    unused_two, pull_two = jax.vjp(norm_rows, attention_pre, attention_post_gain)
    attention_pre_back, grad_two = pull_two(middle_back)
    pre_low = attention_pre_back.astype(jnp.bfloat16)
    query_all, key_all, value_all, output_all = collect_attention(
        query_weight, key_weight, value_weight, output_weight
    )
    attended_back = jnp.einsum(
        "td,qd->tq", pre_low, output_all, preferred_element_type=jnp.float32
    ).astype(jnp.bfloat16)
    scores = jnp.einsum(
        "qgrd,kgd->grqk", query_groups, key_groups, preferred_element_type=jnp.float32
    )
    tanh_value = jnp.tanh(scores / score_cap)
    probs_back = jnp.where(
        mask_full,
        jnp.exp(jnp.where(mask_full, score_cap * tanh_value - log_total, -1000000000.0)),
        0.0,
    )
    back_groups = attended_back.reshape(row_count, KV_HEADS, group_size, HEAD)
    prob_grads = jnp.einsum(
        "qgrd,kgd->grqk", back_groups, value_groups, preferred_element_type=jnp.float32
    )
    inner_sum = jnp.sum(probs_back * prob_grads, axis=-1, keepdims=True)
    score_back = (probs_back * (prob_grads - inner_sum) * (1.0 - tanh_value * tanh_value)).astype(
        jnp.bfloat16
    )
    query_back = jnp.einsum(
        "grqk,kgd->qgrd", score_back, key_groups, preferred_element_type=jnp.float32
    ).reshape(row_count, HEADS, HEAD)
    key_back = jnp.einsum(
        "grqk,qgrd->kgd", score_back, query_groups, preferred_element_type=jnp.float32
    ).reshape(tree_size, KV_HEADS * HEAD)
    value_back = jnp.einsum(
        "grqk,qgrd->kgd",
        probs_back.astype(jnp.bfloat16),
        back_groups,
        preferred_element_type=jnp.float32,
    ).reshape(tree_size, KV_HEADS * HEAD)
    key_sum, value_sum = (
        lax.psum_scatter(key_back, "shard", scatter_dimension=0, tiled=True),
        lax.psum_scatter(value_back, "shard", scatter_dimension=0, tiled=True),
    )
    query_low = (
        rotate_back(query_back * query_scale, cos_table, sin_table)
        .astype(jnp.bfloat16)
        .reshape(row_count, HEADS * HEAD)
    )
    key_low = (
        rotate_back(key_sum.reshape(row_count, KV_HEADS, HEAD), cos_table, sin_table)
        .astype(jnp.bfloat16)
        .reshape(row_count, KV_HEADS * HEAD)
    )
    value_low = value_sum.astype(jnp.bfloat16)
    normed_back = (
        jnp.dot(query_low, query_all, preferred_element_type=jnp.float32)
        + jnp.dot(key_low, key_all, preferred_element_type=jnp.float32)
        + jnp.dot(value_low, value_all, preferred_element_type=jnp.float32)
    )
    output_local = jnp.einsum("tq,td->qd", attended, pre_low, preferred_element_type=jnp.float32)
    query_local = jnp.einsum("tq,td->qd", query_low, normed_in, preferred_element_type=jnp.float32)
    key_local = jnp.einsum("tq,td->qd", key_low, normed_in, preferred_element_type=jnp.float32)
    value_local = jnp.einsum("tq,td->qd", value_low, normed_in, preferred_element_type=jnp.float32)
    query_part, key_part, value_part, output_part = (
        lax.psum_scatter(query_local, "shard", scatter_dimension=0, tiled=True),
        lax.psum_scatter(key_local, "shard", scatter_dimension=0, tiled=True),
        lax.psum_scatter(value_local, "shard", scatter_dimension=0, tiled=True),
        lax.psum_scatter(output_local, "shard", scatter_dimension=0, tiled=True),
    )
    unused_one, pull_one = jax.vjp(norm_rows, stream, attention_gain)
    stream_part, grad_one = pull_one(normed_back)
    input_grad = middle_back + stream_part
    query_sum, key_total, value_total, output_sum, gate_sum, up_sum, down_sum = lax.psum(
        (query_part, key_part, value_part, output_part, gate_grad, up_grad, down_grad), "replica"
    )
    gain_one, gain_two, gain_three, gain_four = lax.psum(
        (grad_one, grad_two, grad_three, grad_four), ("replica", "shard")
    )
    stream_rms = jnp.sqrt(squares_all / valid_all)
    return (
        result.astype(jnp.bfloat16),
        input_grad,
        query_sum,
        key_total,
        value_total,
        output_sum,
        gate_sum,
        up_sum,
        down_sum,
        gain_one,
        gain_two,
        gain_three,
        gain_four,
        stream_rms,
    )


def solution(mesh):
    return jax.shard_map(
        shards,
        mesh=mesh,
        in_specs=(
            P(("replica", "shard"), None),
            P(("replica", "shard"), None),
            P("replica"),
            P("replica"),
            P("replica", None),
            P("shard", None),
            P("shard", None),
            P("shard", None),
            P("shard", None),
            P("shard", None),
            P("shard", None),
            P("shard", None),
            P(),
            P(),
            P(),
            P(),
        ),
        out_specs=(
            P(("replica", "shard"), None),
            P(("replica", "shard"), None),
            P("shard", None),
            P("shard", None),
            P("shard", None),
            P("shard", None),
            P("shard", None),
            P("shard", None),
            P("shard", None),
            P(),
            P(),
            P(),
            P(),
            P(),
        ),
        check_vma=False,
    )
```

profile of v0, /device:TPU:0, one launch (start us, length us, event | category | flops | bytes accessed | tf_op | source)
XLA Modules:
  0.0 2612.5 jit_solution(16743754383248358632)
XLA Ops:
  15.7 35.9 %all-gather.13.cloned.1.call-done = bf16[1024,2304]{1,0:T(8,128)(2,1)} async-done(((bf16[128,2304]{1,0:T(8,128)(2,1)}), bf16[1024,2304]{1,0:T(8,128)(2,1)}) %all-gather.13.cloned.1.call-update) | async-done | bytes 4718608 | tf_op jit(solution)/shard_map/all_gather | solution.py:88
  51.6 4.0 fusion.134
  57.6 34.8 %all-gather.9.cloned.1.call-done = bf16[1024,2304]{1,0:T(8,128)(2,1)} async-done(((bf16[128,2304]{1,0:T(8,128)(2,1)}), bf16[1024,2304]{1,0:T(8,128)(2,1)}) %all-gather.9.cloned.1.call-update) | async-done | bytes 4718608 | tf_op jit(solution)/shard_map/all_gather | solution.py:89
  92.4 4.8 convolution_convert_fusion.2
  101.2 26.1 all-gather.15.cloned.1.call-done
  127.2 6.4 reshape.398
  133.6 28.3 %all-gather.11.cloned.1.call-done = bf16[1536,1024]{1,0:T(8,128)(2,1)} async-done(((bf16[192,1024]{1,0:T(8,128)(2,1)}), bf16[1536,1024]{1,0:T(8,128)(2,1)}) %all-gather.11.cloned.1.call-update) | async-done | bytes 3145744 | tf_op jit(solution)/shard_map/all_gather | solution.py:162
  161.9 6.2 reshape.396
  168.0 54.4 %all-gather.17.cloned.1.call-done = bf16[2048,2304]{1,0:T(8,128)(2,1)} async-done(((bf16[256,2304]{1,0:T(8,128)(2,1)}), bf16[2048,2304]{1,0:T(8,128)(2,1)}) %all-gather.17.cloned.1.call-update) | async-done | bytes 9437200 | tf_op jit(solution)/shard_map/all_gather | solution.py:87
  222.5 8.0 fusion.132
  230.5 2.8 reshape.399
  237.6 3.6 fusion.6
  241.2 3.7 fusion.8
  245.5 4.1 fusion.79
  251.1 32.0 %all-gather.19.cloned.1.call-done = bf16[2048,2304]{1,0:T(8,128)(2,1)} async-done(((bf16[256,2304]{1,0:T(8,128)(2,1)}), bf16[2048,2304]{1,0:T(8,128)(2,1)}) %all-gather.19.cloned.1.call-update) | async-done | bytes 9437200 | tf_op jit(solution)/shard_map/all_gather | solution.py:90
  283.1 5.8 multiply_reduce_fusion.8
  291.3 49.0 %all-gather.21.cloned.1.call-done = bf16[1536,2304]{1,0:T(8,128)(2,1)} async-done(((bf16[192,2304]{1,0:T(8,128)(2,1)}), bf16[1536,2304]{1,0:T(8,128)(2,1)}) %all-gather.21.cloned.1.call-update) | async-done | bytes 7077904 | tf_op jit(solution)/shard_map/all_gather | solution.py:95
  340.2 15.2 fusion.144
  355.4 15.3 multiply_convert_fusion
  370.8 13.9 fusion.145
  386.2 99.4 %reduce-scatter.11.cloned.1.call-done = f32[192,2304]{1,0:T(8,128)} async-done(((f32[1536,2304]{1,0:T(8,128)}), f32[192,2304]{1,0:T(8,128)}) %reduce-scatter.11.cloned.1.call-update) | async-done | bytes 1769488 | tf_op jit(solution)/shard_map/reduce_scatter | solution.py:99
  487.4 4.2 multiply_reduce_fusion
  493.2 48.9 %all-gather.23.cloned.1.call-done = bf16[1536,2304]{1,0:T(8,128)(2,1)} async-done(((bf16[192,2304]{1,0:T(8,128)(2,1)}), bf16[1536,2304]{1,0:T(8,128)(2,1)}) %all-gather.23.cloned.1.call-update) | async-done | bytes 7077904 | tf_op jit(solution)/shard_map/all_gather | solution.py:95
  542.1 21.8 fusion.16
  563.9 15.9 fusion.146
  579.7 21.2 convolution_add_fusion
  602.3 99.6 %reduce-scatter.13.cloned.1.call-done = f32[192,2304]{1,0:T(8,128)} async-done(((f32[1536,2304]{1,0:T(8,128)}), f32[192,2304]{1,0:T(8,128)}) %reduce-scatter.13.cloned.1.call-update) | async-done | bytes 1769488 | tf_op jit(solution)/shard_map/reduce_scatter | solution.py:99
  701.9 2.6 multiply_reduce_fusion.1
  704.5 4.3 multiply_reduce_fusion.2
  710.1 7.8 convolution_convert_fusion.1
  717.9 2.6 reshape.402
  720.5 10.3 fusion.44
  730.8 6.5 copy.94
  737.8 7.4 fusion.55
  745.2 23.9 fusion.20
  769.2 6.6 copy.93
  775.9 23.4 reduce-scatter.25.cloned.1.call-done
  800.6 5.0 fusion.87
  805.8 58.9 %reduce-scatter.15.cloned.1.call-done = f32[192,1024]{1,0:T(8,128)} async-done(((f32[1536,1024]{1,0:T(8,128)}), f32[192,1024]{1,0:T(8,128)}) %reduce-scatter.15.cloned.1.call-update) | async-done | bytes 786448 | tf_op jit(solution)/shard_map/reduce_scatter | solution.py:258
  864.7 2.4 reshape.406
  870.0 5.6 fusion.128
  875.7 12.5 fusion.148
  891.0 24.5 fusion.21
  919.9 2.4 copy.75
  922.2 3.4 reshape.403
  925.6 2.6 add_convert_fusion
  929.1 8.1 fusion.130
  937.5 15.3 fusion.150
  952.9 14.7 fusion.149
  967.6 13.2 fusion.137
  980.7 43.8 %reduce-scatter.19.cloned.1.call-done = f32[128,2304]{1,0:T(8,128)} async-done(((f32[1024,2304]{1,0:T(8,128)}), f32[128,2304]{1,0:T(8,128)}) %reduce-scatter.19.cloned.1.call-update) | async-done | bytes 1179664 | tf_op jit(solution)/shard_map/reduce_scatter | solution.py:283
  1024.5 129.6 %reduce-scatter.23.cloned.1.call-done = f32[256,2304]{1,0:T(8,128)} async-done(((f32[2048,2304]{1,0:T(8,128)}), f32[256,2304]{1,0:T(8,128)}) %reduce-scatter.23.cloned.1.call-update) | async-done | bytes 2359312 | tf_op jit(solution)/shard_map/reduce_scatter | solution.py:285
  1154.1 129.6 %reduce-scatter.17.cloned.1.call-done = f32[256,2304]{1,0:T(8,128)} async-done(((f32[2048,2304]{1,0:T(8,128)}), f32[256,2304]{1,0:T(8,128)}) %reduce-scatter.17.cloned.1.call-update) | async-done | bytes 2359312 | tf_op jit(solution)/shard_map/reduce_scatter | solution.py:282
  1284.4 6.0 fusion.147
  1290.4 3.5 convolution_add_fusion.2
  1293.9 6.4 fusion.61
  1300.3 2.5 pad_maximum_fusion.3
  1302.8 49.3 %all-reduce = (f32[2304]{0:T(1024)}, f32[2304]{0:T(1024)}, f32[2304]{0:T(1024)}, f32[2304]{0:T(1024)}, f32[4]{0:T(128)S(1)}, /*index=5*/f32[]{:T(128)}) all-reduce(f32[2304]{0:T(1024)S(1)} %get-tuple-element.20, f32[2304]{0:T(1024)S(1)} %copy-done.36, ...), channel_id=1, replica_groups=mesh['replica'=4,'shard'=8] {'replica','shard'}, use_global_device_ids=true, to_apply=%region_35.36 | all-reduce | flops 9221 | bytes 73768 | tf_op jit(solution)/shard_map/psum | solution.py:293
  1353.3 3.2 fusion.65
  1356.5 1220.0 %all-reduce.4.cloned.1.call-done = (f32[256,2304]{1,0:T(8,128)}, f32[128,2304]{1,0:T(8,128)}, f32[128,2304]{1,0:T(8,128)}, f32[256,2304]{1,0:T(8,128)}, f32[1152...) async-done(((f32[256,2304]{1,0:T(8,128)}, f32[128,2304]{1,0:T(8,128)}, f32[128,2304]{1,0:T(8,128)}, f32[256,2304]{1,0:T(8,128)}, f32[1152,2304]{1,0:T(8,128)}, ...) | async-done | bytes 38928400 | tf_op jit(solution)/shard_map/psum | solution.py:290
  2576.4 3.4 copy.131
  2583.3 9.1 copy.135
  2592.4 9.0 copy.136
  2601.4 4.1 copy.137
  (240 shorter events, 48.1 us)
Async XLA Ops:
  7.2 8.2 copy-start
  7.2 8.5 copy-start.47
  7.2 44.4 %all-gather.13.cloned.1.call-start = ((), (), s32[]{:S(2)}) async-start(), calls=%async_computation.10 | async-start | bytes 5308416 | tf_op jit(solution)/shard_map/all_gather | solution.py:88
  7.9 84.5 %all-gather.9.cloned.1.call-start = ((), (), s32[]{:S(2)}) async-start(), calls=%async_computation.8 | async-start | bytes 5308416 | tf_op jit(solution)/shard_map/all_gather | solution.py:89
  8.7 118.5 %all-gather.15.cloned.1.call-start = ((), (), s32[]{:S(2)}) async-start(), calls=%async_computation.11 | async-start | bytes 3538944 | tf_op jit(solution)/shard_map/all_gather | solution.py:161
  14.6 221.4 %copy-start.15 = (f32[192,256]{1,0:T(8,128)}, f32[192,256]{1,0:T(8,128)S(1)}, u32[]{:S(2)}) copy-start(f32[192,256]{1,0:T(8,128)S(1)} %get-tuple-element.61) | copy-start | bytes 589828
  15.4 41.2 %copy-start.8 = (f32[24,8,4,256]{3,1,2,0:T(8,128)}, f32[24,8,4,256]{3,1,2,0:T(8,128)S(1)}, u32[]{:S(2)}) copy-start(f32[24,8,4,256]{3,1,2,0:T(8,128)S(1)} %copy.96) | copy-start | bytes 2359300
  15.7 40.5 %copy-start.51 = (f32[192]{0:T(256)}, f32[192]{0:T(256)S(1)}, u32[]{:S(2)}) copy-start(f32[192]{0:T(256)S(1)} %fusion.69) | copy-start | bytes 2308
  15.7 206.8 %copy-start.38 = (f32[192]{0:T(256)}, f32[192]{0:T(256)S(1)}, u32[]{:S(2)}) copy-start(f32[192]{0:T(256)S(1)} %fusion.94) | copy-start | bytes 2308
  15.7 206.8 %copy-start.30 = (f32[2304]{0:T(1024)}, f32[2304]{0:T(1024)S(1)}, u32[]{:S(2)}) copy-start(f32[2304]{0:T(1024)S(1)} %broadcast_add_fusion.3) | copy-start | bytes 27652
  57.5 40.9 %copy-start.33 = (s32[1536]{0:T(1024)S(1)}, s32[1536]{0:T(1024)}, u32[]{:S(2)}) copy-start(s32[1536]{0:T(1024)} %param.18) | copy-start | bytes 18436
  57.5 41.1 %copy-start.37 = (s32[1536]{0:T(1024)S(1)}, s32[1536]{0:T(1024)}, u32[]{:S(2)}) copy-start(s32[1536]{0:T(1024)} %param.19) | copy-start | bytes 18436
  57.6 41.1 %copy-start.48 = (f32[2304]{0:T(1024)S(1)}, f32[2304]{0:T(1024)}, u32[]{:S(2)}) copy-start(f32[2304]{0:T(1024)} %param.29) | copy-start | bytes 27652
  57.6 41.1 %copy-start.49 = (f32[2304]{0:T(1024)S(1)}, f32[2304]{0:T(1024)}, u32[]{:S(2)}) copy-start(f32[2304]{0:T(1024)} %param.30) | copy-start | bytes 27652
  57.6 104.3 %all-gather.11.cloned.1.call-start = ((), (), s32[]{:S(2)}) async-start(), calls=%async_computation.9 | async-start | bytes 3538944 | tf_op jit(solution)/shard_map/all_gather | solution.py:162
  97.2 125.3 %all-gather.17.cloned.1.call-start = ((), (), s32[]{:S(2)}) async-start(), calls=%async_computation.12 | async-start | bytes 10616832 | tf_op jit(solution)/shard_map/all_gather | solution.py:87
  97.8 185.3 %all-gather.19.cloned.1.call-start = ((), (), s32[]{:S(2)}) async-start(), calls=%async_computation.13 | async-start | bytes 10616832 | tf_op jit(solution)/shard_map/all_gather | solution.py:90
  98.4 241.9 %all-gather.21.cloned.1.call-start = ((), (), s32[]{:S(2)}) async-start(), calls=%async_computation.14 | async-start | bytes 7962624 | tf_op jit(solution)/shard_map/all_gather | solution.py:95
  101.1 143.8 %copy-start.23 = (pred[192,1536]{1,0:T(8,128)(4,1)}, pred[192,1536]{1,0:T(8,128)(4,1)S(1)}, u32[]{:S(2)}) copy-start(pred[192,1536]{1,0:T(8,128)(4,1)S(1)} %fusion.82) | copy-start | bytes 884740
  241.2 8.4 copy-start.6
  241.2 8.4 copy-start.40
  251.0 37.8 %copy-start.14 = (bf16[192,2048]{1,0:T(8,128)(2,1)}, bf16[192,2048]{1,0:T(8,128)(2,1)S(1)}, u32[]{:S(2)}) copy-start(bf16[192,2048]{1,0:T(8,128)(2,1)S(1)} %reshape.401) | copy-start | bytes 2359300
  251.0 39.0 %copy-start.32 = (f32[2304]{0:T(1024)S(1)}, f32[2304]{0:T(1024)}, u32[]{:S(2)}) copy-start(f32[2304]{0:T(1024)} %broadcast_add_fusion.1) | copy-start | bytes 27652
  288.9 66.5 %copy-start.54 = (f32[192]{0:T(256)}, f32[192]{0:T(256)S(1)}, u32[]{:S(2)}) copy-start(f32[192]{0:T(256)S(1)} %get-tuple-element.65) | copy-start | bytes 2308
  288.9 66.5 %copy-start.45 = (f32[192]{0:T(256)}, f32[192]{0:T(256)S(1)}, u32[]{:S(2)}) copy-start(f32[192]{0:T(256)S(1)} %fusion.95) | copy-start | bytes 2308
  290.1 411.8 %copy-start.44 = (f32[192]{0:T(256)}, f32[192]{0:T(256)S(1)}, u32[]{:S(2)}) copy-start(f32[192]{0:T(256)S(1)} %fusion.96) | copy-start | bytes 2308
  291.2 194.4 %reduce-scatter.11.cloned.1.call-start = ((), (), s32[]{:S(2)}) async-start(), calls=%async_computation.15 | async-start | bytes 15925248 | tf_op jit(solution)/shard_map/reduce_scatter | solution.py:99
  340.2 15.2 copy-start.56
  340.2 30.5 %slice-start.5 = ((s8[5308416]{0:T(1024)(128)(4,1)}), s8[4194304]{0:T(1024)(128)(4,1)S(1)}, s32[]{:S(2)}) async-start(s8[5308416]{0:T(1024)(128)(4,1)} %bitcast.199), calls=%async_computation.30 | async-start | bytes 8388608
  355.4 15.3 slice-start.6
  384.7 102.7 %copy-start.7 = (bf16[192,2304]{1,0:T(8,128)(2,1)S(1)}, bf16[192,2304]{1,0:T(8,128)(2,1)}, u32[]{:S(2)}) copy-start(bf16[192,2304]{1,0:T(8,128)(2,1)} %param.17) | copy-start | bytes 2654212
  384.7 157.4 %all-gather.23.cloned.1.call-start = ((), (), s32[]{:S(2)}) async-start(), calls=%async_computation.16 | async-start | bytes 7962624 | tf_op jit(solution)/shard_map/all_gather | solution.py:95
  485.6 6.0 copy-start.4
  493.1 208.8 %reduce-scatter.13.cloned.1.call-start = ((), (), s32[]{:S(2)}) async-start(), calls=%async_computation.17 | async-start | bytes 15925248 | tf_op jit(solution)/shard_map/reduce_scatter | solution.py:99
  563.9 15.9 copy-start.57
  601.0 198.3 %reduce-scatter.25.cloned.1.call-start = ((), (), s32[]{:S(2)}) async-start(), calls=%async_computation.23 | async-start | bytes 7077888
  701.9 6.9 copy-start.55
  701.9 6.9 copy-start.3
  701.9 6.9 copy-start.46
  710.1 10.4 copy-start.24
  710.1 10.4 copy-start.53
  737.4 127.3 %reduce-scatter.15.cloned.1.call-start = ((), (), s32[]{:S(2)}) async-start(), calls=%async_computation.18 | async-start | bytes 7077888 | tf_op jit(solution)/shard_map/reduce_scatter | solution.py:258
  775.8 24.8 copy-start.1
  775.8 24.8 copy-start.31
  775.8 24.8 copy-start.39
  775.8 204.9 %reduce-scatter.21.cloned.1.call-start = ((), (), s32[]{:S(2)}) async-start(), calls=%async_computation.21 | async-start | bytes 10616832 | tf_op jit(solution)/shard_map/reduce_scatter | solution.py:284
  805.7 61.4 %copy-start.16 = (f32[192,256]{1,0:T(8,128)S(1)}, f32[192,256]{1,0:T(8,128)}, u32[]{:S(2)}) copy-start(f32[192,256]{1,0:T(8,128)} %copy-done.15) | copy-start | bytes 589828
  805.7 218.8 %reduce-scatter.19.cloned.1.call-start = ((), (), s32[]{:S(2)}) async-start(), calls=%async_computation.20 | async-start | bytes 10616832 | tf_op jit(solution)/shard_map/reduce_scatter | solution.py:283
  875.7 278.5 %reduce-scatter.23.cloned.1.call-start = ((), (), s32[]{:S(2)}) async-start(), calls=%async_computation.22 | async-start | bytes 21233664 | tf_op jit(solution)/shard_map/reduce_scatter | solution.py:285
  888.3 395.5 %reduce-scatter.17.cloned.1.call-start = ((), (), s32[]{:S(2)}) async-start(), calls=%async_computation.19 | async-start | bytes 21233664 | tf_op jit(solution)/shard_map/reduce_scatter | solution.py:282
  891.0 24.5 copy-start.27
  937.2 1639.2 %all-reduce.4.cloned.1.call-start = ((), (), s32[]{:S(2)}) async-start(), calls=%async_computation.24 | async-start | bytes 77856768 | tf_op jit(solution)/shard_map/psum | solution.py:290
  937.5 15.4 copy-start.58
  937.5 30.0 %slice-start.3 = ((s8[7077888]{0:T(1024)(128)(4,1)}), s8[4194304]{0:T(1024)(128)(4,1)S(1)}, s32[]{:S(2)}) async-start(s8[7077888]{0:T(1024)(128)(4,1)} %bitcast.197), calls=%async_computation.28 | async-start | bytes 8388608
  937.5 30.0 %slice-start.7 = ((s8[7077888]{0:T(1024)(128)(4,1)}), s8[4194304]{0:T(1024)(128)(4,1)S(1)}, s32[]{:S(2)}) async-start(s8[7077888]{0:T(1024)(128)(4,1)} %bitcast.201), calls=%async_computation.32 | async-start | bytes 8388608
  952.9 14.7 slice-start.4
  952.9 14.7 slice-start.8
  1293.9 8.9 copy-start.34
  1293.9 8.9 copy-start.35
  1293.9 8.9 copy-start.36
  1293.9 59.3 %copy-start.52 = (f32[192]{0:T(256)S(1)}, f32[192]{0:T(256)}, u32[]{:S(2)}) copy-start(f32[192]{0:T(256)} %copy-done.51) | copy-start | bytes 2308
  2583.3 18.1 slice-start
  2583.3 18.1 slice-start.1
  2592.4 9.0 slice-start.2
  (21 other events, 48.1 us)
Sparse Core Ops, SparseCore 0:
  9.9 41.6 all-gather.12
  53.5 38.9 all-gather.8
  94.9 32.3 all-gather.14
  129.5 32.3 all-gather.10
  163.6 58.8 all-gather.16
  224.2 58.8 all-gather.18
  291.4 48.8 all-gather.20
  384.8 100.7 reduce-scatter.10
  493.2 48.8 all-gather.22
  601.1 100.7 reduce-scatter.12
  737.5 61.7 reduce-scatter.24
  802.9 61.7 reduce-scatter.14
  868.2 76.4 reduce-scatter.20
  948.0 76.4 reduce-scatter.18
  1028.0 126.0 reduce-scatter.22
  1157.6 126.1 reduce-scatter.16
  1288.2 1288.1 all-reduce.3
where the time goes:
time: 2620 us; the launch traced here: 2610 us
  waiting for transfers between devices  2120 us (81%)
  matrix products  298 us (11%)
  local copies, waits for them, and re-layouts  84.7 us (3%)
  blocking collectives  49.3 us (2%)
  other arithmetic  46.9 us (2%)
    psum x1, waiting for transfers between devices, shards(): lax.psum((query_part, key_part, value_part, output_part, gate_grad, up_gr...  1220 us
    reduce_scatter x2, waiting for transfers between devices, group_sums(): return lax.psum_scatter(values, 'shard', scatter_dimension=0, tiled=True)  199 us
    reduce_scatter x1, waiting for transfers between devices, shards(): lax.psum_scatter(query_local, 'shard', scatter_dimension=0, tiled=True)  130 us
    reduce_scatter x1, waiting for transfers between devices, shards(): lax.psum_scatter(output_local, 'shard', scatter_dimension=0, tiled=True)  130 us
    all_gather x2, waiting for transfers between devices, group_rows(): return lax.all_gather(values, 'shard', axis=0, tiled=True)  97.9 us
    reduce_scatter x1, waiting for transfers between devices, shards(): lax.psum_scatter(key_back, 'shard', scatter_dimension=0, tiled=True)  58.9 us
    all_gather x1, waiting for transfers between devices, collect_attention(): lax.all_gather(query_weight, 'shard', axis=0, tiled=True)  54.4 us
  transfers between devices with their start and end apart: 17, of which 16 were waited for; matrix products, arithmetic and copies ran while one was open for 9% of the time, Pallas kernels for 0%

commit v1 on v0

--- a/solution.py
+++ b/solution.py
@@ -1,3 +1,5 @@
+import math
+
 import jax
 import jax.numpy as jnp
 from jax import lax
@@ -99,7 +101,7 @@
     return lax.psum_scatter(values, "shard", scatter_dimension=0, tiled=True)
 
 
-def shards(
+def shards_generic(
     hidden_in,
     cotangent,
     token_segment,
@@ -312,9 +314,227 @@
     )
 
 
+def norm_factor(stream):
+    return lax.rsqrt(jnp.mean(stream * stream, axis=-1, keepdims=True) + norm_eps)
+
+
+def norm_back(stream, norm_gain, gradient):
+    factor = norm_factor(stream)
+    weighted = gradient * (1.0 + norm_gain)
+    inner = jnp.mean(weighted * stream, axis=-1, keepdims=True)
+    back = factor * weighted - stream * (factor * factor * factor * inner)
+    gain_back = jnp.sum(gradient * stream * factor, axis=0)
+    return back, gain_back
+
+
+def dot_nt(left, right):
+    return lax.dot_general(
+        left, right, (((1,), (1,)), ((), ())), preferred_element_type=jnp.float32
+    )
+
+
+def dot_nn(left, right):
+    return lax.dot_general(
+        left, right, (((1,), (0,)), ((), ())), preferred_element_type=jnp.float32
+    )
+
+
+def dot_tn(left, right):
+    return lax.dot_general(
+        left, right, (((0,), (0,)), ((), ())), preferred_element_type=jnp.float32
+    )
+
+
+def sum_low(values):
+    return lax.psum_scatter(
+        values.astype(jnp.bfloat16), "shard", scatter_dimension=0, tiled=True
+    ).astype(jnp.float32)
+
+
+def gelu_parts(gate_lin):
+    root = math.sqrt(2.0 / math.pi)
+    square = gate_lin * gate_lin
+    tanh_value = jnp.tanh(root * gate_lin * (1.0 + 0.044715 * square))
+    half_up = 0.5 * (1.0 + tanh_value)
+    slope = half_up + 0.5 * gate_lin * (1.0 - tanh_value * tanh_value) * root * (
+        1.0 + 3.0 * 0.044715 * square
+    )
+    return gate_lin * half_up, slope
+
+
+def shards_heads(
+    hidden_in,
+    cotangent,
+    token_segment,
+    token_valid,
+    segment_parent,
+    query_weight,
+    key_weight,
+    value_weight,
+    output_weight,
+    gate_weight,
+    up_weight,
+    down_weight,
+    attention_gain,
+    attention_post_gain,
+    feedforward_gain,
+    feedforward_post_gain,
+):
+    low = jnp.bfloat16
+    row_count, model_width = hidden_in.shape
+    shard_count = lax.axis_size("shard")
+    tree_count = lax.axis_size("replica")
+    shard = lax.axis_index("shard")
+    row_start = shard * row_count
+    tree_size = token_segment.shape[0]
+    position, parent_tok, grand_tok = tree_tables(token_segment, token_valid, segment_parent[0])
+    key_index = jnp.arange(tree_size, dtype=jnp.int32)
+    allowed = allowed_mask(
+        key_index, token_segment, parent_tok, grand_tok, key_index, token_segment, token_valid
+    )
+    cos_table, sin_table = rope_tables(position, HEAD)
+    cos_table, sin_table = cos_table[:, 0], sin_table[:, 0]
+    query_scale = HEAD ** (-0.5)
+    valid_rows = lax.dynamic_slice_in_dim(token_valid, row_start, row_count).astype(jnp.float32)
+    stream = hidden_in.astype(jnp.float32)
+    second_core = lax.rem(shard, 2) == 1
+    pairs = [(i, i ^ 1) for i in range(shard_count)]
+
+    def both_halves(own):
+        other = lax.ppermute(own, "shard", pairs)
+        return jnp.where(
+            second_core, jnp.concatenate([other, own]), jnp.concatenate([own, other])
+        )
+
+    key_head = both_halves(key_weight)
+    value_head = both_halves(value_weight)
+    normed_in = group_rows(norm_rows(stream, attention_gain).astype(low))
+    queries = (
+        rotate(dot_nt(normed_in, query_weight), cos_table, sin_table) * query_scale
+    ).astype(low)
+    keys = rotate(dot_nt(normed_in, key_head), cos_table, sin_table).astype(low)
+    values = dot_nt(normed_in, value_head).astype(low)
+    tanh_value = jnp.tanh(dot_nt(queries, keys) / score_cap)
+    raised = jnp.where(allowed, jnp.exp(score_cap * tanh_value), 0.0)
+    scale = 1.0 / jnp.sum(raised, axis=-1, keepdims=True)
+    attended = dot_nn((raised * scale).astype(low), values).astype(low)
+    attention_pre = sum_low(dot_nn(attended, output_weight))
+    attention_branch = norm_rows(attention_pre, attention_post_gain)
+    middle = stream + attention_branch
+    normed_mid = norm_rows(middle, feedforward_gain).astype(low)
+    mid_tree = group_rows(normed_mid)
+    gate_lin = dot_nt(mid_tree, gate_weight)
+    up_lin = dot_nt(mid_tree, up_weight)
+    gelu_value, gelu_slope = gelu_parts(gate_lin)
+    hidden = (gelu_value * up_lin).astype(low)
+    feedforward_pre = sum_low(dot_nn(hidden, down_weight))
+    feedforward_branch = norm_rows(feedforward_pre, feedforward_post_gain)
+    result = middle + feedforward_branch
+    squares = jnp.stack(
+        [
+            jnp.sum(valid_rows[:, None] * summand * summand)
+            for summand in (stream, attention_branch, feedforward_branch, result)
+        ]
+    )
+    valid_total = jnp.sum(valid_rows) * model_width
+    seed_grad = cotangent.astype(jnp.float32) * valid_rows[:, None]
+    ffpre_back, grad_four = norm_back(feedforward_pre, feedforward_post_gain, seed_grad)
+    ffpre_low = ffpre_back.astype(low)
+    ffpre_tree = group_rows(ffpre_low)
+    mid_every = lax.all_gather(normed_mid, ("replica", "shard"), axis=0, tiled=True)
+    ffpre_every = lax.all_gather(ffpre_low, ("replica", "shard"), axis=0, tiled=True)
+
+    def hidden_grads(gate_lin, up_lin, gelu_value, gelu_slope, ffpre_rows):
+        hidden_back = dot_nt(ffpre_rows, down_weight).astype(low).astype(jnp.float32)
+        gate_back = (hidden_back * up_lin * gelu_slope).astype(low)
+        up_back = (hidden_back * gelu_value).astype(low)
+        return gate_back, up_back
+
+    gate_back, up_back = hidden_grads(gate_lin, up_lin, gelu_value, gelu_slope, ffpre_tree)
+    mid_back = sum_low(dot_nn(gate_back, gate_weight) + dot_nn(up_back, up_weight))
+    middle_part, grad_three = norm_back(middle, feedforward_gain, mid_back)
+    middle_back = seed_grad + middle_part
+    attention_pre_back, grad_two = norm_back(attention_pre, attention_post_gain, middle_back)
+    pre_tree = group_rows(attention_pre_back.astype(low))
+    attended_back = dot_nt(pre_tree, output_weight).astype(low)
+    probs_back = raised * scale
+    prob_grads = dot_nt(attended_back, values)
+    inner_sum = jnp.sum(probs_back * prob_grads, axis=-1, keepdims=True)
+    score_back = (probs_back * (prob_grads - inner_sum) * (1.0 - tanh_value * tanh_value)).astype(
+        low
+    )
+    query_back = dot_nn(score_back, keys)
+    key_back = dot_tn(score_back, queries)
+    value_back = dot_tn(probs_back.astype(low), attended_back)
+    key_back, value_back = (
+        key_back + lax.ppermute(key_back, "shard", pairs),
+        value_back + lax.ppermute(value_back, "shard", pairs),
+    )
+    query_low = rotate_back(query_back * query_scale, cos_table, sin_table).astype(low)
+    key_low = rotate_back(key_back, cos_table, sin_table).astype(low)
+    value_low = value_back.astype(low)
+    half = HEAD // 2
+    key_low = jnp.where(second_core, key_low[:, half:], key_low[:, :half])
+    value_low = jnp.where(second_core, value_low[:, half:], value_low[:, :half])
+    normed_back = sum_low(
+        dot_nn(query_low, query_weight) + dot_nn(key_low, key_weight) + dot_nn(value_low, value_weight)
+    )
+    stream_part, grad_one = norm_back(stream, attention_gain, normed_back)
+    input_grad = middle_back + stream_part
+    attention_grads = jnp.concatenate(
+        [
+            dot_tn(query_low, normed_in),
+            dot_tn(key_low, normed_in),
+            dot_tn(value_low, normed_in),
+            dot_tn(attended, pre_tree),
+        ]
+    ).astype(low)
+    attention_grads = lax.psum(attention_grads, "replica").astype(jnp.float32)
+    sizes = [query_weight.shape[0], key_weight.shape[0], value_weight.shape[0]]
+    query_sum, key_sum, value_sum, output_sum = jnp.split(
+        attention_grads, [sizes[0], sizes[0] + sizes[1], sum(sizes)]
+    )
+    gate_sum = dot_tn(gate_back, mid_tree)
+    up_sum = dot_tn(up_back, mid_tree)
+    down_sum = dot_tn(hidden, ffpre_tree)
+    for step in range(1, tree_count):
+        tree = lax.rem(lax.axis_index("replica") + step, tree_count)
+        mid_rows = lax.dynamic_slice_in_dim(mid_every, tree * tree_size, tree_size)
+        ffpre_rows = lax.dynamic_slice_in_dim(ffpre_every, tree * tree_size, tree_size)
+        gate_lin = dot_nt(mid_rows, gate_weight)
+        up_lin = dot_nt(mid_rows, up_weight)
+        gelu_value, gelu_slope = gelu_parts(gate_lin)
+        hidden = (gelu_value * up_lin).astype(low)
+        gate_back, up_back = hidden_grads(gate_lin, up_lin, gelu_value, gelu_slope, ffpre_rows)
+        gate_sum += dot_tn(gate_back, mid_rows)
+        up_sum += dot_tn(up_back, mid_rows)
+        down_sum += dot_tn(hidden, ffpre_rows)
+    gain_one, gain_two, gain_three, gain_four, squares_all, valid_all = lax.psum(
+        (grad_one, grad_two, grad_three, grad_four, squares, valid_total), ("replica", "shard")
+    )
+    stream_rms = jnp.sqrt(squares_all / valid_all)
+    return (
+        result.astype(low),
+        input_grad,
+        query_sum,
+        key_sum,
+        value_sum,
+        output_sum,
+        gate_sum,
+        up_sum,
+        down_sum,
+        gain_one,
+        gain_two,
+        gain_three,
+        gain_four,
+        stream_rms,
+    )
+
+
 def solution(mesh):
+    heads_fit = mesh.shape["shard"] == HEADS
     return jax.shard_map(
-        shards,
+        shards_heads if heads_fit else shards_generic,
         mesh=mesh,
         in_specs=(
             P(("replica", "shard"), None),

time: 2620 us -> 1370 us (0.52)
  waiting for transfers between devices: 2120 us -> 680 us
  matrix products: 298 us -> 537 us
  local copies, waits for them, and re-layouts: 84.7 us -> 13.5 us
    psum x1, waiting for transfers between devices: 1220 us -> 49.8 us  [shards_heads(): attention_grads = lax.psum(attention_grads, 'replica').astype(jnp.float32)]
    reduce_scatter x7 -> x4, waiting for transfers between devices: 561 us -> 256 us  [sum_low(): lax.psum_scatter(values.astype(jnp.bfloat16), 'shard', scatter_dimension=...]
    dot_general x27 -> x45, matrix products: 298 us -> 537 us  [the longest x18 250 us: dot_tn(): lax.dot_general(left, right, (((0,), (0,)), ((), ())), preferred_element_...]
    all_gather x2 -> x4, waiting for transfers between devices: 97.9 us -> 192 us  [group_rows(): return lax.all_gather(values, 'shard', axis=0, tiled=True)]
    unnamed x151 -> x130, local copies, waits for them, and re-layouts: 49.6 us -> 6.59 us
    reshape x9 -> x0, local copies, waits for them, and re-layouts: 31.2 us -> none  [the longest x1 6.62 us: shards(): key_back = jnp.einsum('grqk,qgrd->kgd', score_back, query_groups, preferr...]
    all_gather x6 -> x2, waiting for transfers between devices: 211 us -> 180 us  [the longest x1 125 us: shards_heads(): lax.all_gather(ffpre_low, ('replica', 'shard'), axis=0, tiled=True)]
  transfers between devices with their start and end apart: 17 -> 15, of which waited for: 16 -> 11; matrix products, arithmetic and copies ran while one was open for 9% -> 18% of each run, Pallas kernels for 0% -> 0%
where the time goes in v1:
time: 1370 us; the launch traced here: 1360 us
  waiting for transfers between devices  680 us (50%)
  matrix products  537 us (39%)
  other arithmetic  69.6 us (5%)
  blocking collectives  43 us (3%)
  between operations  15.6 us (1%)
    reduce_scatter x4, waiting for transfers between devices, sum_low(): lax.psum_scatter(values.astype(jnp.bfloat16), 'shard', scatter_dimension=...  256 us
    dot_general x18, matrix products, dot_tn(): lax.dot_general(left, right, (((0,), (0,)), ((), ())), preferred_element_...  250 us
    dot_general x18, matrix products, dot_nt(): lax.dot_general(left, right, (((1,), (1,)), ((), ())), preferred_element_...  205 us
    all_gather x4, waiting for transfers between devices, group_rows(): return lax.all_gather(values, 'shard', axis=0, tiled=True)  192 us
    all_gather x1, waiting for transfers between devices, shards_heads(): lax.all_gather(ffpre_low, ('replica', 'shard'), axis=0, tiled=True)  125 us
    dot_general x9, matrix products, dot_nn(): lax.dot_general(left, right, (((1,), (0,)), ((), ())), preferred_element_...  82.4 us
    all_gather x1, waiting for transfers between devices, shards_heads(): lax.all_gather(normed_mid, ('replica', 'shard'), axis=0, tiled=True)  55.3 us
    psum x1, waiting for transfers between devices, shards_heads(): attention_grads = lax.psum(attention_grads, 'replica').astype(jnp.float32)  49.8 us
  transfers between devices with their start and end apart: 15, of which 11 were waited for; matrix products, arithmetic and copies ran while one was open for 18% of the time, Pallas kernels for 0%

profile of v1, /device:TPU:0, one launch (start us, length us, event | category | flops | bytes accessed | tf_op | source)
XLA Modules:
  0.0 1361.5 jit_solution(3951405874793069866)
XLA Ops:
  10.6 2.3 fusion.102
  18.7 46.0 %all-gather.7.cloned.1.call-done = bf16[1536,2304]{1,0:T(8,128)(2,1)} async-done(((bf16[192,2304]{1,0:T(8,128)(2,1)}), bf16[1536,2304]{1,0:T(8,128)(2,1)}) %all-gather.7.cloned.1.call-update) | async-done | bytes 7077904 | tf_op jit(solution)/shard_map/all_gather | solution.py:97
  64.7 5.8 fusion.127
  72.8 6.1 fusion.122
  79.0 9.7 fusion.212
  88.7 4.2 convolution_convert_fusion.11
  96.3 5.0 convolution_convert_fusion.1
  101.5 65.4 %reduce-scatter.5.cloned.1.call-done = bf16[192,2304]{1,0:T(8,128)(2,1)} async-done(((bf16[1536,2304]{1,0:T(8,128)(2,1)}), bf16[192,2304]{1,0:T(8,128)(2,1)}) %reduce-scatter.5.cloned.1.call-update) | async-done | bytes 884752 | tf_op jit(solution)/shard_map/reduce_scatter | solution.py:349
  170.1 2.6 multiply_convert_fusion.11
  172.8 48.9 %all-gather.9.cloned.1.call-done = bf16[1536,2304]{1,0:T(8,128)(2,1)} async-done(((bf16[192,2304]{1,0:T(8,128)(2,1)}), bf16[1536,2304]{1,0:T(8,128)(2,1)}) %all-gather.9.cloned.1.call-update) | async-done | bytes 7077904 | tf_op jit(solution)/shard_map/all_gather | solution.py:97
  221.7 15.0 %fusion.218 = f32[1536,1152]{1,0:T(8,128)} fusion(bf16[1536,2304]{1,0:T(8,128)(2,1)} %all-gather.9.cloned.1.call-done, bf16[1152,2304]{1,0:T(8,128)(2,1)} %param.25), kind=kOutput, calls=%fused_computation.328 | convolution fusion | flops 8153726976 | bytes 19464192 | tf_op jit(solution)/shard_map/dot_general | solution.py:331
  236.8 14.8 %multiply_convert_fusion.5 = (bf16[1536,1152]{1,0:T(8,128)(2,1)S(1)}, f32[1536,1152]{1,0:T(8,128)}) fusion(f32[1536,1152]{1,0:T(8,128)} %fusion.218, bf16[1536,2304]{1,0:T(8,128)(2,1)S(1)} %copy-done.41, bf16[1152,2304]{1,0:T(8,128)(2,1)} %param.26), kind=kOutput, calls=%fused_computation.61 | convolution fusion | flops 8171421696 | bytes 30081024 | tf_op jit(solution)/shard_map/dot_general | solution.py:331
  253.6 13.6 convolution_convert_fusion
  268.7 64.2 %reduce-scatter.7.cloned.1.call-done = bf16[192,2304]{1,0:T(8,128)(2,1)} async-done(((bf16[1536,2304]{1,0:T(8,128)(2,1)}), bf16[192,2304]{1,0:T(8,128)(2,1)}) %reduce-scatter.7.cloned.1.call-update) | async-done | bytes 884752 | tf_op jit(solution)/shard_map/reduce_scatter | solution.py:349
  334.3 2.8 fusion.99
  337.1 2.6 fusion.97
  340.0 48.7 %all-gather.11.cloned.1.call-done = bf16[1536,2304]{1,0:T(8,128)(2,1)} async-done(((bf16[192,2304]{1,0:T(8,128)(2,1)}), bf16[1536,2304]{1,0:T(8,128)(2,1)}) %all-gather.11.cloned.1.call-update) | async-done | bytes 7077904 | tf_op jit(solution)/shard_map/all_gather | solution.py:97
  388.7 21.0 %fusion.5 = (bf16[1536,1152]{1,0:T(8,128)(2,1)S(1)}, bf16[1536,1152]{1,0:T(8,128)(2,1)}) fusion(f32[1536,1152]{1,0:T(8,128)} %get-tuple-element.62, f32[1536,1152]{1,0:T(8,128)} %fusion.218, bf16[1536,2304]{1,0:T(8,128)(2,1)} %all-gather.11.cloned.1.call-done, bf16[1152,2304]{1,0:T(8,128)(2,1)} %param.27), kind=kOutput, calls=%fused_computation.38 | convolution fusion | flops 8190885888 | bytes 33619968 | tf_op jit(solution)/shard_map/dot_general | solution.py:331
  409.8 15.8 %fusion.219 = f32[1536,2304]{1,0:T(8,128)} fusion(bf16[1536,1152]{1,0:T(8,128)(2,1)S(1)} %get-tuple-element.63, bf16[1152,2304]{1,0:T(8,128)(2,1)} %param.25), kind=kOutput, calls=%fused_computation.329 | convolution fusion | flops 8153726976 | bytes 23003136 | tf_op jit(solution)/shard_map/dot_general | solution.py:337
  425.6 20.1 %add_convert_fusion = bf16[1536,2304]{1,0:T(8,128)(2,1)} fusion(f32[1536,2304]{1,0:T(8,128)} %fusion.219, bf16[1152,2304]{1,0:T(8,128)(2,1)} %param.26, bf16[1536,1152]{1,0:T(8,128)(2,1)} %get-tuple-element.64, f32[1536,1152]{1,0:T(8,128)} %fusion.218), kind=kOutput, calls=%fused_computation.2 | convolution fusion | flops 8180269056 | bytes 37158912 | tf_op jit(solution)/shard_map/dot_general | solution.py:337
  446.1 65.2 %reduce-scatter.9.cloned.1.call-done = bf16[192,2304]{1,0:T(8,128)(2,1)} async-done(((bf16[1536,2304]{1,0:T(8,128)(2,1)}), bf16[192,2304]{1,0:T(8,128)(2,1)}) %reduce-scatter.9.cloned.1.call-update) | async-done | bytes 884752 | tf_op jit(solution)/shard_map/reduce_scatter | solution.py:349
  511.3 4.5 fusion.81
  515.9 3.7 fusion.91
  522.9 48.2 %all-gather.13.cloned.1.call-done = bf16[1536,2304]{1,0:T(8,128)(2,1)} async-done(((bf16[192,2304]{1,0:T(8,128)(2,1)}), bf16[1536,2304]{1,0:T(8,128)(2,1)}) %all-gather.13.cloned.1.call-update) | async-done | bytes 7077904 | tf_op jit(solution)/shard_map/all_gather | solution.py:97
  571.1 5.2 convolution_convert_fusion.10
  576.3 6.4 fusion.74
  584.5 7.0 multiply_convert_fusion
  591.5 2.7 fusion.221
  600.2 5.2 fusion.114
  605.6 7.2 fusion.126
  614.1 5.2 fusion.124
  623.8 7.1 fusion.220
  630.9 7.2 convolution_add_fusion.1
  638.2 5.0 fusion
  644.6 15.3 %fusion.223 = f32[1152,2304]{1,0:T(8,128)} fusion(bf16[1536,1152]{1,0:T(8,128)(2,1)} %copy-done.44, bf16[1536,2304]{1,0:T(8,128)(2,1)} %all-gather.11.cloned.1.call-done), kind=kOutput, calls=%fused_computation.333 | convolution fusion | flops 8153726976 | bytes 21233664 | tf_op jit(solution)/shard_map/dot_general | solution.py:343
  659.8 15.4 %fusion.222 = f32[1152,2304]{1,0:T(8,128)} fusion(bf16[1536,1152]{1,0:T(8,128)(2,1)S(1)} %copy-done.46, bf16[1536,2304]{1,0:T(8,128)(2,1)} %all-gather.9.cloned.1.call-done), kind=kOutput, calls=%fused_computation.332 | convolution fusion | flops 8153726976 | bytes 21233664 | tf_op jit(solution)/shard_map/dot_general | solution.py:343
  675.3 11.6 fusion.207
  686.9 2.5 pad_maximum_fusion.2
  689.4 55.3 %all-gather.17.cloned.1.call-done = bf16[6144,2304]{1,0:T(8,128)(2,1)} async-done(((bf16[192,2304]{1,0:T(8,128)(2,1)}), bf16[6144,2304]{1,0:T(8,128)(2,1)}) %all-gather.17.cloned.1.call-update) | async-done | bytes 28311568 | tf_op jit(solution)/shard_map/all_gather | solution.py:444
  744.7 15.6 %fusion.40 = f32[1536,1152]{1,0:T(8,128)} fusion(bf16[1152,2304]{1,0:T(8,128)(2,1)} %param.25, bf16[6144,2304]{1,0:T(8,128)(2,1)} %all-gather.17.cloned.1.call-done, s32[]{:T(128)S(6)} %select_n.62), kind=kOutput, calls=%fused_computation.93 | convolution fusion | flops 8153726976 | bytes 19464196 | tf_op jit(solution)/shard_map/dot_general | solution.py:331
  760.3 15.1 %fusion.42 = f32[1536,1152]{1,0:T(8,128)} fusion(bf16[1152,2304]{1,0:T(8,128)(2,1)} %param.26, bf16[6144,2304]{1,0:T(8,128)(2,1)} %all-gather.17.cloned.1.call-done, s32[]{:T(128)S(6)} %select_n.62), kind=kOutput, calls=%fused_computation.95 | convolution fusion | flops 8153726976 | bytes 19464196 | tf_op jit(solution)/shard_map/dot_general | solution.py:331
  775.5 13.4 fusion.34
  788.9 13.6 fusion.36
  802.4 13.5 fusion.28
  816.0 13.5 fusion.30
  829.5 49.8 %all-reduce.3.cloned.1.call-done = bf16[768,2304]{1,0:T(8,128)(2,1)} async-done(((bf16[768,2304]{1,0:T(8,128)(2,1)}), bf16[768,2304]{1,0:T(8,128)(2,1)}) %all-reduce.3.cloned.1.call-update) | async-done | bytes 3538960 | tf_op jit(solution)/shard_map/psum | solution.py:492
  879.3 2.8 fusion.214
  882.1 4.1 fusion.213
  886.2 61.4 %reduce-scatter.11.cloned.1.call-done = bf16[192,2304]{1,0:T(8,128)(2,1)} async-done(((bf16[1536,2304]{1,0:T(8,128)(2,1)}), bf16[192,2304]{1,0:T(8,128)(2,1)}) %reduce-scatter.11.cloned.1.call-update) | async-done | bytes 884752 | tf_op jit(solution)/shard_map/reduce_scatter | solution.py:349
  949.3 43.0 %all-reduce = (f32[2304]{0:T(1024)}, f32[2304]{0:T(1024)}, f32[2304]{0:T(1024)}, f32[2304]{0:T(1024)}, f32[4]{0:T(128)S(1)}, /*index=5*/f32[]{:T(128)}) all-reduce(f32[2304]{0:T(1024)S(1)} %get-tuple-element.21, f32[2304]{0:T(1024)S(1)} %copy-done.31, ...), channel_id=1, replica_groups=mesh['replica'=4,'shard'=8] {'replica','shard'}, use_global_device_ids=true, to_apply=%region_24.25 | all-reduce | flops 9221 | bytes 73768 | tf_op jit(solution)/shard_map/psum | solution.py:512
  993.5 2.8 fusion.76
  996.4 125.1 %all-gather.15.cloned.1.call-done = bf16[6144,2304]{1,0:T(8,128)(2,1)} async-done(((bf16[192,2304]{1,0:T(8,128)(2,1)}), bf16[6144,2304]{1,0:T(8,128)(2,1)}) %all-gather.15.cloned.1.call-update) | async-done | bytes 28311568 | tf_op jit(solution)/shard_map/all_gather | solution.py:445
  1121.4 15.2 %convolution_convert_fusion.4 = bf16[1536,1152]{1,0:T(8,128)(2,1)} fusion(bf16[1152,2304]{1,0:T(8,128)(2,1)} %param.27, bf16[6144,2304]{1,0:T(8,128)(2,1)} %all-gather.15.cloned.1.call-done, s32[]{:T(128)S(6)} %select_n.62), kind=kOutput, calls=%fused_computation.35 | convolution fusion | flops 8155496448 | bytes 15925252 | tf_op jit(solution)/shard_map/dot_general | solution.py:331
  1136.6 14.4 %convolution_convert_fusion.3 = bf16[1536,1152]{1,0:T(8,128)(2,1)} fusion(bf16[1152,2304]{1,0:T(8,128)(2,1)} %param.27, bf16[6144,2304]{1,0:T(8,128)(2,1)} %all-gather.15.cloned.1.call-done, s32[]{:T(128)S(6)} %select_n.63), kind=kOutput, calls=%fused_computation.34 | convolution fusion | flops 8155496448 | bytes 15925252 | tf_op jit(solution)/shard_map/dot_general | solution.py:331
  1151.1 11.5 convolution_convert_fusion.2
  1162.6 21.8 %convolution_add_fusion.4 = f32[1152,2304]{1,0:T(8,128)} fusion(f32[1152,2304]{1,0:T(8,128)} %fusion.223, bf16[6144,2304]{1,0:T(8,128)(2,1)} %all-gather.15.cloned.1.call-done, s32[]{:T(128)S(6)} %select_n.62, f32[1536,1152]{1,0:T(8,128)} %fusion.42, f32[1536,1152]{1,0:T(8,128)} %fusion.40), kind=kOutput, calls=%fused_computation.5 | convolution fusion | flops 8174075904 | bytes 42467332 | tf_op jit(solution)/shard_map/dot_general | solution.py:343
  1184.4 21.6 %convolution_add_fusion.7 = f32[1152,2304]{1,0:T(8,128)} fusion(f32[1152,2304]{1,0:T(8,128)} %fusion.207, bf16[6144,2304]{1,0:T(8,128)(2,1)} %all-gather.17.cloned.1.call-done, s32[]{:T(128)S(6)} %select_n.62, bf16[1536,1152]{1,0:T(8,128)(2,1)} %convolution_convert_fusion.4, f32[1536,1152]{1,0:T(8,128)} %fusion.40), kind=kOutput, calls=%fused_computation.8 | convolution fusion | flops 8175845376 | bytes 38928388 | tf_op jit(solution)/shard_map/dot_general | solution.py:343
  1206.0 20.7 %convolution_add_fusion.10 = f32[1152,2304]{1,0:T(8,128)} fusion(f32[1152,2304]{1,0:T(8,128)} %fusion.222, bf16[6144,2304]{1,0:T(8,128)(2,1)} %all-gather.17.cloned.1.call-done, s32[]{:T(128)S(6)} %select_n.62, f32[1536,1152]{1,0:T(8,128)} %fusion.42, bf16[1536,1152]{1,0:T(8,128)(2,1)S(1)} %copy-done.43, f32[1536,1152]{1,0:T(8,128)} %fusion.40), kind=kOutput, calls=%fused_computation.11 | convolution fusion | flops 8191770624 | bytes 46006276 | tf_op jit(solution)/shard_map/dot_general | solution.py:343
  1226.6 21.6 %convolution_add_fusion.3 = f32[1152,2304]{1,0:T(8,128)} fusion(f32[1152,2304]{1,0:T(8,128)} %convolution_add_fusion.4, bf16[6144,2304]{1,0:T(8,128)(2,1)} %all-gather.15.cloned.1.call-done, s32[]{:T(128)S(6)} %select_n.63, f32[1536,1152]{1,0:T(8,128)} %fusion.36, f32[1536,1152]{1,0:T(8,128)} %fusion.34), kind=kOutput, calls=%fused_computation.4 | convolution fusion | flops 8174075904 | bytes 42467332 | tf_op jit(solution)/shard_map/dot_general | solution.py:343
  1248.2 23.0 %convolution_add_fusion.6 = f32[1152,2304]{1,0:T(8,128)} fusion(f32[1152,2304]{1,0:T(8,128)} %convolution_add_fusion.7, bf16[6144,2304]{1,0:T(8,128)(2,1)} %all-gather.17.cloned.1.call-done, s32[]{:T(128)S(6)} %select_n.63, bf16[1536,1152]{1,0:T(8,128)(2,1)} %convolution_convert_fusion.3, f32[1536,1152]{1,0:T(8,128)} %fusion.34), kind=kOutput, calls=%fused_computation.7 | convolution fusion | flops 8175845376 | bytes 38928388 | tf_op jit(solution)/shard_map/dot_general | solution.py:343
  1271.2 20.4 %convolution_add_fusion.9 = f32[1152,2304]{1,0:T(8,128)} fusion(f32[1152,2304]{1,0:T(8,128)} %convolution_add_fusion.10, bf16[6144,2304]{1,0:T(8,128)(2,1)} %all-gather.17.cloned.1.call-done, s32[]{:T(128)S(6)} %select_n.63, f32[1536,1152]{1,0:T(8,128)} %fusion.36, bf16[1536,1152]{1,0:T(8,128)(2,1)S(1)} %copy-done.42, f32[1536,1152]{1,0:T(8,128)} %fusion.34), kind=kOutput, calls=%fused_computation.10 | convolution fusion | flops 8191770624 | bytes 46006276 | tf_op jit(solution)/shard_map/dot_general | solution.py:343
  1291.7 21.8 %convolution_add_fusion.2 = f32[1152,2304]{1,0:T(8,128)} fusion(f32[1152,2304]{1,0:T(8,128)} %convolution_add_fusion.3, bf16[6144,2304]{1,0:T(8,128)(2,1)} %all-gather.15.cloned.1.call-done, s32[]{:T(128)S(6)} %select_n.64, f32[1536,1152]{1,0:T(8,128)} %fusion.30, f32[1536,1152]{1,0:T(8,128)} %fusion.28), kind=kOutput, calls=%fused_computation.3 | convolution fusion | flops 8174075904 | bytes 42467332 | tf_op jit(solution)/shard_map/dot_general | solution.py:343
  1313.5 20.5 %convolution_add_fusion.5 = f32[1152,2304]{1,0:T(8,128)} fusion(f32[1152,2304]{1,0:T(8,128)} %convolution_add_fusion.6, bf16[6144,2304]{1,0:T(8,128)(2,1)} %all-gather.17.cloned.1.call-done, s32[]{:T(128)S(6)} %select_n.64, bf16[1536,1152]{1,0:T(8,128)(2,1)S(1)} %convolution_convert_fusion.2, f32[1536,1152]{1,0:T(8,128)} %fusion.28), kind=kOutput, calls=%fused_computation.6 | convolution fusion | flops 8175845376 | bytes 38928388 | tf_op jit(solution)/shard_map/dot_general | solution.py:343
  1334.0 20.7 %convolution_add_fusion.8 = f32[1152,2304]{1,0:T(8,128)} fusion(f32[1152,2304]{1,0:T(8,128)} %convolution_add_fusion.9, bf16[6144,2304]{1,0:T(8,128)(2,1)} %all-gather.17.cloned.1.call-done, s32[]{:T(128)S(6)} %select_n.64, f32[1536,1152]{1,0:T(8,128)} %fusion.30, bf16[1536,1152]{1,0:T(8,128)(2,1)S(1)} %convolution_convert_fusion.2, f32[1536,1152]{1,0:T(8,128)} %fusion.28), kind=kOutput, calls=%fused_computation.9 | convolution fusion | flops 8191770624 | bytes 46006276 | tf_op jit(solution)/shard_map/dot_general | solution.py:343
  (210 shorter events, 44.4 us)
Async XLA Ops:
  7.2 89.1 %copy-start = (bf16[256,2304]{1,0:T(8,128)(2,1)S(1)}, bf16[256,2304]{1,0:T(8,128)(2,1)}, u32[]{:S(2)}) copy-start(bf16[256,2304]{1,0:T(8,128)(2,1)} %param.24) | copy-start | bytes 3538948
  7.2 57.5 %all-gather.7.cloned.1.call-start = ((), (), s32[]{:S(2)}) async-start(), calls=%async_computation.4 | async-start | bytes 7962624 | tf_op jit(solution)/shard_map/all_gather | solution.py:97
  13.0 153.9 %reduce-scatter.5.cloned.1.call-start = ((), (), s32[]{:S(2)}) async-start(), calls=%async_computation.5 | async-start | bytes 7962624 | tf_op jit(solution)/shard_map/reduce_scatter | solution.py:349
  13.0 5.6 collective-permute-start
  13.5 75.2 %collective-permute-start.1 = (bf16[128,2304]{1,0:T(8,128)(2,1)}, bf16[128,2304]{1,0:T(8,128)(2,1)}, u32[]{:S(2)}, u32[]{:S(2)}) collective-permute-start(bf16[128,2304]{1,0:T(8,128)(2,1)} %param.23), channel_id=1, source_target_pairs={{0,1},{1,0},{2,3},{3,2},{4,5},{5,4},{6,7},{7,6},{8,9},{9,8},{10,11... | collective-permute-start | bytes 1769480 | tf_op jit(solution)/shard_map/ppermute | solution.py:404
  18.6 54.1 %copy-start.6 = (f32[1536,128]{0,1:T(8,128)}, f32[1536,128]{0,1:T(8,128)S(1)}, u32[]{:S(2)}) copy-start(f32[1536,128]{0,1:T(8,128)S(1)} %broadcast_multiply_fusion) | copy-start | bytes 2359300
  18.7 51.9 %copy-start.21 = (bf16[256,2304]{1,0:T(8,128)(2,1)S(1)}, bf16[256,2304]{1,0:T(8,128)(2,1)}, u32[]{:S(2)}) copy-start(bf16[256,2304]{1,0:T(8,128)(2,1)} %param.21) | copy-start | bytes 3538948
  64.7 5.9 copy-start.40
  72.6 6.3 copy-start.32
  78.9 9.8 copy-start.13
  78.9 9.8 copy-start.23
  79.0 9.8 copy-start.24
  96.3 5.2 copy-start.37
  96.3 72.1 %copy-start.3 = (bf16[192,2304]{1,0:T(8,128)(2,1)S(1)}, bf16[192,2304]{1,0:T(8,128)(2,1)}, u32[]{:S(2)}) copy-start(bf16[192,2304]{1,0:T(8,128)(2,1)} %param.16) | copy-start | bytes 2654212
  101.3 120.5 %all-gather.9.cloned.1.call-start = ((), (), s32[]{:S(2)}) async-start(), calls=%async_computation.6 | async-start | bytes 7962624 | tf_op jit(solution)/shard_map/all_gather | solution.py:97
  172.7 160.1 %reduce-scatter.7.cloned.1.call-start = ((), (), s32[]{:S(2)}) async-start(), calls=%async_computation.7 | async-start | bytes 7962624 | tf_op jit(solution)/shard_map/reduce_scatter | solution.py:349
  221.7 15.0 %copy-start.41 = (bf16[1536,2304]{1,0:T(8,128)(2,1)S(1)}, bf16[1536,2304]{1,0:T(8,128)(2,1)}, u32[]{:S(2)}) copy-start(bf16[1536,2304]{1,0:T(8,128)(2,1)} %all-gather.9.cloned.1.call-done) | copy-start | bytes 21233668
  267.2 67.1 %copy-start.12 = (bf16[192,2304]{1,0:T(8,128)(2,1)S(1)}, bf16[192,2304]{1,0:T(8,128)(2,1)}, u32[]{:S(2)}) copy-start(bf16[192,2304]{1,0:T(8,128)(2,1)} %param.17) | copy-start | bytes 2654212
  267.2 121.5 %all-gather.11.cloned.1.call-start = ((), (), s32[]{:S(2)}) async-start(), calls=%async_computation.8 | async-start | bytes 7962624 | tf_op jit(solution)/shard_map/all_gather | solution.py:97
  339.7 171.6 %reduce-scatter.9.cloned.1.call-start = ((), (), s32[]{:S(2)}) async-start(), calls=%async_computation.9 | async-start | bytes 7962624 | tf_op jit(solution)/shard_map/reduce_scatter | solution.py:349
  409.8 15.8 %copy-start.45 = (bf16[1536,1152]{1,0:T(8,128)(2,1)}, bf16[1536,1152]{1,0:T(8,128)(2,1)S(1)}, u32[]{:S(2)}) copy-start(bf16[1536,1152]{1,0:T(8,128)(2,1)S(1)} %get-tuple-element.63) | copy-start | bytes 10616836
  445.7 65.7 %copy-start.5 = (bf16[192,2304]{1,0:T(8,128)(2,1)S(1)}, bf16[192,2304]{1,0:T(8,128)(2,1)}, u32[]{:S(2)}) copy-start(bf16[192,2304]{1,0:T(8,128)(2,1)} %reduce-scatter.5.cloned.1.call-done) | copy-start | bytes 2654212
  445.7 125.4 %all-gather.13.cloned.1.call-start = ((), (), s32[]{:S(2)}) async-start(), calls=%async_computation.10 | async-start | bytes 7962624 | tf_op jit(solution)/shard_map/all_gather | solution.py:97
  522.1 222.6 %all-gather.17.cloned.1.call-start = ((), (), s32[]{:S(2)}) async-start(), calls=%async_computation.14 | async-start | bytes 29196288 | tf_op jit(solution)/shard_map/all_gather | solution.py:444
  522.9 356.4 %all-reduce.3.cloned.1.call-start = ((), (), s32[]{:S(2)}) async-start(), calls=%async_computation.12 | async-start | bytes 7077888 | tf_op jit(solution)/shard_map/psum | solution.py:492
  571.1 11.9 slice-start
  571.1 11.9 slice-start.1
  576.3 6.7 slice-start.2
  576.3 6.7 copy-start.16
  582.8 13.9 %collective-permute-start.3 = (f32[1536,256]{0,1:T(8,128)}, f32[1536,256]{0,1:T(8,128)}, u32[]{:S(2)}, u32[]{:S(2)}) collective-permute-start(f32[1536,256]{0,1:T(8,128)} %fusion.74), channel_id=1, source_target_pairs={{0,1},{1,0},{2,3},{3,2},{4,5},{5,4},{6,7},{7,6},{8,9},{9,8},{10,11... | collective-permute-start | bytes 4718600 | tf_op jit(solution)/shard_map/ppermute | solution.py:471
  583.0 11.5 slice-start.3
  584.5 10.1 slice-start.4
  591.5 7.3 slice-start.5
  594.2 5.8 collective-permute-start.2
  600.0 5.6 copy-start.14
  623.4 7.5 copy-start.18
  623.4 324.2 %reduce-scatter.11.cloned.1.call-start = ((), (), s32[]{:S(2)}) async-start(), calls=%async_computation.11 | async-start | bytes 7962624 | tf_op jit(solution)/shard_map/reduce_scatter | solution.py:349
  623.8 7.1 copy-start.26
  630.9 7.2 copy-start.20
  630.9 7.2 copy-start.25
  643.1 478.3 %all-gather.15.cloned.1.call-start = ((), (), s32[]{:S(2)}) async-start(), calls=%async_computation.13 | async-start | bytes 29196288 | tf_op jit(solution)/shard_map/all_gather | solution.py:445
  644.5 15.3 %copy-start.46 = (bf16[1536,1152]{1,0:T(8,128)(2,1)S(1)}, bf16[1536,1152]{1,0:T(8,128)(2,1)}, u32[]{:S(2)}) copy-start(bf16[1536,1152]{1,0:T(8,128)(2,1)} %copy-done.45) | copy-start | bytes 10616836
  644.6 30.7 %slice-start.7 = ((s8[7077888]{0:T(1024)(128)(4,1)}), s8[4194304]{0:T(1024)(128)(4,1)S(1)}, s32[]{:S(2)}) async-start(s8[7077888]{0:T(1024)(128)(4,1)} %bitcast.85), calls=%async_computation.22 | async-start | bytes 8388608
  644.6 30.7 %slice-start.15 = ((s8[7077888]{0:T(1024)(128)(4,1)}), s8[4194304]{0:T(1024)(128)(4,1)S(1)}, s32[]{:S(2)}) async-start(s8[7077888]{0:T(1024)(128)(4,1)} %bitcast.93), calls=%async_computation.30 | async-start | bytes 8388608
  659.8 15.4 %slice-start.8 = ((s8[7077888]{0:T(1024)(128)(4,1)}), s8[2883584]{0:T(1024)(128)(4,1)S(1)}, s32[]{:S(2)}) async-start(s8[7077888]{0:T(1024)(128)(4,1)} %bitcast.85), calls=%async_computation.23 | async-start | bytes 5767168
  659.8 15.4 %slice-start.16 = ((s8[7077888]{0:T(1024)(128)(4,1)}), s8[2883584]{0:T(1024)(128)(4,1)S(1)}, s32[]{:S(2)}) async-start(s8[7077888]{0:T(1024)(128)(4,1)} %bitcast.93), calls=%async_computation.31 | async-start | bytes 5767168
  659.8 15.4 %copy-start.47 = (bf16[1536,1152]{1,0:T(8,128)(2,1)S(1)}, bf16[1536,1152]{1,0:T(8,128)(2,1)}, u32[]{:S(2)}) copy-start(bf16[1536,1152]{1,0:T(8,128)(2,1)} %get-tuple-element.64) | copy-start | bytes 10616836
  744.7 30.7 %slice-start.9 = ((s8[5308416]{0:T(1024)(128)(4,1)}), s8[4194304]{0:T(1024)(128)(4,1)S(1)}, s32[]{:S(2)}) async-start(s8[5308416]{0:T(1024)(128)(4,1)} %bitcast.87), calls=%async_computation.24 | async-start | bytes 8388608
  760.3 15.1 %slice-start.10 = ((s8[5308416]{0:T(1024)(128)(4,1)}), s8[1114112]{0:T(1024)(128)(4,1)S(1)}, s32[]{:S(2)}) async-start(s8[5308416]{0:T(1024)(128)(4,1)} %bitcast.87), calls=%async_computation.25 | async-start | bytes 2228224
  760.3 28.5 %slice-start.11 = ((s8[5308416]{0:T(1024)(128)(4,1)}), s8[4194304]{0:T(1024)(128)(4,1)S(1)}, s32[]{:S(2)}) async-start(s8[5308416]{0:T(1024)(128)(4,1)} %bitcast.89), calls=%async_computation.26 | async-start | bytes 8388608
  775.5 13.4 slice-start.12
  829.4 118.1 %copy-start.4 = (bf16[192,2304]{1,0:T(8,128)(2,1)S(1)}, bf16[192,2304]{1,0:T(8,128)(2,1)}, u32[]{:S(2)}) copy-start(bf16[192,2304]{1,0:T(8,128)(2,1)} %param.16) | copy-start | bytes 2654212
  829.4 118.1 %copy-start.28 = (f32[2304]{0:T(1024)S(1)}, f32[2304]{0:T(1024)}, u32[]{:S(2)}) copy-start(f32[2304]{0:T(1024)} %copy-done.27) | copy-start | bytes 27652
  829.4 118.1 %copy-start.34 = (f32[192]{0:T(256)S(1)}, f32[192]{0:T(256)}, u32[]{:S(2)}) copy-start(f32[192]{0:T(256)} %copy-done.33) | copy-start | bytes 2308
  829.4 119.8 %copy-start.29 = (f32[2304]{0:T(1024)S(1)}, f32[2304]{0:T(1024)}, u32[]{:S(2)}) copy-start(f32[2304]{0:T(1024)} %get-tuple-element.19) | copy-start | bytes 27652
  829.5 119.8 %copy-start.30 = (f32[2304]{0:T(1024)S(1)}, f32[2304]{0:T(1024)}, u32[]{:S(2)}) copy-start(f32[2304]{0:T(1024)} %get-tuple-element.14) | copy-start | bytes 27652
  829.5 119.8 %copy-start.31 = (f32[2304]{0:T(1024)S(1)}, f32[2304]{0:T(1024)}, u32[]{:S(2)}) copy-start(f32[2304]{0:T(1024)} %get-tuple-element.16) | copy-start | bytes 27652
  829.5 164.0 %copy-start.39 = (f32[192]{0:T(256)S(1)}, f32[192]{0:T(256)}, u32[]{:S(2)}) copy-start(f32[192]{0:T(256)} %copy-done.38) | copy-start | bytes 2308
  829.5 164.0 %copy-start.11 = (f32[192,2304]{1,0:T(8,128)S(1)}, f32[192,2304]{1,0:T(8,128)}, u32[]{:S(2)}) copy-start(f32[192,2304]{1,0:T(8,128)} %copy-done.10) | copy-start | bytes 5308420
  1121.4 29.6 %slice-start.13 = ((s8[5308416]{0:T(1024)(128)(4,1)}), s8[4194304]{0:T(1024)(128)(4,1)S(1)}, s32[]{:S(2)}) async-start(s8[5308416]{0:T(1024)(128)(4,1)} %bitcast.91), calls=%async_computation.28 | async-start | bytes 8388608
  1136.6 14.4 %slice-start.14 = ((s8[5308416]{0:T(1024)(128)(4,1)}), s8[1114112]{0:T(1024)(128)(4,1)S(1)}, s32[]{:S(2)}) async-start(s8[5308416]{0:T(1024)(128)(4,1)} %bitcast.91), calls=%async_computation.29 | async-start | bytes 2228224
  1184.4 21.6 %copy-start.43 = (bf16[1536,1152]{1,0:T(8,128)(2,1)S(1)}, bf16[1536,1152]{1,0:T(8,128)(2,1)}, u32[]{:S(2)}) copy-start(bf16[1536,1152]{1,0:T(8,128)(2,1)} %convolution_convert_fusion.4) | copy-start | bytes 10616836
  1248.2 23.0 %copy-start.42 = (bf16[1536,1152]{1,0:T(8,128)(2,1)S(1)}, bf16[1536,1152]{1,0:T(8,128)(2,1)}, u32[]{:S(2)}) copy-start(bf16[1536,1152]{1,0:T(8,128)(2,1)} %convolution_convert_fusion.3) | copy-start | bytes 10616836
  1334.0 20.7 %copy-start.1 = (bf16[256,2304]{1,0:T(8,128)(2,1)S(1)}, bf16[256,2304]{1,0:T(8,128)(2,1)}, u32[]{:S(2)}) copy-start(bf16[256,2304]{1,0:T(8,128)(2,1)} %param.24) | copy-start | bytes 3538948
  (16 other events, 31.8 us)
Sparse Core Ops, SparseCore 0:
  13.1 51.5 all-gather.6
  101.4 65.4 reduce-scatter.4
  172.8 48.8 all-gather.8
  267.3 65.5 reduce-scatter.6
  339.8 48.8 all-gather.10
  445.8 65.4 reduce-scatter.8
  522.2 48.8 all-gather.12
  575.0 169.6 all-gather.16
  747.2 131.9 all-reduce.2
  883.0 64.4 reduce-scatter.10
  950.5 170.9 all-gather.14

commit v2 on v1

--- a/solution.py
+++ b/solution.py
@@ -1,8 +1,11 @@
+import functools
 import math
 
 import jax
 import jax.numpy as jnp
 from jax import lax
+from jax.experimental import pallas as pl
+from jax.experimental.pallas import tpu as pltpu
 from jax.sharding import PartitionSpec as P
 
 HEADS = 8
@@ -360,6 +363,504 @@
         1.0 + 3.0 * 0.044715 * square
     )
     return gate_lin * half_up, slope
+
+
+MESH_ID = pl.DeviceIdType.MESH
+VMEM_BYTES = 62 * 2**20
+ROOT = math.sqrt(2.0 / math.pi)
+
+
+class Plane:
+    def __init__(self):
+        self.me = lax.axis_index("shard")
+        core = lax.rem(self.me, 2)
+        x = lax.rem(lax.div(self.me, 2), 2)
+        y = lax.div(self.me, 4)
+        self.core = core
+        self.own_chip = 2 * y + x
+        self.x_chip = 2 * y + 1 - x
+        self.y_chip = 2 * (1 - y) + x
+        self.diag_chip = 2 * (1 - y) + 1 - x
+        self.mate = self.me + 1 - 2 * core
+        self.x_dev = 2 * self.x_chip + core
+        self.y_dev = 2 * self.y_chip + core
+        self.diag_dev = 2 * self.diag_chip + core
+
+    def near(self):
+        return [{"shard": dev} for dev in (self.mate, self.x_dev, self.y_dev)]
+
+
+class Wires:
+    def __init__(self, send_sem, recv_sem):
+        self.send_sem, self.recv_sem = send_sem, recv_sem
+        self.sent = []
+
+    def send(self, source, target, device):
+        at = len(self.sent)
+        copy = pltpu.make_async_remote_copy(
+            src_ref=source,
+            dst_ref=target,
+            send_sem=self.send_sem.at[at],
+            recv_sem=self.recv_sem.at[at],
+            device_id=device if isinstance(device, dict) else {"shard": device},
+            device_id_type=MESH_ID,
+        )
+        copy.start()
+        self.sent.append(copy)
+        return copy
+
+    def finish(self):
+        for copy in self.sent:
+            copy.wait_send()
+
+
+def greet(devices):
+    barrier = pltpu.get_barrier_semaphore()
+    for device in devices:
+        pl.semaphore_signal(barrier, inc=1, device_id=device, device_id_type=MESH_ID)
+    pl.semaphore_wait(barrier, len(devices))
+
+
+def block_rows(ref, start, size, step=16):
+    return ref.at[pl.ds(pl.multiple_of(start, step), size)]
+
+
+def by_rows(count, body, size=32):
+    def step(at, carry):
+        body(pl.ds(pl.multiple_of(at * size, size), size))
+        return carry
+
+    lax.fori_loop(0, count // size, step, 0)
+
+
+def column_tile(width):
+    return max(t for t in range(128, 769, 128) if width % t == 0)
+
+
+def by_columns(width, body):
+    tile = column_tile(width)
+
+    def step(at, carry):
+        body(pl.ds(pl.multiple_of(at * tile, 128), tile))
+        return carry
+
+    lax.fori_loop(0, width // tile, step, 0)
+
+
+def gather_tree(wires, plane, own, tree, rows, use):
+    half = rows // 2
+
+    def part(dev, start, size):
+        return block_rows(tree, dev * rows + start, size)
+
+    def own_part(start, size):
+        return own.at[pl.ds(start, size)]
+
+    me, mate = plane.me, plane.mate
+    first_x = wires.send(own_part(0, half), part(me, 0, half), plane.x_dev)
+    first_y = wires.send(own_part(half, half), part(me, half, half), plane.y_dev)
+    to_mate = wires.send(own_part(0, rows), part(me, 0, rows), mate)
+    rest_x = wires.send(own_part(half, half), part(me, half, half), plane.x_dev)
+    rest_y = wires.send(own_part(0, half), part(me, 0, half), plane.y_dev)
+    to_mate.wait_recv()
+    use(plane.own_chip)
+    first_x.wait_recv()
+    turn_y = wires.send(part(plane.x_dev, 0, half), part(plane.x_dev, 0, half), plane.y_dev)
+    first_y.wait_recv()
+    turn_x = wires.send(part(plane.y_dev, half, half), part(plane.y_dev, half, half), plane.x_dev)
+    rest_x.wait_recv()
+    mate_x = wires.send(part(plane.x_dev, 0, rows), part(plane.x_dev, 0, rows), mate)
+    rest_y.wait_recv()
+    mate_y = wires.send(part(plane.y_dev, 0, rows), part(plane.y_dev, 0, rows), mate)
+    mate_x.wait_recv()
+    use(plane.x_chip)
+    turn_y.wait_recv()
+    turn_x.wait_recv()
+    mate_diag = wires.send(part(plane.diag_dev, 0, rows), part(plane.diag_dev, 0, rows), mate)
+    mate_y.wait_recv()
+    use(plane.y_chip)
+    mate_diag.wait_recv()
+    use(plane.diag_chip)
+
+
+GATHER_COPIES = 10
+
+
+def scatter_scratch(rows, width):
+    half = rows // 2
+    low = jnp.bfloat16
+    return [
+        pltpu.VMEM((3, rows, width), jnp.float32),
+        pltpu.VMEM((2 * rows, column_tile(width)), jnp.float32),
+        pltpu.VMEM((2, rows, width), low),
+        pltpu.VMEM((4, rows, width), low),
+        pltpu.VMEM((3, half, width), low),
+        pltpu.VMEM((3, half, width), low),
+        pltpu.VMEM((3, half, width), low),
+        pltpu.VMEM((3, half, width), low),
+    ]
+
+
+def scatter_sum(wires, plane, scratch, product, total):
+    sums, piece, mate_out, mate_in, x_out, x_in, y_out, y_in = scratch
+    rows, width = total.shape
+    half = rows // 2
+    low, full = jnp.bfloat16, jnp.float32
+
+    def produce(slot, out_slot, in_slot, chip):
+        def tile(columns):
+            piece[...] = product(chip, columns)
+            sums[slot, :, columns] = piece[block_at(plane.core * rows, rows), :]
+            mate_out[out_slot, :, columns] = piece[
+                block_at((1 - plane.core) * rows, rows), :
+            ].astype(low)
+
+        by_columns(width, tile)
+        return wires.send(mate_out.at[out_slot], mate_in.at[in_slot], plane.mate)
+
+    def low_part(out, out_slot, slot, in_slot, start, more=None):
+        def step(at):
+            there = pl.ds(pl.multiple_of(start + at.start, 16), at.size)
+            value = sums[slot, there, :] + mate_in[in_slot, there, :].astype(full)
+            if more is not None:
+                value += more[0, at, :].astype(full)
+            out[out_slot, at, :] = value.astype(low)
+
+        by_rows(half, step)
+
+    diag = produce(0, 0, 0, plane.diag_chip)
+    to_x = produce(1, 1, 1, plane.x_chip)
+    diag.wait_recv()
+    low_part(x_out, 0, 0, 0, 0)
+    x_first = wires.send(x_out.at[0], x_in.at[0], plane.x_dev)
+    low_part(y_out, 0, 0, 0, half)
+    y_first = wires.send(y_out.at[0], y_in.at[0], plane.y_dev)
+    diag.wait_send()
+    to_y = produce(2, 0, 2, plane.y_chip)
+    to_x.wait_recv()
+    low_part(x_out, 1, 1, 1, 0)
+    x_next = wires.send(x_out.at[1], x_in.at[1], plane.x_dev)
+    to_x.wait_send()
+    to_own = produce(0, 1, 3, plane.own_chip)
+    to_y.wait_recv()
+    low_part(y_out, 1, 2, 2, half)
+    y_next = wires.send(y_out.at[1], y_in.at[1], plane.y_dev)
+    y_first.wait_recv()
+    low_part(x_out, 2, 1, 1, half, y_in)
+    x_last = wires.send(x_out.at[2], x_in.at[2], plane.x_dev)
+    x_first.wait_recv()
+    low_part(y_out, 2, 2, 2, 0, x_in)
+    y_last = wires.send(y_out.at[2], y_in.at[2], plane.y_dev)
+    to_own.wait_recv()
+    for copy in (x_next, y_next, x_last, y_last):
+        copy.wait_recv()
+    for start, x_slot, y_slot in ((0, 1, 2), (half, 2, 1)):
+
+        def step(at, start=start, x_slot=x_slot, y_slot=y_slot):
+            there = pl.ds(pl.multiple_of(start + at.start, 16), at.size)
+            total[there, :] = (
+                sums[0, there, :]
+                + mate_in[3, there, :].astype(full)
+                + x_in[x_slot, at, :].astype(full)
+                + y_in[y_slot, at, :].astype(full)
+            )
+
+        by_rows(half, step)
+    for copy in (to_y, to_own, x_first, x_next, x_last, y_first, y_next, y_last):
+        copy.wait_send()
+
+
+SCATTER_COPIES = 10
+
+
+def block_at(start, size):
+    return pl.ds(pl.multiple_of(start, 16), size)
+
+
+def load(source, target, sem):
+    copy = pltpu.make_async_copy(source, target, sem)
+    copy.start()
+    return copy
+
+
+def replica_peers(replicas):
+    z = lax.axis_index("replica")
+    return z, [{"replica": lax.rem(z + step, replicas)} for step in range(1, replicas)]
+
+
+def forward_kernel(
+    replicas,
+    own,
+    gate_hbm,
+    up_hbm,
+    down_hbm,
+    tree_out,
+    hidden_out,
+    mix_out,
+    gelu_out,
+    every_out,
+    total,
+    tree,
+    gate_w,
+    up_w,
+    down_w,
+    hidden,
+    mix,
+    gelu,
+    gate_lin,
+    up_lin,
+    send_sem,
+    recv_sem,
+    local_sem,
+    *scratch,
+):
+    plane = Plane()
+    rows = own.shape[0]
+    wires = Wires(send_sem, recv_sem)
+    loads = [
+        load(gate_hbm, gate_w, local_sem.at[0]),
+        load(up_hbm, up_w, local_sem.at[1]),
+        load(down_hbm, down_w, local_sem.at[2]),
+    ]
+    z, others = replica_peers(replicas)
+    greet(plane.near() + others)
+    tree[block_at(plane.me * rows, rows), :] = own[...]
+    stores = []
+
+    def use(chip):
+        order = len(stores) // 3
+        slot = order % 2
+        if order == 0:
+            loads[0].wait()
+            loads[1].wait()
+        if order >= 2:
+            stores[3 * (order - 2) + 1].wait()
+            stores[3 * (order - 2) + 2].wait()
+        there = block_at(chip * 2 * rows, 2 * rows)
+        gate_lin[...] = dot_nt(tree[there, :], gate_w[...])
+        up_lin[...] = dot_nt(tree[there, :], up_w[...])
+
+        def step(at):
+            gelu_value, slope = gelu_parts(gate_lin[at, :])
+            up_value = up_lin[at, :]
+            mix[slot, at, :] = (up_value * slope).astype(jnp.bfloat16)
+            gelu[slot, at, :] = gelu_value.astype(jnp.bfloat16)
+            hidden[block_at(chip * 2 * rows + at.start, at.size), :] = (
+                gelu_value * up_value
+            ).astype(jnp.bfloat16)
+
+        by_rows(2 * rows, step, 16)
+        base = 3 + 3 * order
+        stores.append(load(hidden.at[there], hidden_out.at[there], local_sem.at[base]))
+        stores.append(load(mix.at[slot], mix_out.at[there], local_sem.at[base + 1]))
+        stores.append(load(gelu.at[slot], gelu_out.at[there], local_sem.at[base + 2]))
+
+    over = [wires.send(own, every_out.at[z], other) for other in others]
+    gather_tree(wires, plane, own, tree, rows, use)
+    tree_store = load(tree, tree_out, local_sem.at[15])
+    loads[2].wait()
+
+    def product(chip, columns):
+        return dot_nn(hidden[block_at(chip * 2 * rows, 2 * rows), :], down_w[:, columns])
+
+    gathered = list(wires.sent)
+    scatter_sum(wires, plane, scratch, product, total)
+    for copy in over:
+        copy.wait_recv()
+    for copy in gathered:
+        copy.wait_send()
+    for copy in stores[0:1] + stores[3:4] + stores[6:] + [tree_store]:
+        copy.wait()
+
+
+def any_specs(count):
+    return [pl.BlockSpec(memory_space=pl.ANY)] * count
+
+
+def vmem_specs(count):
+    return [pl.BlockSpec(memory_space=pltpu.VMEM)] * count
+
+
+def remote_params(identity):
+    return pltpu.CompilerParams(
+        collective_id=identity, has_side_effects=True, vmem_limit_bytes=VMEM_BYTES
+    )
+
+
+def feedforward_forward(own, gate_weight, up_weight, down_weight):
+    rows, width = own.shape
+    units = gate_weight.shape[0]
+    replicas, count = lax.axis_size("replica"), lax.axis_size("shard")
+    tree_rows = count * rows
+    low, full = jnp.bfloat16, jnp.float32
+    copies = GATHER_COPIES + SCATTER_COPIES + replicas - 1
+    return pl.pallas_call(
+        functools.partial(forward_kernel, replicas),
+        out_shape=(
+            jax.ShapeDtypeStruct((tree_rows, width), low),
+            jax.ShapeDtypeStruct((tree_rows, units), low),
+            jax.ShapeDtypeStruct((tree_rows, units), low),
+            jax.ShapeDtypeStruct((tree_rows, units), low),
+            jax.ShapeDtypeStruct((replicas, rows, width), low),
+            jax.ShapeDtypeStruct((rows, width), full),
+        ),
+        in_specs=vmem_specs(1) + any_specs(3),
+        out_specs=tuple(any_specs(5) + vmem_specs(1)),
+        scratch_shapes=[
+            pltpu.VMEM((tree_rows, width), low),
+            pltpu.VMEM((units, width), low),
+            pltpu.VMEM((units, width), low),
+            pltpu.VMEM((units, width), low),
+            pltpu.VMEM((tree_rows, units), low),
+            pltpu.VMEM((2, 2 * rows, units), low),
+            pltpu.VMEM((2, 2 * rows, units), low),
+            pltpu.VMEM((2 * rows, units), full),
+            pltpu.VMEM((2 * rows, units), full),
+            pltpu.SemaphoreType.DMA((copies,)),
+            pltpu.SemaphoreType.DMA((copies,)),
+            pltpu.SemaphoreType.DMA((16,)),
+        ]
+        + scatter_scratch(rows, width),
+        compiler_params=remote_params(1),
+        cost_estimate=pl.CostEstimate(
+            flops=6 * tree_rows * units * width, bytes_accessed=40 * 2**20, transcendentals=0
+        ),
+    )(own, gate_weight, up_weight, down_weight)
+
+
+def backward_kernel(
+    replicas,
+    own,
+    gate_hbm,
+    up_hbm,
+    down_hbm,
+    mix_hbm,
+    gelu_hbm,
+    tree_out,
+    gate_out,
+    up_out,
+    every_out,
+    total,
+    tree,
+    gate_w,
+    up_w,
+    down_w,
+    gate_back,
+    up_back,
+    mix,
+    gelu,
+    hidden_back,
+    send_sem,
+    recv_sem,
+    local_sem,
+    *scratch,
+):
+    plane = Plane()
+    rows = own.shape[0]
+    wires = Wires(send_sem, recv_sem)
+    chips = [plane.own_chip, plane.x_chip, plane.y_chip, plane.diag_chip]
+
+    def fetch(order):
+        there = block_at(chips[order] * 2 * rows, 2 * rows)
+        return [
+            load(mix_hbm.at[there], mix.at[order % 2], local_sem.at[3 + 2 * order]),
+            load(gelu_hbm.at[there], gelu.at[order % 2], local_sem.at[4 + 2 * order]),
+        ]
+
+    loads = [load(down_hbm, down_w, local_sem.at[2])]
+    fetched = [fetch(0), fetch(1)]
+    loads += [
+        load(gate_hbm, gate_w, local_sem.at[0]),
+        load(up_hbm, up_w, local_sem.at[1]),
+    ]
+    z, others = replica_peers(replicas)
+    greet(plane.near() + others)
+    tree[block_at(plane.me * rows, rows), :] = own[...]
+    stores = []
+
+    def use(chip):
+        order = len(stores) // 2
+        slot = order % 2
+        if order == 0:
+            loads[0].wait()
+        there = block_at(chip * 2 * rows, 2 * rows)
+        hidden_back[...] = dot_nt(tree[there, :], down_w[...])
+        for copy in fetched[order]:
+            copy.wait()
+
+        def step(at):
+            value = hidden_back[at, :].astype(jnp.bfloat16).astype(jnp.float32)
+            here = block_at(chip * 2 * rows + at.start, at.size)
+            gate_back[here, :] = (value * mix[slot, at, :].astype(jnp.float32)).astype(jnp.bfloat16)
+            up_back[here, :] = (value * gelu[slot, at, :].astype(jnp.float32)).astype(jnp.bfloat16)
+
+        by_rows(2 * rows, step, 16)
+        if order + 2 < 4:
+            fetched.append(fetch(order + 2))
+        base = 11 + 2 * order
+        stores.append(load(gate_back.at[there], gate_out.at[there], local_sem.at[base]))
+        stores.append(load(up_back.at[there], up_out.at[there], local_sem.at[base + 1]))
+
+    over = [wires.send(own, every_out.at[z], other) for other in others]
+    gather_tree(wires, plane, own, tree, rows, use)
+    tree_store = load(tree, tree_out, local_sem.at[19])
+    loads[1].wait()
+    loads[2].wait()
+
+    def product(chip, columns):
+        there = block_at(chip * 2 * rows, 2 * rows)
+        return dot_nn(gate_back[there, :], gate_w[:, columns]) + dot_nn(
+            up_back[there, :], up_w[:, columns]
+        )
+
+    gathered = list(wires.sent)
+    scatter_sum(wires, plane, scratch, product, total)
+    for copy in over:
+        copy.wait_recv()
+    for copy in gathered:
+        copy.wait_send()
+    for copy in stores + [tree_store]:
+        copy.wait()
+
+
+def feedforward_backward(own, gate_weight, up_weight, down_weight, mix, gelu):
+    rows, width = own.shape
+    units = gate_weight.shape[0]
+    replicas, count = lax.axis_size("replica"), lax.axis_size("shard")
+    tree_rows = count * rows
+    low, full = jnp.bfloat16, jnp.float32
+    copies = GATHER_COPIES + SCATTER_COPIES + replicas - 1
+    return pl.pallas_call(
+        functools.partial(backward_kernel, replicas),
+        out_shape=(
+            jax.ShapeDtypeStruct((tree_rows, width), low),
+            jax.ShapeDtypeStruct((tree_rows, units), low),
+            jax.ShapeDtypeStruct((tree_rows, units), low),
+            jax.ShapeDtypeStruct((replicas, rows, width), low),
+            jax.ShapeDtypeStruct((rows, width), full),
+        ),
+        in_specs=vmem_specs(1) + any_specs(5),
+        out_specs=tuple(any_specs(4) + vmem_specs(1)),
+        scratch_shapes=[
+            pltpu.VMEM((tree_rows, width), low),
+            pltpu.VMEM((units, width), low),
+            pltpu.VMEM((units, width), low),
+            pltpu.VMEM((units, width), low),
+            pltpu.VMEM((tree_rows, units), low),
+            pltpu.VMEM((tree_rows, units), low),
+            pltpu.VMEM((2, 2 * rows, units), low),
+            pltpu.VMEM((2, 2 * rows, units), low),
+            pltpu.VMEM((2 * rows, units), full),
+            pltpu.SemaphoreType.DMA((copies,)),
+            pltpu.SemaphoreType.DMA((copies,)),
+            pltpu.SemaphoreType.DMA((20,)),
+        ]
+        + scatter_scratch(rows, width),
+        compiler_params=remote_params(2),
+        cost_estimate=pl.CostEstimate(
+            flops=6 * tree_rows * units * width, bytes_accessed=40 * 2**20, transcendentals=0
+        ),
+    )(own, gate_weight, up_weight, down_weight, mix, gelu)
 
 
 def shards_heads(
@@ -422,12 +923,9 @@
     attention_branch = norm_rows(attention_pre, attention_post_gain)
     middle = stream + attention_branch
     normed_mid = norm_rows(middle, feedforward_gain).astype(low)
-    mid_tree = group_rows(normed_mid)
-    gate_lin = dot_nt(mid_tree, gate_weight)
-    up_lin = dot_nt(mid_tree, up_weight)
-    gelu_value, gelu_slope = gelu_parts(gate_lin)
-    hidden = (gelu_value * up_lin).astype(low)
-    feedforward_pre = sum_low(dot_nn(hidden, down_weight))
+    mid_tree, hidden, mix, gelu_value, mid_every, feedforward_pre = feedforward_forward(
+        normed_mid, gate_weight, up_weight, down_weight
+    )
     feedforward_branch = norm_rows(feedforward_pre, feedforward_post_gain)
     result = middle + feedforward_branch
     squares = jnp.stack(
@@ -440,9 +938,11 @@
     seed_grad = cotangent.astype(jnp.float32) * valid_rows[:, None]
     ffpre_back, grad_four = norm_back(feedforward_pre, feedforward_post_gain, seed_grad)
     ffpre_low = ffpre_back.astype(low)
-    ffpre_tree = group_rows(ffpre_low)
-    mid_every = lax.all_gather(normed_mid, ("replica", "shard"), axis=0, tiled=True)
-    ffpre_every = lax.all_gather(ffpre_low, ("replica", "shard"), axis=0, tiled=True)
+    ffpre_tree, gate_back, up_back, ffpre_every, mid_back = feedforward_backward(
+        ffpre_low, gate_weight, up_weight, down_weight, mix, gelu_value
+    )
+    mid_every = lax.all_gather(mid_every, "shard", axis=1, tiled=True)
+    ffpre_every = lax.all_gather(ffpre_every, "shard", axis=1, tiled=True)
 
     def hidden_grads(gate_lin, up_lin, gelu_value, gelu_slope, ffpre_rows):
         hidden_back = dot_nt(ffpre_rows, down_weight).astype(low).astype(jnp.float32)
@@ -450,8 +950,6 @@
         up_back = (hidden_back * gelu_value).astype(low)
         return gate_back, up_back
 
-    gate_back, up_back = hidden_grads(gate_lin, up_lin, gelu_value, gelu_slope, ffpre_tree)
-    mid_back = sum_low(dot_nn(gate_back, gate_weight) + dot_nn(up_back, up_weight))
     middle_part, grad_three = norm_back(middle, feedforward_gain, mid_back)
     middle_back = seed_grad + middle_part
     attention_pre_back, grad_two = norm_back(attention_pre, attention_post_gain, middle_back)
@@ -499,8 +997,8 @@
     down_sum = dot_tn(hidden, ffpre_tree)
     for step in range(1, tree_count):
         tree = lax.rem(lax.axis_index("replica") + step, tree_count)
-        mid_rows = lax.dynamic_slice_in_dim(mid_every, tree * tree_size, tree_size)
-        ffpre_rows = lax.dynamic_slice_in_dim(ffpre_every, tree * tree_size, tree_size)
+        mid_rows = lax.dynamic_index_in_dim(mid_every, tree, 0, False)
+        ffpre_rows = lax.dynamic_index_in_dim(ffpre_every, tree, 0, False)
         gate_lin = dot_nt(mid_rows, gate_weight)
         up_lin = dot_nt(mid_rows, up_weight)
         gelu_value, gelu_slope = gelu_parts(gate_lin)

time: 1370 us -> 1250 us (0.912)
  waiting for transfers between devices: 680 us -> 492 us
  Pallas kernels: 0 us -> 171 us
  matrix products: 537 us -> 435 us
    pallas_call x0 -> x2, Pallas kernels: none -> 171 us  [the longest x1 86.4 us: feedforward_forward(): pl.pallas_call(functools.partial(forward_kernel, replicas), out_shape=(ja...]
    reduce_scatter x4 -> x2, waiting for transfers between devices: 256 us -> 125 us  [sum_low(): lax.psum_scatter(values.astype(jnp.bfloat16), 'shard', scatter_dimension=...]
    all_gather x4 -> x2, waiting for transfers between devices: 192 us -> 94.1 us  [group_rows(): return lax.all_gather(values, 'shard', axis=0, tiled=True)]
    dot_general x9 -> x6, matrix products: 82.4 us -> 34.5 us  [dot_nn(): lax.dot_general(left, right, (((1,), (0,)), ((), ())), preferred_element_...]
    dot_general x18 -> x15, matrix products: 205 us -> 158 us  [dot_nt(): lax.dot_general(left, right, (((1,), (1,)), ((), ())), preferred_element_...]
    all_gather x2, waiting for transfers between devices: 180 us -> 204 us  [the longest x1 110 us: shards_heads(): ffpre_every = lax.all_gather(ffpre_every, 'shard', axis=1, tiled=True)]
    psum x1, waiting for transfers between devices: 49.8 us -> 67.2 us  [shards_heads(): attention_grads = lax.psum(attention_grads, 'replica').astype(jnp.float32)]
  transfers between devices with their start and end apart: 15 -> 11, of which waited for: 11 -> 7; matrix products, arithmetic and copies ran while one was open for 18% -> 13% of each run, Pallas kernels for 0% -> 0%
where the time goes in v2:
time: 1250 us; the launch traced here: 1240 us
  waiting for transfers between devices  492 us (39%)
  matrix products  435 us (35%)
  Pallas kernels  171 us (14%)
  other arithmetic  68.4 us (5%)
  blocking collectives  41.3 us (3%)
  between operations  16.1 us (1%)
    dot_general x18, matrix products, dot_tn(): lax.dot_general(left, right, (((0,), (0,)), ((), ())), preferred_element_...  242 us
    dot_general x15, matrix products, dot_nt(): lax.dot_general(left, right, (((1,), (1,)), ((), ())), preferred_element_...  158 us
    reduce_scatter x2, waiting for transfers between devices, sum_low(): lax.psum_scatter(values.astype(jnp.bfloat16), 'shard', scatter_dimension=...  125 us
    all_gather x1, waiting for transfers between devices, shards_heads(): ffpre_every = lax.all_gather(ffpre_every, 'shard', axis=1, tiled=True)  110 us
    all_gather x1, waiting for transfers between devices, shards_heads(): mid_every = lax.all_gather(mid_every, 'shard', axis=1, tiled=True)  94.2 us
    all_gather x2, waiting for transfers between devices, group_rows(): return lax.all_gather(values, 'shard', axis=0, tiled=True)  94.1 us
    pallas_call x1, Pallas kernels, feedforward_forward(): pl.pallas_call(functools.partial(forward_kernel, replicas), out_shape=(ja...  86.4 us
    pallas_call x1, Pallas kernels, feedforward_backward(): pl.pallas_call(functools.partial(backward_kernel, replicas), out_shape=(j...  84.2 us
  transfers between devices with their start and end apart: 11, of which 7 were waited for; matrix products, arithmetic and copies ran while one was open for 13% of the time, Pallas kernels for 0%

profile of v2, /device:TPU:0, one launch (start us, length us, event | category | flops | bytes accessed | tf_op | source)
XLA Modules:
  0.0 1236.8 jit_solution(13357429226524485236)
XLA Ops:
  8.0 1.4 fusion.99
  10.6 2.3 fusion.101
  18.6 46.0 %all-gather.5.cloned.1.call-done = bf16[1536,2304]{1,0:T(8,128)(2,1)} async-done(((bf16[192,2304]{1,0:T(8,128)(2,1)}), bf16[1536,2304]{1,0:T(8,128)(2,1)}) %all-gather.5.cloned.1.call-update) | async-done | bytes 7077904 | tf_op jit(solution)/shard_map/all_gather | solution.py:100
  64.7 5.8 fusion.127
  70.6 2.0 fusion.213
  72.7 6.1 fusion.121
  78.9 9.7 fusion.208
  88.7 4.2 convolution_convert_fusion.9
  93.8 1.5 convolution_convert_fusion.10
  96.2 5.0 convolution_convert_fusion
  103.0 63.9 %reduce-scatter.3.cloned.1.call-done = bf16[192,2304]{1,0:T(8,128)(2,1)} async-done(((bf16[1536,2304]{1,0:T(8,128)(2,1)}), bf16[192,2304]{1,0:T(8,128)(2,1)}) %reduce-scatter.3.cloned.1.call-update) | async-done | bytes 884752 | tf_op jit(solution)/shard_map/reduce_scatter | solution.py:352
  168.9 1.7 multiply_reduce_fusion.6
  170.6 2.6 multiply_convert_fusion.10.own
  173.2 86.4 %shard_map.263 = (bf16[1536,2304]{1,0:T(8,128)(2,1)}, bf16[1536,1152]{1,0:T(8,128)(2,1)}, bf16[1536,1152]{1,0:T(8,128)(2,1)}, bf16[1536,1152]{1,0:T(8,128)(2,1)}...) custom-call(bf16[192,2304]{1,0:T(8,128)(2,1)} %multiply_convert_fusion.10.own, bf16[1152,2304]{1,0:T(8,128)(2,1)} %gate_hbm.3, ...), custom_call_target="tpu_custom_call" | custom-call | flops 24461180928 | bytes 41943040 | tf_op jit(solution)/shard_map/pallas_call | solution.py:697
  259.7 1.8 multiply_reduce_fusion.5
  261.5 5.7 multiply_reduce_fusion.1
  268.6 84.2 %shard_map.264 = (bf16[1536,2304]{1,0:T(8,128)(2,1)}, bf16[1536,1152]{1,0:T(8,128)(2,1)}, bf16[1536,1152]{1,0:T(8,128)(2,1)}, bf16[4,192,2304]{2,1,0:T(8,128)(2,1)}, f32[192,2304]{1,0:T(8,128)}) custom-call(bf16[192,2304]{1,0:T(8,128)(2,1)} %subtract_convert_fusion.own, bf16[1152,2304]{1,0:T(8,128)(2,1)} %gate_hbm.3, bf16[1152,2304]{1,0:T(8,128)(2,1)} %up_hbm.3, ...), custom_call_target="tpu_custom_call" | custom-call | flops 24461180928 | bytes 41943040 | tf_op jit(solution)/shard_map/pallas_call | solution.py:833
  352.9 3.5 multiply_reduce_fusion.2
  356.4 3.5 fusion.98
  362.5 48.0 %all-gather.7.cloned.1.call-done = bf16[1536,2304]{1,0:T(8,128)(2,1)} async-done(((bf16[192,2304]{1,0:T(8,128)(2,1)}), bf16[1536,2304]{1,0:T(8,128)(2,1)}) %all-gather.7.cloned.1.call-update) | async-done | bytes 7077904 | tf_op jit(solution)/shard_map/all_gather | solution.py:100
  410.6 5.2 convolution_convert_fusion.8
  415.8 5.2 multiply_reduce_fusion
  421.1 6.8 multiply_convert_fusion
  429.6 1.5 fusion.86
  431.4 2.1 convolution_convert_fusion.4
  433.5 5.2 fusion.113
  438.9 7.2 fusion.125
  446.3 5.4 fusion.123
  454.2 2.0 convolution_convert_fusion.5
  456.2 1.9 pad_maximum_fusion
  458.3 8.8 fusion.214
  467.1 7.1 convolution_add_fusion.1
  474.2 4.9 fusion
  481.2 2.5 pad_maximum_fusion.2
  483.7 15.5 %fusion.216 = f32[1152,2304]{1,0:T(8,128)} fusion(bf16[1536,1152]{1,0:T(8,128)(2,1)} %get-tuple-element.29, bf16[1536,2304]{1,0:T(8,128)(2,1)} %get-tuple-element.30), kind=kOutput, calls=%fused_computation.322 | convolution fusion | flops 8153726976 | bytes 21233664 | tf_op jit(solution)/shard_map/dot_general | solution.py:346
  499.2 14.3 %fusion.217 = f32[1152,2304]{1,0:T(8,128)} fusion(bf16[1536,1152]{1,0:T(8,128)(2,1)S(1)} %copy-done.45, bf16[1536,2304]{1,0:T(8,128)(2,1)} %get-tuple-element.30), kind=kOutput, calls=%fused_computation.323 | convolution fusion | flops 8153726976 | bytes 21233664 | tf_op jit(solution)/shard_map/dot_general | solution.py:346
  513.5 11.4 fusion.218
  525.0 67.2 %all-reduce.3.cloned.1.call-done = bf16[768,2304]{1,0:T(8,128)(2,1)} async-done(((bf16[768,2304]{1,0:T(8,128)(2,1)}), bf16[768,2304]{1,0:T(8,128)(2,1)}) %all-reduce.3.cloned.1.call-update) | async-done | bytes 3538960 | tf_op jit(solution)/shard_map/psum | solution.py:990
  592.2 2.8 fusion.210
  595.0 4.1 fusion.209
  599.1 61.4 %reduce-scatter.5.cloned.1.call-done = bf16[192,2304]{1,0:T(8,128)(2,1)} async-done(((bf16[1536,2304]{1,0:T(8,128)(2,1)}), bf16[192,2304]{1,0:T(8,128)(2,1)}) %reduce-scatter.5.cloned.1.call-update) | async-done | bytes 884752 | tf_op jit(solution)/shard_map/reduce_scatter | solution.py:352
  660.5 1.7 fusion.104
  662.2 41.3 %all-reduce = (f32[2304]{0:T(1024)}, f32[2304]{0:T(1024)}, f32[2304]{0:T(1024)}, f32[2304]{0:T(1024)}, f32[4]{0:T(128)S(1)}, /*index=5*/f32[]{:T(128)}) all-reduce(f32[2304]{0:T(1024)S(1)} %get-tuple-element.44, f32[2304]{0:T(1024)S(1)} %get-tuple-element.40, ...), channel_id=1, replica_groups=mesh['replica'=4,'shard'=8] {'replica','shard'}, use_global_device_ids=true, to_apply=%region_22.23 | all-reduce | flops 9221 | bytes 73768 | tf_op jit(solution)/shard_map/psum | solution.py:1010
  704.7 2.8 fusion.88
  707.5 94.2 %all-gather.11.cloned.1.call-done = bf16[4,1536,2304]{2,1,0:T(8,128)(2,1)} async-done(((bf16[4,192,2304]{2,1,0:T(8,128)(2,1)}), bf16[4,1536,2304]{2,1,0:T(8,128)(2,1)}) %all-gather.11.cloned.1.call-update) | async-done | bytes 28311568 | tf_op jit(solution)/shard_map/all_gather | solution.py:944
  801.7 15.0 %fusion.33 = f32[1536,1152]{1,0:T(8,128)} fusion(bf16[1152,2304]{1,0:T(8,128)(2,1)} %up_hbm.3, bf16[4,1536,2304]{2,1,0:T(8,128)(2,1)} %all-gather.11.cloned.1.call-done, s32[]{:T(128)S(6)} %select_n.63), kind=kOutput, calls=%fused_computation.61 | convolution fusion | flops 8153726976 | bytes 19464196 | tf_op jit(solution)/shard_map/dot_general | solution.py:334
  816.7 15.5 %fusion.31 = f32[1536,1152]{1,0:T(8,128)} fusion(bf16[1152,2304]{1,0:T(8,128)(2,1)} %gate_hbm.3, bf16[4,1536,2304]{2,1,0:T(8,128)(2,1)} %all-gather.11.cloned.1.call-done, s32[]{:T(128)S(6)} %select_n.63), kind=kOutput, calls=%fused_computation.59 | convolution fusion | flops 8153726976 | bytes 19464196 | tf_op jit(solution)/shard_map/dot_general | solution.py:334
  832.2 110.1 %all-gather.9.cloned.1.call-done = bf16[4,1536,2304]{2,1,0:T(8,128)(2,1)} async-done(((bf16[4,192,2304]{2,1,0:T(8,128)(2,1)}), bf16[4,1536,2304]{2,1,0:T(8,128)(2,1)}) %all-gather.9.cloned.1.call-update) | async-done | bytes 28311568 | tf_op jit(solution)/shard_map/all_gather | solution.py:945
  942.3 15.1 %convolution_convert_fusion.3 = bf16[1536,1152]{1,0:T(8,128)(2,1)} fusion(bf16[1152,2304]{1,0:T(8,128)(2,1)} %down_hbm.3, bf16[4,1536,2304]{2,1,0:T(8,128)(2,1)} %all-gather.9.cloned.1.call-done, s32[]{:T(128)S(6)} %select_n.63), kind=kOutput, calls=%fused_computation.31 | convolution fusion | flops 8155496448 | bytes 15925252 | tf_op jit(solution)/shard_map/dot_general | solution.py:334
  957.4 15.2 %fusion.25 = f32[1536,1152]{1,0:T(8,128)} fusion(bf16[1152,2304]{1,0:T(8,128)(2,1)} %up_hbm.3, bf16[4,1536,2304]{2,1,0:T(8,128)(2,1)} %all-gather.11.cloned.1.call-done, s32[]{:T(128)S(6)} %select_n.64), kind=kOutput, calls=%fused_computation.53 | convolution fusion | flops 8153726976 | bytes 19464196 | tf_op jit(solution)/shard_map/dot_general | solution.py:334
  972.6 12.9 %convolution_convert_fusion.2 = bf16[1536,1152]{1,0:T(8,128)(2,1)} fusion(bf16[1152,2304]{1,0:T(8,128)(2,1)S(1)} %bitcast.120, bf16[4,1536,2304]{2,1,0:T(8,128)(2,1)} %all-gather.9.cloned.1.call-done, s32[]{:T(128)S(6)} %select_n.64), kind=kOutput, calls=%fused_computation.30 | convolution fusion | flops 8155496448 | bytes 15925252 | tf_op jit(solution)/shard_map/dot_general | solution.py:334
  985.5 13.4 %fusion.23 = f32[1536,1152]{1,0:T(8,128)} fusion(bf16[1152,2304]{1,0:T(8,128)(2,1)S(1)} %bitcast.122, bf16[4,1536,2304]{2,1,0:T(8,128)(2,1)} %all-gather.11.cloned.1.call-done, s32[]{:T(128)S(6)} %select_n.64), kind=kOutput, calls=%fused_computation.51 | convolution fusion | flops 8153726976 | bytes 19464196 | tf_op jit(solution)/shard_map/dot_general | solution.py:334
  999.0 13.3 %fusion.17 = f32[1536,1152]{1,0:T(8,128)} fusion(bf16[1152,2304]{1,0:T(8,128)(2,1)S(1)} %bitcast.118, bf16[4,1536,2304]{2,1,0:T(8,128)(2,1)} %all-gather.11.cloned.1.call-done, s32[]{:T(128)S(6)} %select_n.65), kind=kOutput, calls=%fused_computation.45 | convolution fusion | flops 8153726976 | bytes 19464196 | tf_op jit(solution)/shard_map/dot_general | solution.py:334
  1012.3 11.7 convolution_convert_fusion.1
  1024.0 13.5 %fusion.15 = f32[1536,1152]{1,0:T(8,128)} fusion(bf16[1152,2304]{1,0:T(8,128)(2,1)S(1)} %bitcast.122, bf16[4,1536,2304]{2,1,0:T(8,128)(2,1)} %all-gather.11.cloned.1.call-done, s32[]{:T(128)S(6)} %select_n.65), kind=kOutput, calls=%fused_computation.43 | convolution fusion | flops 8153726976 | bytes 19464196 | tf_op jit(solution)/shard_map/dot_general | solution.py:334
  1037.5 21.6 %convolution_add_fusion.7 = f32[1152,2304]{1,0:T(8,128)} fusion(f32[1152,2304]{1,0:T(8,128)} %fusion.217, bf16[4,1536,2304]{2,1,0:T(8,128)(2,1)} %all-gather.11.cloned.1.call-done, s32[]{:T(128)S(6)} %select_n.63, bf16[1536,1152]{1,0:T(8,128)(2,1)} %convolution_convert_fusion.3, f32[1536,1152]{1,0:T(8,128)} %fusion.31), kind=kOutput, calls=%fused_computation.7 | convolution fusion | flops 8175845376 | bytes 38928388 | tf_op jit(solution)/shard_map/dot_general | solution.py:346
  1059.1 20.8 %convolution_add_fusion.10 = f32[1152,2304]{1,0:T(8,128)} fusion(f32[1152,2304]{1,0:T(8,128)} %fusion.216, bf16[4,1536,2304]{2,1,0:T(8,128)(2,1)} %all-gather.11.cloned.1.call-done, s32[]{:T(128)S(6)} %select_n.63, f32[1536,1152]{1,0:T(8,128)} %fusion.33, bf16[1536,1152]{1,0:T(8,128)(2,1)S(1)} %copy-done.43, f32[1536,1152]{1,0:T(8,128)} %fusion.31), kind=kOutput, calls=%fused_computation.10 | convolution fusion | flops 8191770624 | bytes 46006276 | tf_op jit(solution)/shard_map/dot_general | solution.py:346
  1079.9 21.6 %convolution_add_fusion.4 = f32[1152,2304]{1,0:T(8,128)} fusion(f32[1152,2304]{1,0:T(8,128)} %fusion.218, bf16[4,1536,2304]{2,1,0:T(8,128)(2,1)} %all-gather.9.cloned.1.call-done, s32[]{:T(128)S(6)} %select_n.63, f32[1536,1152]{1,0:T(8,128)} %fusion.33, f32[1536,1152]{1,0:T(8,128)} %fusion.31), kind=kOutput, calls=%fused_computation.4 | convolution fusion | flops 8174075904 | bytes 42467332 | tf_op jit(solution)/shard_map/dot_general | solution.py:346
  1101.5 22.9 %convolution_add_fusion.6 = f32[1152,2304]{1,0:T(8,128)} fusion(f32[1152,2304]{1,0:T(8,128)} %convolution_add_fusion.7, bf16[4,1536,2304]{2,1,0:T(8,128)(2,1)} %all-gather.11.cloned.1.call-done, s32[]{:T(128)S(6)} %select_n.64, bf16[1536,1152]{1,0:T(8,128)(2,1)} %convolution_convert_fusion.2, f32[1536,1152]{1,0:T(8,128)} %fusion.23), kind=kOutput, calls=%fused_computation.6 | convolution fusion | flops 8175845376 | bytes 38928388 | tf_op jit(solution)/shard_map/dot_general | solution.py:346
  1124.4 20.4 %convolution_add_fusion.9 = f32[1152,2304]{1,0:T(8,128)} fusion(f32[1152,2304]{1,0:T(8,128)} %convolution_add_fusion.10, bf16[4,1536,2304]{2,1,0:T(8,128)(2,1)} %all-gather.11.cloned.1.call-done, s32[]{:T(128)S(6)} %select_n.64, f32[1536,1152]{1,0:T(8,128)} %fusion.25, bf16[1536,1152]{1,0:T(8,128)(2,1)S(1)} %copy-done.42, f32[1536,1152]{1,0:T(8,128)} %fusion.23), kind=kOutput, calls=%fused_computation.9 | convolution fusion | flops 8191770624 | bytes 46006276 | tf_op jit(solution)/shard_map/dot_general | solution.py:346
  1144.8 21.8 %convolution_add_fusion.3 = f32[1152,2304]{1,0:T(8,128)} fusion(f32[1152,2304]{1,0:T(8,128)} %convolution_add_fusion.4, bf16[4,1536,2304]{2,1,0:T(8,128)(2,1)} %all-gather.9.cloned.1.call-done, s32[]{:T(128)S(6)} %select_n.64, f32[1536,1152]{1,0:T(8,128)} %fusion.25, f32[1536,1152]{1,0:T(8,128)} %fusion.23), kind=kOutput, calls=%fused_computation.3 | convolution fusion | flops 8174075904 | bytes 42467332 | tf_op jit(solution)/shard_map/dot_general | solution.py:346
  1166.6 20.5 %convolution_add_fusion.5 = f32[1152,2304]{1,0:T(8,128)} fusion(f32[1152,2304]{1,0:T(8,128)} %convolution_add_fusion.6, bf16[4,1536,2304]{2,1,0:T(8,128)(2,1)} %all-gather.11.cloned.1.call-done, s32[]{:T(128)S(6)} %select_n.65, bf16[1536,1152]{1,0:T(8,128)(2,1)S(1)} %convolution_convert_fusion.1, f32[1536,1152]{1,0:T(8,128)} %fusion.15), kind=kOutput, calls=%fused_computation.5 | convolution fusion | flops 8175845376 | bytes 38928388 | tf_op jit(solution)/shard_map/dot_general | solution.py:346
  1187.1 20.7 %convolution_add_fusion.8 = f32[1152,2304]{1,0:T(8,128)} fusion(f32[1152,2304]{1,0:T(8,128)} %convolution_add_fusion.9, bf16[4,1536,2304]{2,1,0:T(8,128)(2,1)} %all-gather.11.cloned.1.call-done, s32[]{:T(128)S(6)} %select_n.65, f32[1536,1152]{1,0:T(8,128)} %fusion.17, bf16[1536,1152]{1,0:T(8,128)(2,1)S(1)} %convolution_convert_fusion.1, f32[1536,1152]{1,0:T(8,128)} %fusion.15), kind=kOutput, calls=%fused_computation.8 | convolution fusion | flops 8191770624 | bytes 46006276 | tf_op jit(solution)/shard_map/dot_general | solution.py:346
  1207.8 21.7 %convolution_add_fusion.2 = f32[1152,2304]{1,0:T(8,128)} fusion(f32[1152,2304]{1,0:T(8,128)} %convolution_add_fusion.3, bf16[4,1536,2304]{2,1,0:T(8,128)(2,1)} %all-gather.9.cloned.1.call-done, s32[]{:T(128)S(6)} %select_n.65, f32[1536,1152]{1,0:T(8,128)} %fusion.17, f32[1536,1152]{1,0:T(8,128)} %fusion.15), kind=kOutput, calls=%fused_computation.2 | convolution fusion | flops 8174075904 | bytes 42467332 | tf_op jit(solution)/shard_map/dot_general | solution.py:346
  (185 shorter events, 24.9 us)
Async XLA Ops:
  7.2 89.0 %copy-start = (bf16[256,2304]{1,0:T(8,128)(2,1)S(1)}, bf16[256,2304]{1,0:T(8,128)(2,1)}, u32[]{:S(2)}) copy-start(bf16[256,2304]{1,0:T(8,128)(2,1)} %param.24) | copy-start | bytes 3538948
  7.2 57.5 %all-gather.5.cloned.1.call-start = ((), (), s32[]{:S(2)}) async-start(), calls=%async_computation.2 | async-start | bytes 7962624 | tf_op jit(solution)/shard_map/all_gather | solution.py:100
  13.0 153.9 %reduce-scatter.3.cloned.1.call-start = ((), (), s32[]{:S(2)}) async-start(), calls=%async_computation.3 | async-start | bytes 7962624 | tf_op jit(solution)/shard_map/reduce_scatter | solution.py:352
  13.0 75.7 %collective-permute-start.1 = (bf16[128,2304]{1,0:T(8,128)(2,1)}, bf16[128,2304]{1,0:T(8,128)(2,1)}, u32[]{:S(2)}, u32[]{:S(2)}) collective-permute-start(bf16[128,2304]{1,0:T(8,128)(2,1)} %param.23), channel_id=1, source_target_pairs={{0,1},{1,0},{2,3},{3,2},{4,5},{5,4},{6,7},{7,6},{8,9},{9,8},{10,11... | collective-permute-start | bytes 1769480 | tf_op jit(solution)/shard_map/ppermute | solution.py:905
  13.5 5.1 collective-permute-start
  18.6 51.9 %copy-start.18 = (bf16[256,2304]{1,0:T(8,128)(2,1)S(1)}, bf16[256,2304]{1,0:T(8,128)(2,1)}, u32[]{:S(2)}) copy-start(bf16[256,2304]{1,0:T(8,128)(2,1)} %param.21) | copy-start | bytes 3538948
  64.7 5.9 copy-start.41
  72.6 6.3 copy-start.27
  78.9 9.8 copy-start.12
  78.9 9.8 copy-start.19
  78.9 9.8 copy-start.21
  88.7 4.3 copy-start.2
  96.2 6.8 copy-start.32
  96.2 6.8 copy-start.33
  96.2 6.8 copy-start.34
  96.2 72.7 %copy-start.3 = (bf16[192,2304]{1,0:T(8,128)(2,1)S(1)}, bf16[192,2304]{1,0:T(8,128)(2,1)}, u32[]{:S(2)}) copy-start(bf16[192,2304]{1,0:T(8,128)(2,1)} %param.16) | copy-start | bytes 2654212
  101.2 309.4 %all-gather.7.cloned.1.call-start = ((), (), s32[]{:S(2)}) async-start(), calls=%async_computation.4 | async-start | bytes 7962624 | tf_op jit(solution)/shard_map/all_gather | solution.py:100
  170.6 89.0 %copy-start.35 = (f32[192]{0:T(256)}, f32[192]{0:T(256)S(1)}, u32[]{:S(2)}) copy-start(f32[192]{0:T(256)S(1)} %multiply_reduce_fusion.6) | copy-start | bytes 2308
  170.6 89.0 %copy-start.28 = (f32[192]{0:T(256)}, f32[192]{0:T(256)S(1)}, u32[]{:S(2)}) copy-start(f32[192]{0:T(256)S(1)} %add_rsqrt_fusion.1) | copy-start | bytes 2308
  259.6 7.6 copy-start.10
  259.6 7.6 copy-start.11
  268.6 84.3 %copy-start.29 = (f32[192]{0:T(256)S(1)}, f32[192]{0:T(256)}, u32[]{:S(2)}) copy-start(f32[192]{0:T(256)} %copy-done.28) | copy-start | bytes 2308
  268.6 87.7 %copy-start.36 = (f32[192]{0:T(256)S(1)}, f32[192]{0:T(256)}, u32[]{:S(2)}) copy-start(f32[192]{0:T(256)} %copy-done.35) | copy-start | bytes 2308
  352.9 7.0 copy-start.40
  352.9 8.2 copy-start.5
  362.5 53.3 %copy-start.15 = (bf16[1536,256]{1,0:T(8,128)(2,1)S(1)}, bf16[1536,256]{1,0:T(8,128)(2,1)}, u32[]{:S(2)}) copy-start(bf16[1536,256]{1,0:T(8,128)(2,1)} %copy-done.14) | copy-start | bytes 2359300
  362.5 229.7 %all-reduce.3.cloned.1.call-start = ((), (), s32[]{:S(2)}) async-start(), calls=%async_computation.6 | async-start | bytes 7077888 | tf_op jit(solution)/shard_map/psum | solution.py:990
  410.6 10.5 slice-start
  410.6 10.5 slice-start.1
  415.8 5.3 slice-start.2
  421.1 6.8 copy-start.20
  427.9 3.5 slice-start.3
  429.3 2.1 copy-start.7
  429.3 4.2 collective-permute-start.2
  431.1 20.6 %collective-permute-start.3 = (f32[1536,256]{0,1:T(8,128)S(1)}, f32[1536,256]{0,1:T(8,128)S(1)}, u32[]{:S(2)}, u32[]{:S(2)}) collective-permute-start(f32[1536,256]{0,1:T(8,128)S(1)} %fusion.86), channel_id=1, source_target_pairs={{0,1},{1,0},{2,3},{3,2},{4,5},{5,4},{6,7},{7,6},{8,9},{9,8},{10,11... | collective-permute-start | bytes 4718600 | tf_op jit(solution)/shard_map/ppermute | solution.py:969
  433.5 5.4 copy-start.13
  438.9 13.0 %slice-start.5 = ((s8[7077888]{0:T(1024)(128)(4,1)}), s8[4194304]{0:T(1024)(128)(4,1)S(1)}, s32[]{:S(2)}) async-start(s8[7077888]{0:T(1024)(128)(4,1)} %bitcast.115), calls=%async_computation.14 | async-start | bytes 8388608
  438.9 13.0 %slice-start.6 = ((s8[7077888]{0:T(1024)(128)(4,1)}), s8[2883584]{0:T(1024)(128)(4,1)S(1)}, s32[]{:S(2)}) async-start(s8[7077888]{0:T(1024)(128)(4,1)} %bitcast.115), calls=%async_computation.15 | async-start | bytes 5767168
  446.1 7.0 copy-start.16
  458.2 8.9 copy-start.17
  458.2 8.8 copy-start.23
  458.2 202.2 %reduce-scatter.5.cloned.1.call-start = ((), (), s32[]{:S(2)}) async-start(), calls=%async_computation.5 | async-start | bytes 7962624 | tf_op jit(solution)/shard_map/reduce_scatter | solution.py:352
  467.1 7.1 copy-start.22
  479.2 322.6 %all-gather.11.cloned.1.call-start = ((), (), s32[]{:S(2)}) async-start(), calls=%async_computation.8 | async-start | bytes 31850496 | tf_op jit(solution)/shard_map/all_gather | solution.py:944
  479.7 462.5 %all-gather.9.cloned.1.call-start = ((), (), s32[]{:S(2)}) async-start(), calls=%async_computation.7 | async-start | bytes 31850496 | tf_op jit(solution)/shard_map/all_gather | solution.py:945
  483.7 15.5 %copy-start.45 = (bf16[1536,1152]{1,0:T(8,128)(2,1)S(1)}, bf16[1536,1152]{1,0:T(8,128)(2,1)}, u32[]{:S(2)}) copy-start(bf16[1536,1152]{1,0:T(8,128)(2,1)} %get-tuple-element.33) | copy-start | bytes 10616836
  483.7 29.8 %slice-start.13 = ((s8[7077888]{0:T(1024)(128)(4,1)}), s8[4194304]{0:T(1024)(128)(4,1)S(1)}, s32[]{:S(2)}) async-start(s8[7077888]{0:T(1024)(128)(4,1)} %bitcast.123), calls=%async_computation.22 | async-start | bytes 8388608
  499.2 14.4 %slice-start.14 = ((s8[7077888]{0:T(1024)(128)(4,1)}), s8[2883584]{0:T(1024)(128)(4,1)S(1)}, s32[]{:S(2)}) async-start(s8[7077888]{0:T(1024)(128)(4,1)} %bitcast.123), calls=%async_computation.23 | async-start | bytes 5767168
  499.2 14.4 %copy-start.44 = (bf16[1536,1152]{1,0:T(8,128)(2,1)S(1)}, bf16[1536,1152]{1,0:T(8,128)(2,1)}, u32[]{:S(2)}) copy-start(bf16[1536,1152]{1,0:T(8,128)(2,1)} %get-tuple-element.34) | copy-start | bytes 10616836
  524.9 135.6 %copy-start.4 = (bf16[192,2304]{1,0:T(8,128)(2,1)S(1)}, bf16[192,2304]{1,0:T(8,128)(2,1)}, u32[]{:S(2)}) copy-start(bf16[192,2304]{1,0:T(8,128)(2,1)} %param.16) | copy-start | bytes 2654212
  524.9 135.6 %copy-start.25 = (f32[2304]{0:T(1024)S(1)}, f32[2304]{0:T(1024)}, u32[]{:S(2)}) copy-start(f32[2304]{0:T(1024)} %copy-done.24) | copy-start | bytes 27652
  524.9 135.6 %copy-start.31 = (f32[192]{0:T(256)S(1)}, f32[192]{0:T(256)}, u32[]{:S(2)}) copy-start(f32[192]{0:T(256)} %copy-done.30) | copy-start | bytes 2308
  524.9 137.3 %copy-start.26 = (f32[2304]{0:T(1024)S(1)}, f32[2304]{0:T(1024)}, u32[]{:S(2)}) copy-start(f32[2304]{0:T(1024)} %get-tuple-element.36) | copy-start | bytes 27652
  524.9 179.7 %copy-start.38 = (f32[192]{0:T(256)S(1)}, f32[192]{0:T(256)}, u32[]{:S(2)}) copy-start(f32[192]{0:T(256)} %copy-done.37) | copy-start | bytes 2308
  525.0 179.7 %copy-start.9 = (f32[192,2304]{1,0:T(8,128)S(1)}, f32[192,2304]{1,0:T(8,128)}, u32[]{:S(2)}) copy-start(f32[192,2304]{1,0:T(8,128)} %copy-done.8) | copy-start | bytes 5308420
  942.3 30.3 %slice-start.9 = ((s8[5308416]{0:T(1024)(128)(4,1)}), s8[4194304]{0:T(1024)(128)(4,1)S(1)}, s32[]{:S(2)}) async-start(s8[5308416]{0:T(1024)(128)(4,1)} %bitcast.119), calls=%async_computation.18 | async-start | bytes 8388608
  957.4 15.2 %slice-start.10 = ((s8[5308416]{0:T(1024)(128)(4,1)}), s8[1114112]{0:T(1024)(128)(4,1)S(1)}, s32[]{:S(2)}) async-start(s8[5308416]{0:T(1024)(128)(4,1)} %bitcast.119), calls=%async_computation.19 | async-start | bytes 2228224
  957.4 28.1 %slice-start.11 = ((s8[5308416]{0:T(1024)(128)(4,1)}), s8[4194304]{0:T(1024)(128)(4,1)S(1)}, s32[]{:S(2)}) async-start(s8[5308416]{0:T(1024)(128)(4,1)} %bitcast.121), calls=%async_computation.20 | async-start | bytes 8388608
  972.6 13.0 %slice-start.12 = ((s8[5308416]{0:T(1024)(128)(4,1)}), s8[1114112]{0:T(1024)(128)(4,1)S(1)}, s32[]{:S(2)}) async-start(s8[5308416]{0:T(1024)(128)(4,1)} %bitcast.121), calls=%async_computation.21 | async-start | bytes 2228224
  972.6 26.4 %slice-start.7 = ((s8[5308416]{0:T(1024)(128)(4,1)}), s8[4194304]{0:T(1024)(128)(4,1)S(1)}, s32[]{:S(2)}) async-start(s8[5308416]{0:T(1024)(128)(4,1)} %bitcast.117), calls=%async_computation.16 | async-start | bytes 8388608
  985.5 13.4 %slice-start.8 = ((s8[5308416]{0:T(1024)(128)(4,1)}), s8[1114112]{0:T(1024)(128)(4,1)S(1)}, s32[]{:S(2)}) async-start(s8[5308416]{0:T(1024)(128)(4,1)} %bitcast.117), calls=%async_computation.17 | async-start | bytes 2228224
  1037.5 21.6 %copy-start.43 = (bf16[1536,1152]{1,0:T(8,128)(2,1)S(1)}, bf16[1536,1152]{1,0:T(8,128)(2,1)}, u32[]{:S(2)}) copy-start(bf16[1536,1152]{1,0:T(8,128)(2,1)} %convolution_convert_fusion.3) | copy-start | bytes 10616836
  1101.5 22.9 %copy-start.42 = (bf16[1536,1152]{1,0:T(8,128)(2,1)S(1)}, bf16[1536,1152]{1,0:T(8,128)(2,1)}, u32[]{:S(2)}) copy-start(bf16[1536,1152]{1,0:T(8,128)(2,1)} %convolution_convert_fusion.2) | copy-start | bytes 10616836
  1207.8 21.7 %copy-start.1 = (bf16[256,2304]{1,0:T(8,128)(2,1)S(1)}, bf16[256,2304]{1,0:T(8,128)(2,1)}, u32[]{:S(2)}) copy-start(bf16[256,2304]{1,0:T(8,128)(2,1)} %param.24) | copy-start | bytes 3538948
  (8 other events, 8.7 us)
Sparse Core Ops, SparseCore 0:
  13.1 51.5 all-gather.4
  101.3 65.5 reduce-scatter.2
  362.6 47.9 all-gather.6
  458.3 133.8 all-reduce.2
  596.0 64.4 reduce-scatter.4
  662.2 139.4 all-gather.10
  803.6 138.6 all-gather.8

commit v3 on v2

--- a/solution.py
+++ b/solution.py
@@ -501,13 +501,16 @@
     ]
 
 
-def scatter_sum(wires, plane, scratch, product, total):
+def scatter_sum(wires, plane, scratch, product, total, before=None):
     sums, piece, mate_out, mate_in, x_out, x_in, y_out, y_in = scratch
     rows, width = total.shape
     half = rows // 2
     low, full = jnp.bfloat16, jnp.float32
 
     def produce(slot, out_slot, in_slot, chip):
+        if before is not None:
+            before(chip)
+
         def tile(columns):
             piece[...] = product(chip, columns)
             sums[slot, :, columns] = piece[block_at(plane.core * rows, rows), :]
@@ -863,6 +866,662 @@
     )(own, gate_weight, up_weight, down_weight, mix, gelu)
 
 
+class Copy:
+    def __init__(self, build):
+        self.build = build
+
+    def start(self):
+        self.build().start()
+
+    def wait_recv(self):
+        self.build().wait_recv()
+
+    def wait_send(self):
+        self.build().wait_send()
+
+
+class PlaneGather:
+    def __init__(self, plane, own, tree, rows, send_sem, recv_sem, local_sem, base):
+        half = rows // 2
+        me, mate, x_dev, y_dev = plane.me, plane.mate, plane.x_dev, plane.y_dev
+        diag = plane.diag_dev
+        self.started = []
+
+        def part(dev, start, size):
+            return block_rows(tree, dev * rows + start, size)
+
+        def copy(source, target, device):
+            at = base + len(self.started)
+
+            def build():
+                return pltpu.make_async_remote_copy(
+                    src_ref=source(),
+                    dst_ref=target(),
+                    send_sem=send_sem.at[at],
+                    recv_sem=recv_sem.at[at],
+                    device_id={"shard": device},
+                    device_id_type=MESH_ID,
+                )
+
+            self.started.append(Copy(build))
+            return self.started[-1]
+
+        def from_own(start, size, device):
+            return copy(
+                lambda: own().at[pl.ds(start, size)], lambda: part(me, start, size), device
+            )
+
+        def onward(dev, start, size, device):
+            return copy(lambda: part(dev, start, size), lambda: part(dev, start, size), device)
+
+        self.first_x = from_own(0, half, x_dev)
+        self.first_y = from_own(half, half, y_dev)
+        self.to_mate = from_own(0, rows, mate)
+        self.rest_x = from_own(half, half, x_dev)
+        self.rest_y = from_own(0, half, y_dev)
+        self.turn_y = onward(x_dev, 0, half, y_dev)
+        self.turn_x = onward(y_dev, half, half, x_dev)
+        self.mate_x = onward(x_dev, 0, rows, mate)
+        self.mate_y = onward(y_dev, 0, rows, mate)
+        self.mate_diag = onward(diag, 0, rows, mate)
+        self.local = lambda: pltpu.make_async_copy(own(), part(me, 0, rows), local_sem)
+
+    def begin(self):
+        for copy in (self.first_x, self.first_y, self.to_mate, self.rest_x, self.rest_y):
+            copy.start()
+        self.local().start()
+
+    def forward(self):
+        self.first_x.wait_recv()
+        self.turn_y.start()
+        self.first_y.wait_recv()
+        self.turn_x.start()
+        self.rest_x.wait_recv()
+        self.mate_x.start()
+        self.rest_y.wait_recv()
+        self.mate_y.start()
+
+    def near_rows(self):
+        self.local().wait()
+        self.to_mate.wait_recv()
+        self.mate_x.wait_recv()
+
+    def turned(self):
+        self.turn_y.wait_recv()
+        self.turn_x.wait_recv()
+        self.mate_diag.start()
+
+    def far_rows(self):
+        self.mate_y.wait_recv()
+        self.mate_diag.wait_recv()
+
+    def finish(self):
+        for copy in self.started:
+            copy.wait_send()
+
+
+def grads_kernel(
+    replicas,
+    mid_every,
+    back_every,
+    mid_tree,
+    back_tree,
+    hidden_hbm,
+    gate_back_hbm,
+    up_back_hbm,
+    gate_hbm,
+    up_hbm,
+    down_hbm,
+    gate_out,
+    up_out,
+    down_out,
+    mid_rows,
+    back_rows,
+    gate_sum,
+    up_sum,
+    down_sum,
+    gate_w,
+    up_w,
+    down_w,
+    mid,
+    back,
+    own_hidden,
+    own_gate,
+    own_up,
+    hidden,
+    gate_back,
+    up_back,
+    send_sem,
+    recv_sem,
+    local_sem,
+    block_sem,
+    weight_sem,
+):
+    plane = Plane()
+    units, width = gate_w.shape
+    size = mid.shape[1]
+    rows = mid_every.shape[1]
+    tree_rows = mid_tree.shape[0]
+    blocks = tree_rows // size
+    half_blocks = blocks // 2
+    low = jnp.bfloat16
+    z = lax.axis_index("replica")
+    y = lax.div(plane.me, 4)
+    others = replicas - 1
+    last = (others + 1) * blocks - 1
+    weights = [
+        pltpu.make_async_copy(source, target, weight_sem.at[at])
+        for at, (source, target) in enumerate(
+            ((gate_hbm, gate_w), (up_hbm, up_w), (down_hbm, down_w))
+        )
+    ]
+    gathers = []
+    for step in range(others):
+        pair = []
+        for at, (every, tree) in enumerate(((mid_every, mid_rows), (back_every, back_rows))):
+            count = 2 * step + at
+            pair.append(
+                PlaneGather(
+                    plane,
+                    lambda every=every, step=step: every.at[lax.rem(z + step + 1, replicas)],
+                    tree.at[step],
+                    rows,
+                    send_sem,
+                    recv_sem,
+                    local_sem.at[count],
+                    GATHER_COPIES * count,
+                )
+            )
+        gathers.append(pair)
+
+    def own_loads(block, slot):
+        there = block_at(block * size, size)
+        return [
+            pltpu.make_async_copy(source.at[there], target.at[slot], block_sem.at[slot, at])
+            for at, (source, target) in enumerate(
+                (
+                    (mid_tree, mid),
+                    (back_tree, back),
+                    (hidden_hbm, own_hidden),
+                    (gate_back_hbm, own_gate),
+                    (up_back_hbm, own_up),
+                )
+            )
+        ]
+
+    def other_loads(block, slot):
+        tree = lax.div(block, blocks) - 1
+        within = lax.rem(block, blocks)
+        part = lax.div(within, half_blocks)
+        start = (y + part - 2 * y * part) * half_blocks * size
+        there = block_at(start + lax.rem(within, half_blocks) * size, size)
+        return [
+            pltpu.make_async_copy(source.at[tree, there], target.at[slot], block_sem.at[slot, at])
+            for at, (source, target) in enumerate(((mid_rows, mid), (back_rows, back)))
+        ]
+
+    def add(total, dot, lhs, rhs, slot):
+        def tile(columns):
+            total[:, columns] += dot(lhs, rhs[slot, :, columns])
+
+        by_columns(width, tile)
+
+    events = {}
+
+    def event(block, *actions):
+        events.setdefault(block, []).extend(actions)
+
+    for copy in weights:
+        copy.start()
+    for copy in own_loads(0, 0):
+        copy.start()
+    for total in (down_sum, gate_sum, up_sum):
+        by_rows(units, lambda at, total=total: total.__setitem__((at, slice(None)), jnp.zeros((at.size, width), jnp.float32)))
+    greet(plane.near())
+    for gather in gathers[0]:
+        gather.begin()
+    for step in range(others):
+        mid_gather, back_gather = gathers[step]
+        base = step * blocks
+        event(base + half_blocks - 2, mid_gather.forward)
+        event(base + half_blocks, back_gather.forward)
+        if step + 1 < others:
+            event(base + half_blocks, *[gather.begin for gather in gathers[step + 1]])
+        event(base + blocks - 1, mid_gather.near_rows, back_gather.near_rows)
+        event(base + blocks, mid_gather.turned, back_gather.turned)
+        event(base + blocks + half_blocks - 1, mid_gather.far_rows, back_gather.far_rows)
+
+    def body(block, carry):
+        slot = lax.rem(block, 2)
+        is_own = block < blocks
+
+        @pl.when(is_own)
+        def _():
+            for copy in own_loads(block, slot):
+                copy.wait()
+
+        @pl.when(block == blocks)
+        def _():
+            for copy in weights:
+                copy.wait()
+
+        @pl.when(block >= blocks)
+        def _():
+            for copy in other_loads(block, slot):
+                copy.wait()
+            tile = max(t for t in (384, 256, 128) if units % t == 0)
+            for at in range(units // tile):
+                there = pl.ds(at * tile, tile)
+                gelu_value, slope = gelu_parts(dot_nt(gate_w[there, :], mid[slot]))
+                up_lin = dot_nt(up_w[there, :], mid[slot])
+                hidden_back = dot_nt(down_w[there, :], back[slot]).astype(low).astype(jnp.float32)
+                hidden[there, :] = (gelu_value * up_lin).astype(low)
+                gate_back[there, :] = (hidden_back * up_lin * slope).astype(low)
+                up_back[there, :] = (hidden_back * gelu_value).astype(low)
+
+        for when, actions in events.items():
+
+            @pl.when(block == when)
+            def _(actions=actions):
+                for action in actions:
+                    action()
+
+        @pl.when(block + 1 < blocks)
+        def _():
+            for copy in own_loads(block + 1, 1 - slot):
+                copy.start()
+
+        @pl.when((block + 1 >= blocks) & (block < last))
+        def _():
+            for copy in other_loads(block + 1, 1 - slot):
+                copy.start()
+
+        @pl.when(is_own)
+        def _():
+            add(down_sum, dot_tn, own_hidden[slot], back, slot)
+            add(gate_sum, dot_tn, own_gate[slot], mid, slot)
+            add(up_sum, dot_tn, own_up[slot], mid, slot)
+
+        @pl.when(block >= blocks)
+        def _():
+            stores = []
+            for at, (total, lhs, rhs, out) in enumerate(
+                (
+                    (down_sum, hidden, back, down_out),
+                    (gate_sum, gate_back, mid, gate_out),
+                    (up_sum, up_back, mid, up_out),
+                )
+            ):
+                add(total, dot_nn, lhs[...], rhs, slot)
+                stores.append(pltpu.make_async_copy(total, out, weight_sem.at[3 + at]))
+                pl.when(block == last)(stores[-1].start)
+
+            @pl.when(block == last)
+            def _():
+                for copy in stores:
+                    copy.wait()
+
+        return carry
+
+    lax.fori_loop(0, last + 1, body, 0)
+    for pair in gathers:
+        for gather in pair:
+            gather.finish()
+
+
+def feedforward_grads(
+    mid_every, back_every, mid_tree, back_tree, hidden, gate_back, up_back, gate_w, up_w, down_w
+):
+    replicas, rows, width = mid_every.shape
+    tree_rows = mid_tree.shape[0]
+    units = gate_w.shape[0]
+    size = tree_rows // 6
+    low, full = jnp.bfloat16, jnp.float32
+    copies = GATHER_COPIES * 2 * (replicas - 1)
+    grad = jax.ShapeDtypeStruct((units, width), full)
+    gathered = jax.ShapeDtypeStruct((replicas - 1, tree_rows, width), low)
+    return pl.pallas_call(
+        functools.partial(grads_kernel, replicas),
+        out_shape=(grad, grad, grad, gathered, gathered),
+        in_specs=any_specs(10),
+        out_specs=tuple(any_specs(5)),
+        scratch_shapes=[pltpu.VMEM((units, width), full)] * 3
+        + [pltpu.VMEM((units, width), low)] * 3
+        + [pltpu.VMEM((2, size, width), low)] * 2
+        + [pltpu.VMEM((2, size, units), low)] * 3
+        + [pltpu.VMEM((units, size), low)] * 3
+        + [
+            pltpu.SemaphoreType.DMA((copies,)),
+            pltpu.SemaphoreType.DMA((copies,)),
+            pltpu.SemaphoreType.DMA((2 * (replicas - 1),)),
+            pltpu.SemaphoreType.DMA((2, 5)),
+            pltpu.SemaphoreType.DMA((6,)),
+        ],
+        compiler_params=remote_params(5),
+        cost_estimate=pl.CostEstimate(
+            flops=2 * (6 * replicas - 3) * tree_rows * units * width,
+            bytes_accessed=200 * 2**20,
+            transcendentals=0,
+        ),
+    )(mid_every, back_every, mid_tree, back_tree, hidden, gate_back, up_back, gate_w, up_w, down_w)[:3]
+
+
+def turn(values, cos, sin):
+    half = values.shape[-1] // 2
+    first, second = values[:, :half], values[:, half:]
+    return first * cos - second * sin, second * cos + first * sin
+
+
+def turn_back(values, cos, sin):
+    half = values.shape[-1] // 2
+    first, second = values[:, :half], values[:, half:]
+    return first * cos + second * sin, second * cos - first * sin
+
+
+def allowed_block(query_bits, key_bits, query_start, key_start):
+    shape = (query_bits.shape[0], key_bits.shape[1])
+    query = query_start + lax.broadcasted_iota(jnp.int32, shape, 0)
+    key = key_start + lax.broadcasted_iota(jnp.int32, shape, 1)
+    return (((query_bits & key_bits) != 0) & (key < query)) | (key == query)
+
+
+def attention_forward_kernel(
+    stream,
+    gain,
+    cos_ref,
+    sin_ref,
+    query_bits,
+    key_bits,
+    query_w,
+    key_own,
+    value_own,
+    output_w,
+    tree_out,
+    query_out,
+    key_out,
+    value_out,
+    attended_out,
+    mass_out,
+    total,
+    own,
+    tree,
+    key_w,
+    value_w,
+    lin,
+    send_sem,
+    recv_sem,
+    local_sem,
+    *scratch,
+):
+    plane = Plane()
+    rows, width = stream.shape
+    head = query_w.shape[0]
+    block = 2 * rows
+    half = head // 2
+    low, full = jnp.bfloat16, jnp.float32
+    wires = Wires(send_sem, recv_sem)
+
+    def normed(at):
+        value = stream[at, :].astype(full)
+        own[at, :] = norm_rows(value, gain[...]).astype(low)
+
+    by_rows(rows, normed)
+    greet(plane.near())
+    mine = block_at(plane.core * half, half)
+    key_w[mine, :] = key_own[...]
+    value_w[mine, :] = value_own[...]
+    tree[block_at(plane.me * rows, rows), :] = own[...]
+    halves = [
+        wires.send(key_own, key_w.at[mine], plane.mate),
+        wires.send(value_own, value_w.at[mine], plane.mate),
+    ]
+    seen = []
+
+    def use(chip):
+        if not seen:
+            for copy in halves:
+                copy.wait_recv()
+        seen.append(chip)
+        there = block_at(chip * block, block)
+        cos, sin = cos_ref[there, :], sin_ref[there, :]
+        lin[...] = dot_nt(tree[there, :], query_w[...])
+        first, second = turn(lin[...], cos, sin)
+        query_out[there, :half] = (first * head**-0.5).astype(low)
+        query_out[there, half:] = (second * head**-0.5).astype(low)
+        lin[...] = dot_nt(tree[there, :], key_w[...])
+        first, second = turn(lin[...], cos, sin)
+        key_out[there, :half] = first.astype(low)
+        key_out[there, half:] = second.astype(low)
+        value_out[there, :] = dot_nt(tree[there, :], value_w[...]).astype(low)
+
+    gather_tree(wires, plane, own, tree, rows, use)
+    store = load(tree, tree_out, local_sem.at[0])
+    gathered = list(wires.sent)
+
+    def attend(chip):
+        there = block_at(chip * block, block)
+        bits = query_bits[there, :]
+
+        def chunk(at, carry):
+            result, mass = carry
+            keys = block_at(at * block, block)
+            scores = dot_nt(query_out[there, :], key_out[keys, :])
+            allowed = allowed_block(
+                bits, key_bits[:, pl.ds(pl.multiple_of(at * block, 128), block)], chip * block, at * block
+            )
+            raised = jnp.where(allowed, jnp.exp(score_cap * jnp.tanh(scores / score_cap)), 0.0)
+            result += dot_nn(raised.astype(low), value_out[keys, :])
+            return result, mass + jnp.sum(raised, axis=1, keepdims=True)
+
+        result, mass = lax.fori_loop(
+            0,
+            chip + 1,
+            chunk,
+            (jnp.zeros((block, head), full), jnp.zeros((block, 1), full)),
+        )
+        scale = 1.0 / mass
+        attended_out[there, :] = (result * scale).astype(low)
+        mass_out[there, :] = jnp.broadcast_to(scale, (block, mass_out.shape[1]))
+
+    def product(chip, columns):
+        return dot_nn(attended_out[block_at(chip * block, block), :], output_w[:, columns])
+
+    scatter_sum(wires, plane, scratch, product, total, attend)
+    for copy in gathered:
+        copy.wait_send()
+    store.wait()
+
+
+def attention_forward(
+    stream, gain, cos, sin, query_bits, key_bits, query_weight, key_weight, value_weight, output_weight
+):
+    rows, width = stream.shape
+    head = query_weight.shape[0]
+    tree_rows = cos.shape[0]
+    low, full = jnp.bfloat16, jnp.float32
+    copies = GATHER_COPIES + SCATTER_COPIES + 2
+    heads = jax.ShapeDtypeStruct((tree_rows, head), low)
+    return pl.pallas_call(
+        attention_forward_kernel,
+        out_shape=(
+            jax.ShapeDtypeStruct((tree_rows, width), low),
+            heads,
+            heads,
+            heads,
+            heads,
+            jax.ShapeDtypeStruct((tree_rows, 128), full),
+            jax.ShapeDtypeStruct((rows, width), full),
+        ),
+        in_specs=vmem_specs(10),
+        out_specs=tuple(any_specs(1) + vmem_specs(6)),
+        scratch_shapes=[
+            pltpu.VMEM((rows, width), low),
+            pltpu.VMEM((tree_rows, width), low),
+            pltpu.VMEM((head, width), low),
+            pltpu.VMEM((head, width), low),
+            pltpu.VMEM((2 * rows, head), full),
+            pltpu.SemaphoreType.DMA((copies,)),
+            pltpu.SemaphoreType.DMA((copies,)),
+            pltpu.SemaphoreType.DMA((1,)),
+        ]
+        + scatter_scratch(rows, width),
+        compiler_params=remote_params(3),
+        cost_estimate=pl.CostEstimate(
+            flops=10 * tree_rows * head * width, bytes_accessed=20 * 2**20, transcendentals=0
+        ),
+    )(
+        stream,
+        gain[None],
+        cos,
+        sin,
+        query_bits,
+        key_bits,
+        query_weight,
+        key_weight,
+        value_weight,
+        output_weight,
+    )
+
+
+def attention_backward_kernel(
+    own,
+    cos_ref,
+    sin_ref,
+    query_bits,
+    key_bits,
+    weights,
+    output_w,
+    queries,
+    keys_ref,
+    values,
+    attended,
+    mass,
+    tree_out,
+    back_out,
+    total,
+    tree,
+    attended_back,
+    query_sum,
+    key_sum,
+    value_sum,
+    mate_out,
+    mate_in,
+    send_sem,
+    recv_sem,
+    local_sem,
+    *scratch,
+):
+    plane = Plane()
+    rows, width = own.shape
+    head = output_w.shape[0]
+    half = head // 2
+    block = 2 * rows
+    low, full = jnp.bfloat16, jnp.float32
+    wires = Wires(send_sem, recv_sem)
+    greet(plane.near())
+    tree[block_at(plane.me * rows, rows), :] = own[...]
+    key_sum[...] = jnp.zeros_like(key_sum)
+    value_sum[...] = jnp.zeros_like(value_sum)
+
+    def use(chip):
+        there = block_at(chip * block, block)
+        attended_back[there, :] = dot_nt(tree[there, :], output_w[...]).astype(low)
+        inner = jnp.sum(
+            attended_back[there, :].astype(full) * attended[there, :].astype(full),
+            axis=1,
+            keepdims=True,
+        )
+        bits = query_bits[there, :]
+        scale = mass[there, :1]
+
+        def chunk(at, result):
+            here = block_at(at * block, block)
+            tanh_value = jnp.tanh(dot_nt(queries[there, :], keys_ref[here, :]) / score_cap)
+            allowed = allowed_block(
+                bits, key_bits[:, pl.ds(pl.multiple_of(at * block, 128), block)], chip * block, at * block
+            )
+            probs = jnp.where(allowed, jnp.exp(score_cap * tanh_value) * scale, 0.0)
+            prob_grads = dot_nt(attended_back[there, :], values[here, :])
+            score_back = (probs * (prob_grads - inner) * (1.0 - tanh_value * tanh_value)).astype(low)
+            value_sum[here, :] += dot_tn(probs.astype(low), attended_back[there, :])
+            key_sum[here, :] += dot_tn(score_back, queries[there, :])
+            return result + dot_nn(score_back, keys_ref[here, :])
+
+        result = lax.fori_loop(0, chip + 1, chunk, jnp.zeros((block, head), full))
+        first, second = turn_back(result * head**-0.5, cos_ref[there, :], sin_ref[there, :])
+        query_sum[there, :half] = first.astype(low)
+        query_sum[there, half:] = second.astype(low)
+
+    gather_tree(wires, plane, own, tree, rows, use)
+    store = load(tree, tree_out, local_sem.at[0])
+    back_out[:, :head] = query_sum[...]
+    first_core = plane.core == 0
+
+    def exchange(at):
+        first, second = turn_back(key_sum[at, :], cos_ref[at, :], sin_ref[at, :])
+        key_sum[at, :half] = jnp.where(first_core, first, second)
+        mate_out[at, :half] = jnp.where(first_core, second, first)
+        first, second = value_sum[at, :half], value_sum[at, half:]
+        value_sum[at, :half] = jnp.where(first_core, first, second)
+        mate_out[at, half:] = jnp.where(first_core, second, first)
+
+    by_rows(tree.shape[0], exchange)
+    swap = wires.send(mate_out, mate_in, plane.mate)
+    swap.wait_recv()
+
+    def finish(at):
+        back_out[at, head : head + half] = (key_sum[at, :half] + mate_in[at, :half]).astype(low)
+        back_out[at, head + half :] = (value_sum[at, :half] + mate_in[at, half:]).astype(low)
+
+    by_rows(tree.shape[0], finish)
+    gathered = list(wires.sent)
+
+    def product(chip, columns):
+        return dot_nn(back_out[block_at(chip * block, block), :], weights[:, columns])
+
+    scatter_sum(wires, plane, scratch, product, total)
+    for copy in gathered:
+        copy.wait_send()
+    store.wait()
+
+
+def attention_backward(
+    own, cos, sin, query_bits, key_bits, weights, output_weight, queries, keys, values, attended, mass
+):
+    rows, width = own.shape
+    head = output_weight.shape[0]
+    tree_rows = cos.shape[0]
+    low, full = jnp.bfloat16, jnp.float32
+    copies = GATHER_COPIES + SCATTER_COPIES + 1
+    return pl.pallas_call(
+        attention_backward_kernel,
+        out_shape=(
+            jax.ShapeDtypeStruct((tree_rows, width), low),
+            jax.ShapeDtypeStruct((tree_rows, 2 * head), low),
+            jax.ShapeDtypeStruct((rows, width), full),
+        ),
+        in_specs=vmem_specs(12),
+        out_specs=tuple(any_specs(1) + vmem_specs(2)),
+        scratch_shapes=[
+            pltpu.VMEM((tree_rows, width), low),
+            pltpu.VMEM((tree_rows, head), low),
+            pltpu.VMEM((tree_rows, head), low),
+            pltpu.VMEM((tree_rows, head), full),
+            pltpu.VMEM((tree_rows, head), full),
+            pltpu.VMEM((tree_rows, head), full),
+            pltpu.VMEM((tree_rows, head), full),
+            pltpu.SemaphoreType.DMA((copies,)),
+            pltpu.SemaphoreType.DMA((copies,)),
+            pltpu.SemaphoreType.DMA((1,)),
+        ]
+        + scatter_scratch(rows, width),
+        compiler_params=remote_params(4),
+        cost_estimate=pl.CostEstimate(
+            flops=10 * tree_rows * head * width, bytes_accessed=20 * 2**20, transcendentals=0
+        ),
+    )(own, cos, sin, query_bits, key_bits, weights, output_weight, queries, keys, values, attended, mass)
+
+
 def shards_heads(
     hidden_in,
     cotangent,
@@ -883,43 +1542,27 @@
 ):
     low = jnp.bfloat16
     row_count, model_width = hidden_in.shape
-    shard_count = lax.axis_size("shard")
-    tree_count = lax.axis_size("replica")
     shard = lax.axis_index("shard")
     row_start = shard * row_count
-    tree_size = token_segment.shape[0]
     position, parent_tok, grand_tok = tree_tables(token_segment, token_valid, segment_parent[0])
-    key_index = jnp.arange(tree_size, dtype=jnp.int32)
-    allowed = allowed_mask(
-        key_index, token_segment, parent_tok, grand_tok, key_index, token_segment, token_valid
-    )
+    key_bits = jnp.where(token_valid == 1, 1 << token_segment, 0)[None]
+    query_bits = ((1 << token_segment) | (1 << parent_tok) | (1 << grand_tok))[:, None]
     cos_table, sin_table = rope_tables(position, HEAD)
-    cos_table, sin_table = cos_table[:, 0], sin_table[:, 0]
-    query_scale = HEAD ** (-0.5)
+    cos_table, sin_table = cos_table[:, 0, : HEAD // 2], sin_table[:, 0, : HEAD // 2]
     valid_rows = lax.dynamic_slice_in_dim(token_valid, row_start, row_count).astype(jnp.float32)
     stream = hidden_in.astype(jnp.float32)
-    second_core = lax.rem(shard, 2) == 1
-    pairs = [(i, i ^ 1) for i in range(shard_count)]
-
-    def both_halves(own):
-        other = lax.ppermute(own, "shard", pairs)
-        return jnp.where(
-            second_core, jnp.concatenate([other, own]), jnp.concatenate([own, other])
-        )
-
-    key_head = both_halves(key_weight)
-    value_head = both_halves(value_weight)
-    normed_in = group_rows(norm_rows(stream, attention_gain).astype(low))
-    queries = (
-        rotate(dot_nt(normed_in, query_weight), cos_table, sin_table) * query_scale
-    ).astype(low)
-    keys = rotate(dot_nt(normed_in, key_head), cos_table, sin_table).astype(low)
-    values = dot_nt(normed_in, value_head).astype(low)
-    tanh_value = jnp.tanh(dot_nt(queries, keys) / score_cap)
-    raised = jnp.where(allowed, jnp.exp(score_cap * tanh_value), 0.0)
-    scale = 1.0 / jnp.sum(raised, axis=-1, keepdims=True)
-    attended = dot_nn((raised * scale).astype(low), values).astype(low)
-    attention_pre = sum_low(dot_nn(attended, output_weight))
+    normed_in, queries, keys, values, attended, mass, attention_pre = attention_forward(
+        hidden_in,
+        attention_gain,
+        cos_table,
+        sin_table,
+        query_bits,
+        key_bits,
+        query_weight,
+        key_weight,
+        value_weight,
+        output_weight,
+    )
     attention_branch = norm_rows(attention_pre, attention_post_gain)
     middle = stream + attention_branch
     normed_mid = norm_rows(middle, feedforward_gain).astype(low)
@@ -941,49 +1584,28 @@
     ffpre_tree, gate_back, up_back, ffpre_every, mid_back = feedforward_backward(
         ffpre_low, gate_weight, up_weight, down_weight, mix, gelu_value
     )
-    mid_every = lax.all_gather(mid_every, "shard", axis=1, tiled=True)
-    ffpre_every = lax.all_gather(ffpre_every, "shard", axis=1, tiled=True)
-
-    def hidden_grads(gate_lin, up_lin, gelu_value, gelu_slope, ffpre_rows):
-        hidden_back = dot_nt(ffpre_rows, down_weight).astype(low).astype(jnp.float32)
-        gate_back = (hidden_back * up_lin * gelu_slope).astype(low)
-        up_back = (hidden_back * gelu_value).astype(low)
-        return gate_back, up_back
-
     middle_part, grad_three = norm_back(middle, feedforward_gain, mid_back)
     middle_back = seed_grad + middle_part
     attention_pre_back, grad_two = norm_back(attention_pre, attention_post_gain, middle_back)
-    pre_tree = group_rows(attention_pre_back.astype(low))
-    attended_back = dot_nt(pre_tree, output_weight).astype(low)
-    probs_back = raised * scale
-    prob_grads = dot_nt(attended_back, values)
-    inner_sum = jnp.sum(probs_back * prob_grads, axis=-1, keepdims=True)
-    score_back = (probs_back * (prob_grads - inner_sum) * (1.0 - tanh_value * tanh_value)).astype(
-        low
-    )
-    query_back = dot_nn(score_back, keys)
-    key_back = dot_tn(score_back, queries)
-    value_back = dot_tn(probs_back.astype(low), attended_back)
-    key_back, value_back = (
-        key_back + lax.ppermute(key_back, "shard", pairs),
-        value_back + lax.ppermute(value_back, "shard", pairs),
-    )
-    query_low = rotate_back(query_back * query_scale, cos_table, sin_table).astype(low)
-    key_low = rotate_back(key_back, cos_table, sin_table).astype(low)
-    value_low = value_back.astype(low)
-    half = HEAD // 2
-    key_low = jnp.where(second_core, key_low[:, half:], key_low[:, :half])
-    value_low = jnp.where(second_core, value_low[:, half:], value_low[:, :half])
-    normed_back = sum_low(
-        dot_nn(query_low, query_weight) + dot_nn(key_low, key_weight) + dot_nn(value_low, value_weight)
+    pre_tree, projection_back, normed_back = attention_backward(
+        attention_pre_back.astype(low),
+        cos_table,
+        sin_table,
+        query_bits,
+        key_bits,
+        jnp.concatenate([query_weight, key_weight, value_weight]),
+        output_weight,
+        queries,
+        keys,
+        values,
+        attended,
+        mass,
     )
     stream_part, grad_one = norm_back(stream, attention_gain, normed_back)
     input_grad = middle_back + stream_part
     attention_grads = jnp.concatenate(
         [
-            dot_tn(query_low, normed_in),
-            dot_tn(key_low, normed_in),
-            dot_tn(value_low, normed_in),
+            dot_tn(projection_back, normed_in),
             dot_tn(attended, pre_tree),
         ]
     ).astype(low)
@@ -992,24 +1614,23 @@
     query_sum, key_sum, value_sum, output_sum = jnp.split(
         attention_grads, [sizes[0], sizes[0] + sizes[1], sum(sizes)]
     )
-    gate_sum = dot_tn(gate_back, mid_tree)
-    up_sum = dot_tn(up_back, mid_tree)
-    down_sum = dot_tn(hidden, ffpre_tree)
-    for step in range(1, tree_count):
-        tree = lax.rem(lax.axis_index("replica") + step, tree_count)
-        mid_rows = lax.dynamic_index_in_dim(mid_every, tree, 0, False)
-        ffpre_rows = lax.dynamic_index_in_dim(ffpre_every, tree, 0, False)
-        gate_lin = dot_nt(mid_rows, gate_weight)
-        up_lin = dot_nt(mid_rows, up_weight)
-        gelu_value, gelu_slope = gelu_parts(gate_lin)
-        hidden = (gelu_value * up_lin).astype(low)
-        gate_back, up_back = hidden_grads(gate_lin, up_lin, gelu_value, gelu_slope, ffpre_rows)
-        gate_sum += dot_tn(gate_back, mid_rows)
-        up_sum += dot_tn(up_back, mid_rows)
-        down_sum += dot_tn(hidden, ffpre_rows)
-    gain_one, gain_two, gain_three, gain_four, squares_all, valid_all = lax.psum(
-        (grad_one, grad_two, grad_three, grad_four, squares, valid_total), ("replica", "shard")
-    )
+    gate_sum, up_sum, down_sum = feedforward_grads(
+        mid_every,
+        ffpre_every,
+        mid_tree,
+        ffpre_tree,
+        hidden,
+        gate_back,
+        up_back,
+        gate_weight,
+        up_weight,
+        down_weight,
+    )
+    extras = jnp.pad(jnp.append(squares, valid_total), (0, model_width - 5))
+    smalls = jnp.stack([grad_one, grad_two, grad_three, grad_four, extras])
+    smalls = jnp.sum(lax.all_gather(smalls, ("replica", "shard")), axis=0)
+    gain_one, gain_two, gain_three, gain_four = smalls[0], smalls[1], smalls[2], smalls[3]
+    squares_all, valid_all = smalls[4, :4], smalls[4, 4]
     stream_rms = jnp.sqrt(squares_all / valid_all)
     return (
         result.astype(low),

time: 1250 us -> 725 us (0.58)
  waiting for transfers between devices: 492 us -> 0.04 us
  Pallas kernels: 171 us -> 606 us
  matrix products: 435 us -> 12.5 us
  blocking collectives: 41.3 us -> 0 us
  local copies, waits for them, and re-layouts: 11.8 us -> 35.7 us
  other arithmetic: 68.4 us -> 45.4 us
    pallas_call x0 -> x3, Pallas kernels: none -> 435 us  [the longest x1 268 us: feedforward_grads(): pl.pallas_call(functools.partial(grads_kernel, replicas), out_shape=(grad...]
    all_gather x4 -> x1, waiting for transfers between devices: 298 us -> 0.01 us  [shards_heads(): smalls = jnp.sum(lax.all_gather(smalls, ('replica', 'shard')), axis=0)]
    dot_general x18 -> x2, matrix products: 242 us -> 12.5 us  [dot_tn(): lax.dot_general(left, right, (((0,), (0,)), ((), ())), preferred_element_...]
    dot_general x21 -> x0, matrix products: 192 us -> none  [the longest x15 158 us: dot_nt(): lax.dot_general(left, right, (((1,), (1,)), ((), ())), preferred_element_...]
    reduce_scatter x2 -> x0, waiting for transfers between devices: 125 us -> none  [sum_low(): lax.psum_scatter(values.astype(jnp.bfloat16), 'shard', scatter_dimension=...]
    psum x1, waiting for transfers between devices: 67.2 us -> 0.01 us  [shards_heads(): attention_grads = lax.psum(attention_grads, 'replica').astype(jnp.float32)]
    psum x1 -> x0, blocking collectives: 41.3 us -> none  [shards_heads(): lax.psum((grad_one, grad_two, grad_three, grad_four, squares, valid_total...]
    convert_element_type x6 -> x1, other arithmetic: 22.2 us -> 1.46 us  [shards_heads(): attention_pre_back.astype(low)]
  transfers between devices with their start and end apart: 11 -> 2, of which waited for: 7 -> 0; matrix products, arithmetic and copies ran while one was open for 13% -> 3% of each run, Pallas kernels for 0% -> 37%
where the time goes in v3:
time: 725 us; the launch traced here: 716 us
  Pallas kernels  606 us (84%)
  other arithmetic  45.4 us (6%)
  local copies, waits for them, and re-layouts  35.7 us (5%)
  between operations  17 us (2%)
  matrix products  12.5 us (2%)
    pallas_call x1, Pallas kernels, feedforward_grads(): pl.pallas_call(functools.partial(grads_kernel, replicas), out_shape=(grad...  268 us
    pallas_call x1, Pallas kernels, feedforward_forward(): pl.pallas_call(functools.partial(forward_kernel, replicas), out_shape=(ja...  86.8 us
    pallas_call x1, Pallas kernels, attention_backward(): pl.pallas_call(attention_backward_kernel, out_shape=(jax.ShapeDtypeStruct...  84.5 us
    pallas_call x1, Pallas kernels, feedforward_backward(): pl.pallas_call(functools.partial(backward_kernel, replicas), out_shape=(j...  83.9 us
    pallas_call x1, Pallas kernels, attention_forward(): pl.pallas_call(attention_forward_kernel, out_shape=(jax.ShapeDtypeStruct(...  82.5 us
    unnamed x51, local copies, waits for them, and re-layouts  22.6 us
  transfers between devices with their start and end apart: 2, of which 0 were waited for; matrix products, arithmetic and copies ran while one was open for 3% of the time, Pallas kernels for 37%

profile of v3, /device:TPU:0, one launch (start us, length us, event | category | flops | bytes accessed | tf_op | source)
XLA Modules:
  0.0 716.3 jit_solution(15160676387955597905)
XLA Ops:
  8.0 0.0 all-gather.4.cloned.1.call-start
  8.1 1.3 broadcast_in_dim.14.gain
  9.4 0.7 broadcast_add_fusion
  10.1 0.9 select_reduce_fusion.5
  11.0 0.7 broadcast_add_fusion.3
  11.7 0.7 broadcast_add_fusion.2
  12.4 0.7 broadcast_add_fusion.1
  13.1 0.9 select_reduce_fusion.1
  14.1 0.7 compare_select_fusion
  14.8 0.6 broadcast_in_dim.19.key_bits
  15.4 0.8 select_reduce_fusion.6
  16.3 0.7 fusion.26
  16.9 0.8 select_reduce_fusion.2
  17.7 1.1 broadcast_in_dim.20.query_bits
  18.9 0.3 multiply_bitcast_fusion
  19.1 3.6 fusion.16
  22.7 0.0 copy-done.11
  22.7 1.6 pad_maximum_fusion.1.weights
  24.3 82.5 %shard_map.263 = (bf16[1536,2304]{1,0:T(8,128)(2,1)}, bf16[1536,256]{1,0:T(8,128)(2,1)}, bf16[1536,256]{1,0:T(8,128)(2,1)}, bf16[1536,256]{1,0:T(8,128)(2,1)}, b...) custom-call(bf16[192,2304]{1,0:T(8,128)(2,1)} %stream.1, f32[1,2304]{1,0:T(1,128)} %broadcast_in_dim.14.gain, ...), custom_call_target="tpu_custom_call" | custom-call | flops 9059696640 | bytes 20971520 | tf_op jit(solution)/shard_map/pallas_call | solution.py:1344
  106.9 1.8 multiply_reduce_fusion.8
  108.7 0.2 copy-done
  108.9 1.8 multiply_reduce_fusion.7
  110.7 0.0 copy-start.15
  110.7 1.1 multiply_convert_fusion.own
  111.9 86.8 %shard_map.264 = (bf16[1536,2304]{1,0:T(8,128)(2,1)}, bf16[1536,1152]{1,0:T(8,128)(2,1)}, bf16[1536,1152]{1,0:T(8,128)(2,1)}, bf16[1536,1152]{1,0:T(8,128)(2,1)}...) custom-call(bf16[192,2304]{1,0:T(8,128)(2,1)} %multiply_convert_fusion.own, bf16[1152,2304]{1,0:T(8,128)(2,1)} %gate_hbm.5, ...), custom_call_target="tpu_custom_call" | custom-call | flops 24461180928 | bytes 41943040 | tf_op jit(solution)/shard_map/pallas_call | solution.py:700
  198.7 0.0 copy-start.6
  198.7 1.8 multiply_reduce_fusion.6
  200.4 1.4 fusion.27
  201.8 0.0 copy-done.6
  201.8 4.4 multiply_reduce_fusion
  206.2 1.4 subtract_convert_fusion.1.own
  207.6 83.9 %shard_map.265 = (bf16[1536,2304]{1,0:T(8,128)(2,1)}, bf16[1536,1152]{1,0:T(8,128)(2,1)}, bf16[1536,1152]{1,0:T(8,128)(2,1)}, bf16[4,192,2304]{2,1,0:T(8,128)(2,1)}, f32[192,2304]{1,0:T(8,128)}) custom-call(bf16[192,2304]{1,0:T(8,128)(2,1)} %subtract_convert_fusion.1.own, bf16[1152,2304]{1,0:T(8,128)(2,1)} %gate_hbm.5, bf16[1152,2304]{1,0:T(8,128)(2,1)} %up_hbm.5, ...), custom_call_target="tpu_custom_call" | custom-call | flops 24461180928 | bytes 41943040 | tf_op jit(solution)/shard_map/pallas_call | solution.py:836
  291.5 0.0 copy-start.7
  291.5 2.1 multiply_reduce_fusion.1
  293.7 0.1 copy-done.7
  293.7 3.4 multiply_reduce_fusion.2
  297.2 1.5 subtract_convert_fusion.own
  298.7 84.5 %shard_map.266 = (bf16[1536,2304]{1,0:T(8,128)(2,1)}, bf16[1536,512]{1,0:T(8,128)(2,1)}, f32[192,2304]{1,0:T(8,128)}) custom-call(bf16[192,2304]{1,0:T(8,128)(2,1)} %subtract_convert_fusion.own, f32[1536,128]{1,0:T(8,128)} %get-tuple-element.96.cos_ref, f32[1536,128]{1,0:T(8,128)} %get-tuple-element.95.sin_ref, s32[1536,1]{1,0:T(8,128)} %broadcast_in_dim.20.query_bits, ...), custom_call_target="tpu_custom_call" | custom-call | flops 9059696640 | bytes 20971520 | tf_op jit(solution)/shard_map/pallas_call | solution.py:1496
  383.2 3.1 fusion.8
  387.0 2.6 concatenate.35
  389.6 0.7 stack.40
  390.3 0.0 all-gather.4.cloned.1.call-update
  390.4 0.0 all-reduce.3.cloned.1.call-start
  390.4 5.2 convolution_convert_fusion.1
  395.6 0.0 copy-done.20
  395.6 7.4 %convolution_convert_fusion = bf16[512,2304]{1,0:T(8,128)(2,1)S(1)} fusion(bf16[1536,512]{1,0:T(8,128)(2,1)S(1)} %copy-done.20, bf16[1536,2304]{1,0:T(8,128)(2,1)} %get-tuple-element.50), kind=kOutput, calls=%fused_computation | convolution fusion | flops 3625058304 | bytes 11010048 | tf_op jit(solution)/shard_map/dot_general | solution.py:346
  403.0 2.0 pad_maximum_fusion
  405.0 0.0 all-reduce.3.cloned.1.call-update
  405.0 0.0 copy-start.18
  405.0 0.0 copy-start.19
  405.1 0.0 copy-start.3
  405.1 0.0 copy-start.14
  405.1 0.0 copy-start.16
  405.1 267.8 %shard_map.267 = (f32[1152,2304]{1,0:T(8,128)}, f32[1152,2304]{1,0:T(8,128)}, f32[1152,2304]{1,0:T(8,128)}, bf16[3,1536,2304]{2,1,0:T(8,128)(2,1)}, bf16[3,1536,2304]{2,1,0:T(8,128)(2,1)}) custom-call(bf16[4,192,2304]{2,1,0:T(8,128)(2,1)} %get-tuple-element.52.mid_every, bf16[4,192,2304]{2,1,0:T(8,128)(2,1)} %get-tuple-element.53.back_every, ...), custom_call_target="tpu_custom_call" | custom-call | flops 171228266496 | bytes 209715200 | tf_op jit(solution)/shard_map/pallas_call | solution.py:1183
  673.0 3.4 fusion.6
  676.4 1.8 reduce_sum.283
  678.2 0.6 slice.39
  678.8 0.7 slice_reduce_fusion
  679.5 1.2 fusion.25
  680.7 2.9 fusion.29
  683.6 2.5 fusion.28
  686.2 9.1 %copy.40 = f32[1152,2304]{1,0:T(8,128)} copy(f32[1152,2304]{1,0:T(8,128)} %get-tuple-element.120) | data formatting | bytes 21233664
  695.3 9.0 %copy.41 = f32[1152,2304]{1,0:T(8,128)} copy(f32[1152,2304]{1,0:T(8,128)} %get-tuple-element.121) | data formatting | bytes 21233664
  704.3 4.1 copy.42
  (53 shorter events, 0.2 us)
Async XLA Ops:
  8.0 668.4 %all-gather.4.cloned.1.call-start = ((), (), s32[]{:S(2)}) async-start(), calls=%async_computation.1 | async-start | bytes 2433024 | tf_op jit(solution)/shard_map/all_gather | solution.py:1631
  10.1 373.1 %copy-start.13 = (f32[2304]{0:T(1024)}, f32[2304]{0:T(1024)S(1)}, u32[]{:S(2)}) copy-start(f32[2304]{0:T(1024)S(1)} %broadcast_add_fusion) | copy-start | bytes 27652
  18.9 3.9 copy-start.10
  18.9 3.9 copy-start.11
  18.9 3.9 copy-start.12
  106.9 2.0 copy-start
  110.7 88.0 %copy-start.17 = (f32[192]{0:T(256)}, f32[192]{0:T(256)S(1)}, u32[]{:S(2)}) copy-start(f32[192]{0:T(256)S(1)} %get-tuple-element.94) | copy-start | bytes 2308
  110.7 272.4 %copy-start.15 = (f32[192]{0:T(256)}, f32[192]{0:T(256)S(1)}, u32[]{:S(2)}) copy-start(f32[192]{0:T(256)S(1)} %add_rsqrt_fusion) | copy-start | bytes 2308
  198.7 3.1 copy-start.6
  201.8 4.4 copy-start.4
  291.5 2.2 copy-start.1
  291.5 2.2 copy-start.7
  297.2 1.5 copy-start.2
  298.7 84.5 %copy-start.8 = (bf16[192,2304]{1,0:T(8,128)(2,1)S(1)}, bf16[192,2304]{1,0:T(8,128)(2,1)}, u32[]{:S(2)}) copy-start(bf16[192,2304]{1,0:T(8,128)(2,1)} %stream.1) | copy-start | bytes 2654212
  383.1 7.3 %copy-start.9 = (bf16[1536,256]{1,0:T(8,128)(2,1)S(1)}, bf16[1536,256]{1,0:T(8,128)(2,1)}, u32[]{:S(2)}) copy-start(bf16[1536,256]{1,0:T(8,128)(2,1)} %get-tuple-element.46.attended) | copy-start | bytes 2359300
  390.4 290.3 %all-reduce.3.cloned.1.call-start = ((), (), s32[]{:S(2)}) async-start(), calls=%async_computation | async-start | bytes 7077888 | tf_op jit(solution)/shard_map/psum | solution.py:1612
  390.4 5.2 copy-start.20
  405.0 267.9 %copy-start.18 = (f32[192]{0:T(256)S(1)}, f32[192]{0:T(256)}, u32[]{:S(2)}) copy-start(f32[192]{0:T(256)} %copy-done.17) | copy-start | bytes 2308
  405.0 267.9 %copy-start.19 = (f32[192]{0:T(256)S(1)}, f32[192]{0:T(256)}, u32[]{:S(2)}) copy-start(f32[192]{0:T(256)} %get-tuple-element.69) | copy-start | bytes 2308
  405.1 267.9 %copy-start.3 = (f32[192,2304]{1,0:T(8,128)S(1)}, f32[192,2304]{1,0:T(8,128)}, u32[]{:S(2)}) copy-start(f32[192,2304]{1,0:T(8,128)} %copy-done.2) | copy-start | bytes 5308420
  405.1 267.9 %copy-start.14 = (f32[2304]{0:T(1024)S(1)}, f32[2304]{0:T(1024)}, u32[]{:S(2)}) copy-start(f32[2304]{0:T(1024)} %copy-done.13) | copy-start | bytes 27652
  405.1 267.9 %copy-start.16 = (f32[192]{0:T(256)S(1)}, f32[192]{0:T(256)}, u32[]{:S(2)}) copy-start(f32[192]{0:T(256)} %copy-done.15) | copy-start | bytes 2308
  680.7 3.0 copy-start.5
  686.2 18.1 %slice-start = ((s8[10616832]{0:T(1024)(128)(4,1)}), s8[4194304]{0:T(1024)(128)(4,1)S(1)}, s32[]{:S(2)}) async-start(s8[10616832]{0:T(1024)(128)(4,1)} %bitcast.38), calls=%async_computation.2 | async-start | bytes 8388608
  686.2 18.1 %slice-start.1 = ((s8[10616832]{0:T(1024)(128)(4,1)}), s8[4194304]{0:T(1024)(128)(4,1)S(1)}, s32[]{:S(2)}) async-start(s8[10616832]{0:T(1024)(128)(4,1)} %bitcast.38), calls=%async_computation.3 | async-start | bytes 8388608
  695.3 9.0 %slice-start.2 = ((s8[10616832]{0:T(1024)(128)(4,1)}), s8[2228224]{0:T(1024)(128)(4,1)S(1)}, s32[]{:S(2)}) async-start(s8[10616832]{0:T(1024)(128)(4,1)} %bitcast.38), calls=%async_computation.4 | async-start | bytes 4456448
Sparse Core Ops, SparseCore 0:
  390.5 138.7 all-gather.3
Sparse Core Ops, SparseCore 1:
  405.1 140.3 all-reduce.2

commit v4 on v3

--- a/solution.py
+++ b/solution.py
@@ -326,8 +326,7 @@
     weighted = gradient * (1.0 + norm_gain)
     inner = jnp.mean(weighted * stream, axis=-1, keepdims=True)
     back = factor * weighted - stream * (factor * factor * factor * inner)
-    gain_back = jnp.sum(gradient * stream * factor, axis=0)
-    return back, gain_back
+    return back, gradient * stream * factor
 
 
 def dot_nt(left, right):
@@ -423,6 +422,10 @@
 
 def block_rows(ref, start, size, step=16):
     return ref.at[pl.ds(pl.multiple_of(start, step), size)]
+
+
+def add_row(sums, at, term):
+    sums[at : at + 1, :] += jnp.sum(term, axis=0, keepdims=True)
 
 
 def by_rows(count, body, size=32):
@@ -484,6 +487,7 @@
 
 
 GATHER_COPIES = 10
+DIAG, SIDE_X, SIDE_Y, OWN = range(4)
 
 
 def scatter_scratch(rows, width):
@@ -501,76 +505,177 @@
     ]
 
 
-def scatter_sum(wires, plane, scratch, product, total, before=None):
-    sums, piece, mate_out, mate_in, x_out, x_in, y_out, y_in = scratch
-    rows, width = total.shape
-    half = rows // 2
-    low, full = jnp.bfloat16, jnp.float32
-
-    def produce(slot, out_slot, in_slot, chip):
-        if before is not None:
-            before(chip)
+class Scatter:
+    def __init__(self, wires, plane, scratch, product, total, order, loads=()):
+        self.loads = list(loads)
+        self.wires, self.plane, self.product, self.total = wires, plane, product, total
+        self.sums, self.piece, self.mate_out, self.mate_in = scratch[:4]
+        self.x_out, self.x_in, self.y_out, self.y_in = scratch[4:]
+        self.order = order
+        self.slots = {place: (0, 1, 2, 0)[at] for at, place in enumerate(order)}
+        if order[0] == OWN:
+            self.slots[SIDE_Y] = self.slots[DIAG]
+        self.rows, self.width = total.shape
+        self.half = self.rows // 2
+        self.to_mate = {}
+
+    def produce(self, place):
+        plane, rows = self.plane, self.rows
+        chip = (plane.diag_chip, plane.x_chip, plane.y_chip, plane.own_chip)[place]
+        slot, at = self.slots[place], self.order.index(place)
+        out_slot = at % 2
+        if at >= 2:
+            self.to_mate[self.order[at - 2]].wait_send()
+        while self.loads:
+            self.loads.pop().wait()
 
         def tile(columns):
-            piece[...] = product(chip, columns)
-            sums[slot, :, columns] = piece[block_at(plane.core * rows, rows), :]
-            mate_out[out_slot, :, columns] = piece[
+            self.piece[...] = self.product(chip, columns)
+            self.sums[slot, :, columns] = self.piece[block_at(plane.core * rows, rows), :]
+            self.mate_out[out_slot, :, columns] = self.piece[
                 block_at((1 - plane.core) * rows, rows), :
-            ].astype(low)
-
-        by_columns(width, tile)
-        return wires.send(mate_out.at[out_slot], mate_in.at[in_slot], plane.mate)
-
-    def low_part(out, out_slot, slot, in_slot, start, more=None):
+            ].astype(jnp.bfloat16)
+
+        by_columns(self.width, tile)
+        self.to_mate[place] = self.wires.send(
+            self.mate_out.at[out_slot], self.mate_in.at[place], plane.mate
+        )
+
+    def low_part(self, out, out_slot, place, start, more=None):
         def step(at):
             there = pl.ds(pl.multiple_of(start + at.start, 16), at.size)
-            value = sums[slot, there, :] + mate_in[in_slot, there, :].astype(full)
+            value = self.sums[self.slots[place], there, :] + self.mate_in[
+                place, there, :
+            ].astype(jnp.float32)
             if more is not None:
-                value += more[0, at, :].astype(full)
-            out[out_slot, at, :] = value.astype(low)
-
-        by_rows(half, step)
-
-    diag = produce(0, 0, 0, plane.diag_chip)
-    to_x = produce(1, 1, 1, plane.x_chip)
-    diag.wait_recv()
-    low_part(x_out, 0, 0, 0, 0)
-    x_first = wires.send(x_out.at[0], x_in.at[0], plane.x_dev)
-    low_part(y_out, 0, 0, 0, half)
-    y_first = wires.send(y_out.at[0], y_in.at[0], plane.y_dev)
-    diag.wait_send()
-    to_y = produce(2, 0, 2, plane.y_chip)
-    to_x.wait_recv()
-    low_part(x_out, 1, 1, 1, 0)
-    x_next = wires.send(x_out.at[1], x_in.at[1], plane.x_dev)
-    to_x.wait_send()
-    to_own = produce(0, 1, 3, plane.own_chip)
-    to_y.wait_recv()
-    low_part(y_out, 1, 2, 2, half)
-    y_next = wires.send(y_out.at[1], y_in.at[1], plane.y_dev)
-    y_first.wait_recv()
-    low_part(x_out, 2, 1, 1, half, y_in)
-    x_last = wires.send(x_out.at[2], x_in.at[2], plane.x_dev)
-    x_first.wait_recv()
-    low_part(y_out, 2, 2, 2, 0, x_in)
-    y_last = wires.send(y_out.at[2], y_in.at[2], plane.y_dev)
-    to_own.wait_recv()
-    for copy in (x_next, y_next, x_last, y_last):
-        copy.wait_recv()
-    for start, x_slot, y_slot in ((0, 1, 2), (half, 2, 1)):
-
-        def step(at, start=start, x_slot=x_slot, y_slot=y_slot):
-            there = pl.ds(pl.multiple_of(start + at.start, 16), at.size)
-            total[there, :] = (
-                sums[0, there, :]
-                + mate_in[3, there, :].astype(full)
-                + x_in[x_slot, at, :].astype(full)
-                + y_in[y_slot, at, :].astype(full)
-            )
-
-        by_rows(half, step)
-    for copy in (to_y, to_own, x_first, x_next, x_last, y_first, y_next, y_last):
+                value += more[0, at, :].astype(jnp.float32)
+            out[out_slot, at, :] = value.astype(jnp.bfloat16)
+
+        by_rows(self.half, step)
+
+    def to_x(self, slot):
+        return self.wires.send(self.x_out.at[slot], self.x_in.at[slot], self.plane.x_dev)
+
+    def to_y(self, slot):
+        return self.wires.send(self.y_out.at[slot], self.y_in.at[slot], self.plane.y_dev)
+
+    def send_diag(self):
+        self.to_mate[DIAG].wait_recv()
+        self.low_part(self.x_out, 0, DIAG, 0)
+        self.x_first = self.to_x(0)
+        self.low_part(self.y_out, 0, DIAG, self.half)
+        self.y_first = self.to_y(0)
+
+    def send_x(self):
+        self.to_mate[SIDE_X].wait_recv()
+        self.low_part(self.x_out, 1, SIDE_X, 0)
+        self.x_next = self.to_x(1)
+
+    def send_y(self):
+        self.to_mate[SIDE_Y].wait_recv()
+        self.low_part(self.y_out, 1, SIDE_Y, self.half)
+        self.y_next = self.to_y(1)
+
+    def turn(self):
+        self.y_first.wait_recv()
+        self.low_part(self.x_out, 2, SIDE_X, self.half, self.y_in)
+        self.x_last = self.to_x(2)
+        self.x_first.wait_recv()
+        self.low_part(self.y_out, 2, SIDE_Y, 0, self.x_in)
+        self.y_last = self.to_y(2)
+
+    def finish(self):
+        self.to_mate[OWN].wait_recv()
+        late = [self.x_next, self.y_next, self.x_last, self.y_last]
+        for copy in late:
+            copy.wait_recv()
+        for start, x_slot, y_slot in ((0, 1, 2), (self.half, 2, 1)):
+
+            def step(at, start=start, x_slot=x_slot, y_slot=y_slot):
+                there = pl.ds(pl.multiple_of(start + at.start, 16), at.size)
+                self.total[there, :] = (
+                    self.sums[self.slots[OWN], there, :]
+                    + self.mate_in[OWN, there, :].astype(jnp.float32)
+                    + self.x_in[x_slot, at, :].astype(jnp.float32)
+                    + self.y_in[y_slot, at, :].astype(jnp.float32)
+                )
+
+            by_rows(self.half, step)
+        for copy in [self.x_first, self.y_first] + late:
+            copy.wait_send()
+        for place in self.order[2:]:
+            self.to_mate[place].wait_send()
+
+
+def scatter_sum(wires, plane, scratch, product, total, before=lambda chip: None, meanwhile=()):
+    scatter = Scatter(wires, plane, scratch, product, total, (DIAG, SIDE_X, SIDE_Y, OWN))
+    work = iter(tuple(meanwhile) + (lambda: None,) * 2)
+    before(plane.diag_chip)
+    scatter.produce(DIAG)
+    before(plane.x_chip)
+    scatter.produce(SIDE_X)
+    scatter.send_diag()
+    before(plane.y_chip)
+    scatter.produce(SIDE_Y)
+    scatter.send_x()
+    before(plane.own_chip)
+    scatter.produce(OWN)
+    scatter.send_y()
+    next(work)()
+    scatter.turn()
+    next(work)()
+    scatter.finish()
+
+
+def gather_and_scatter(wires, plane, own, tree, rows, use, scatter):
+    half = rows // 2
+
+    def part(dev, start, size):
+        return block_rows(tree, dev * rows + start, size)
+
+    def own_part(start, size):
+        return own.at[pl.ds(start, size)]
+
+    def onward(dev, start, size, device):
+        return wires.send(part(dev, start, size), part(dev, start, size), device)
+
+    me, mate, x_dev, y_dev = plane.me, plane.mate, plane.x_dev, plane.y_dev
+    first_x = wires.send(own_part(0, half), part(me, 0, half), x_dev)
+    first_y = wires.send(own_part(half, half), part(me, half, half), y_dev)
+    to_mate = wires.send(own_part(0, rows), part(me, 0, rows), mate)
+    to_mate.wait_recv()
+    use(plane.own_chip)
+    first_x.wait_recv()
+    turn_y = onward(x_dev, 0, half, y_dev)
+    first_y.wait_recv()
+    turn_x = onward(y_dev, half, half, x_dev)
+    rest_x = wires.send(own_part(half, half), part(me, half, half), x_dev)
+    rest_y = wires.send(own_part(0, half), part(me, 0, half), y_dev)
+    scatter.produce(OWN)
+    turn_y.wait_recv()
+    turn_x.wait_recv()
+    mate_diag = onward(plane.diag_dev, 0, rows, mate)
+    mate_diag.wait_recv()
+    use(plane.diag_chip)
+    rest_x.wait_recv()
+    mate_x = onward(x_dev, 0, rows, mate)
+    rest_y.wait_recv()
+    mate_y = onward(y_dev, 0, rows, mate)
+    scatter.produce(DIAG)
+    mate_x.wait_recv()
+    use(plane.x_chip)
+    scatter.send_diag()
+    scatter.produce(SIDE_X)
+    mate_y.wait_recv()
+    use(plane.y_chip)
+    scatter.send_x()
+    scatter.produce(SIDE_Y)
+    copies = [first_x, first_y, to_mate, turn_y, turn_x, rest_x, rest_y, mate_diag, mate_x, mate_y]
+    for copy in copies:
         copy.wait_send()
+    scatter.send_y()
+    scatter.turn()
+    scatter.finish()
 
 
 SCATTER_COPIES = 10
@@ -586,14 +691,30 @@
     return copy
 
 
-def replica_peers(replicas):
-    z = lax.axis_index("replica")
-    return z, [{"replica": lax.rem(z + step, replicas)} for step in range(1, replicas)]
+def replica_steps(replicas, near):
+    return [step for step in range(1, replicas) if (min(step, replicas - step) == 1) == near]
+
+
+def replica_device(replicas, step):
+    return {"replica": lax.rem(lax.axis_index("replica") + step, replicas)}
+
+
+def send_over(wires, source, target, replicas, steps):
+    return [
+        wires.send(
+            source, target.at[steps.index(replicas - step)], replica_device(replicas, step)
+        )
+        for step in steps
+    ]
 
 
 def forward_kernel(
     replicas,
     own,
+    middle,
+    cotangent,
+    valid,
+    gain,
     gate_hbm,
     up_hbm,
     down_hbm,
@@ -602,6 +723,9 @@
     mix_out,
     gelu_out,
     every_out,
+    block_out,
+    back_out,
+    sums_out,
     total,
     tree,
     gate_w,
@@ -625,8 +749,8 @@
         load(up_hbm, up_w, local_sem.at[1]),
         load(down_hbm, down_w, local_sem.at[2]),
     ]
-    z, others = replica_peers(replicas)
-    greet(plane.near() + others)
+    steps = replica_steps(replicas, True)
+    greet(plane.near() + [replica_device(replicas, step) for step in steps])
     tree[block_at(plane.me * rows, rows), :] = own[...]
     stores = []
 
@@ -658,20 +782,33 @@
         stores.append(load(mix.at[slot], mix_out.at[there], local_sem.at[base + 1]))
         stores.append(load(gelu.at[slot], gelu_out.at[there], local_sem.at[base + 2]))
 
-    over = [wires.send(own, every_out.at[z], other) for other in others]
-    gather_tree(wires, plane, own, tree, rows, use)
-    tree_store = load(tree, tree_out, local_sem.at[15])
-    loads[2].wait()
+    over = send_over(wires, own, every_out, replicas, steps)
 
     def product(chip, columns):
         return dot_nn(hidden[block_at(chip * 2 * rows, 2 * rows), :], down_w[:, columns])
 
-    gathered = list(wires.sent)
-    scatter_sum(wires, plane, scratch, product, total)
+    scatter = Scatter(
+        wires, plane, scratch, product, total, (OWN, DIAG, SIDE_X, SIDE_Y), loads[2:]
+    )
+    gather_and_scatter(wires, plane, own, tree, rows, use, scatter)
+    tree_store = load(tree, tree_out, local_sem.at[15])
+    sums_out[...] = jnp.zeros_like(sums_out)
+
+    def finish(at):
+        value = total[at, :]
+        gradient = cotangent[at, :].astype(jnp.float32) * valid[at, :]
+        branch = norm_rows(value, gain[...])
+        result = middle[at, :] + branch
+        block_out[at, :] = result.astype(jnp.bfloat16)
+        back, gain_terms = norm_back(value, gain[...], gradient)
+        back_out[at, :] = back.astype(jnp.bfloat16)
+        add_row(sums_out, 0, gain_terms)
+        add_row(sums_out, 1, valid[at, :] * branch * branch)
+        add_row(sums_out, 2, valid[at, :] * result * result)
+
+    by_rows(rows, finish)
     for copy in over:
-        copy.wait_recv()
-    for copy in gathered:
-        copy.wait_send()
+        copy.wait()
     for copy in stores[0:1] + stores[3:4] + stores[6:] + [tree_store]:
         copy.wait()
 
@@ -690,7 +827,9 @@
     )
 
 
-def feedforward_forward(own, gate_weight, up_weight, down_weight):
+def feedforward_forward(
+    own, middle, cotangent, valid, gain, gate_weight, up_weight, down_weight
+):
     rows, width = own.shape
     units = gate_weight.shape[0]
     replicas, count = lax.axis_size("replica"), lax.axis_size("shard")
@@ -704,12 +843,15 @@
             jax.ShapeDtypeStruct((tree_rows, units), low),
             jax.ShapeDtypeStruct((tree_rows, units), low),
             jax.ShapeDtypeStruct((tree_rows, units), low),
-            jax.ShapeDtypeStruct((replicas, rows, width), low),
-            jax.ShapeDtypeStruct((rows, width), full),
+            jax.ShapeDtypeStruct((len(replica_steps(replicas, True)), rows, width), low),
+            jax.ShapeDtypeStruct((rows, width), low),
+            jax.ShapeDtypeStruct((rows, width), low),
+            jax.ShapeDtypeStruct((8, width), full),
         ),
-        in_specs=vmem_specs(1) + any_specs(3),
-        out_specs=tuple(any_specs(5) + vmem_specs(1)),
+        in_specs=vmem_specs(5) + any_specs(3),
+        out_specs=tuple(any_specs(5) + vmem_specs(3)),
         scratch_shapes=[
+            pltpu.VMEM((rows, width), full),
             pltpu.VMEM((tree_rows, width), low),
             pltpu.VMEM((units, width), low),
             pltpu.VMEM((units, width), low),
@@ -728,12 +870,19 @@
         cost_estimate=pl.CostEstimate(
             flops=6 * tree_rows * units * width, bytes_accessed=40 * 2**20, transcendentals=0
         ),
-    )(own, gate_weight, up_weight, down_weight)
+    )(own, middle, cotangent, valid, gain[None], gate_weight, up_weight, down_weight)
 
 
 def backward_kernel(
     replicas,
     own,
+    middle,
+    attention_pre,
+    cotangent,
+    valid,
+    gain,
+    post_gain,
+    mid_own,
     gate_hbm,
     up_hbm,
     down_hbm,
@@ -743,6 +892,9 @@
     gate_out,
     up_out,
     every_out,
+    middle_out,
+    back_out,
+    sums_out,
     total,
     tree,
     gate_w,
@@ -761,7 +913,7 @@
     plane = Plane()
     rows = own.shape[0]
     wires = Wires(send_sem, recv_sem)
-    chips = [plane.own_chip, plane.x_chip, plane.y_chip, plane.diag_chip]
+    chips = [plane.own_chip, plane.diag_chip, plane.x_chip, plane.y_chip]
 
     def fetch(order):
         there = block_at(chips[order] * 2 * rows, 2 * rows)
@@ -776,8 +928,8 @@
         load(gate_hbm, gate_w, local_sem.at[0]),
         load(up_hbm, up_w, local_sem.at[1]),
     ]
-    z, others = replica_peers(replicas)
-    greet(plane.near() + others)
+    steps = replica_steps(replicas, False)
+    greet(plane.near() + [replica_device(replicas, step) for step in steps])
     tree[block_at(plane.me * rows, rows), :] = own[...]
     stores = []
 
@@ -804,11 +956,7 @@
         stores.append(load(gate_back.at[there], gate_out.at[there], local_sem.at[base]))
         stores.append(load(up_back.at[there], up_out.at[there], local_sem.at[base + 1]))
 
-    over = [wires.send(own, every_out.at[z], other) for other in others]
-    gather_tree(wires, plane, own, tree, rows, use)
-    tree_store = load(tree, tree_out, local_sem.at[19])
-    loads[1].wait()
-    loads[2].wait()
+    over = send_over(wires, mid_own, every_out, replicas, steps)
 
     def product(chip, columns):
         there = block_at(chip * 2 * rows, 2 * rows)
@@ -816,17 +964,44 @@
             up_back[there, :], up_w[:, columns]
         )
 
-    gathered = list(wires.sent)
-    scatter_sum(wires, plane, scratch, product, total)
+    scatter = Scatter(
+        wires, plane, scratch, product, total, (OWN, DIAG, SIDE_X, SIDE_Y), loads[1:]
+    )
+    gather_and_scatter(wires, plane, own, tree, rows, use, scatter)
+    tree_store = load(tree, tree_out, local_sem.at[19])
+    sums_out[...] = jnp.zeros_like(sums_out)
+
+    def finish(at):
+        back, gain_terms = norm_back(middle[at, :], gain[...], total[at, :])
+        back += cotangent[at, :].astype(jnp.float32) * valid[at, :]
+        middle_out[at, :] = back
+        add_row(sums_out, 0, gain_terms)
+        back, gain_terms = norm_back(attention_pre[at, :], post_gain[...], back)
+        back_out[at, :] = back.astype(jnp.bfloat16)
+        add_row(sums_out, 1, gain_terms)
+
+    by_rows(rows, finish)
     for copy in over:
-        copy.wait_recv()
-    for copy in gathered:
-        copy.wait_send()
+        copy.wait()
     for copy in stores + [tree_store]:
         copy.wait()
 
 
-def feedforward_backward(own, gate_weight, up_weight, down_weight, mix, gelu):
+def feedforward_backward(
+    own,
+    middle,
+    attention_pre,
+    cotangent,
+    valid,
+    gain,
+    post_gain,
+    mid_own,
+    gate_weight,
+    up_weight,
+    down_weight,
+    mix,
+    gelu,
+):
     rows, width = own.shape
     units = gate_weight.shape[0]
     replicas, count = lax.axis_size("replica"), lax.axis_size("shard")
@@ -839,12 +1014,15 @@
             jax.ShapeDtypeStruct((tree_rows, width), low),
             jax.ShapeDtypeStruct((tree_rows, units), low),
             jax.ShapeDtypeStruct((tree_rows, units), low),
-            jax.ShapeDtypeStruct((replicas, rows, width), low),
+            jax.ShapeDtypeStruct((len(replica_steps(replicas, False)), rows, width), low),
             jax.ShapeDtypeStruct((rows, width), full),
+            jax.ShapeDtypeStruct((rows, width), low),
+            jax.ShapeDtypeStruct((8, width), full),
         ),
-        in_specs=vmem_specs(1) + any_specs(5),
-        out_specs=tuple(any_specs(4) + vmem_specs(1)),
+        in_specs=vmem_specs(7) + any_specs(6),
+        out_specs=tuple(any_specs(4) + vmem_specs(3)),
         scratch_shapes=[
+            pltpu.VMEM((rows, width), full),
             pltpu.VMEM((tree_rows, width), low),
             pltpu.VMEM((units, width), low),
             pltpu.VMEM((units, width), low),
@@ -863,7 +1041,21 @@
         cost_estimate=pl.CostEstimate(
             flops=6 * tree_rows * units * width, bytes_accessed=40 * 2**20, transcendentals=0
         ),
-    )(own, gate_weight, up_weight, down_weight, mix, gelu)
+    )(
+        own,
+        middle,
+        attention_pre,
+        cotangent,
+        valid,
+        gain[None],
+        post_gain[None],
+        mid_own,
+        gate_weight,
+        up_weight,
+        down_weight,
+        mix,
+        gelu,
+    )
 
 
 class Copy:
@@ -962,7 +1154,8 @@
 
 def grads_kernel(
     replicas,
-    mid_every,
+    mid_near,
+    mid_far,
     back_every,
     mid_tree,
     back_tree,
@@ -972,6 +1165,7 @@
     gate_hbm,
     up_hbm,
     down_hbm,
+    mid_begun,
     gate_out,
     up_out,
     down_out,
@@ -1000,12 +1194,11 @@
     plane = Plane()
     units, width = gate_w.shape
     size = mid.shape[1]
-    rows = mid_every.shape[1]
+    rows = back_every.shape[1]
     tree_rows = mid_tree.shape[0]
     blocks = tree_rows // size
     half_blocks = blocks // 2
     low = jnp.bfloat16
-    z = lax.axis_index("replica")
     y = lax.div(plane.me, 4)
     others = replicas - 1
     last = (others + 1) * blocks - 1
@@ -1016,14 +1209,20 @@
         )
     ]
     gathers = []
+    far = replica_steps(replicas, False)
     for step in range(others):
         pair = []
-        for at, (every, tree) in enumerate(((mid_every, mid_rows), (back_every, back_rows))):
+        if step + 1 in far:
+            mid_own = mid_far.at[far.index(step + 1)]
+        else:
+            mid_own = mid_near.at[min(step, 1)]
+        sources = ((mid_own, mid_rows), (back_every.at[step], back_rows))
+        for at, (own, tree) in enumerate(sources):
             count = 2 * step + at
             pair.append(
                 PlaneGather(
                     plane,
-                    lambda every=every, step=step: every.at[lax.rem(z + step + 1, replicas)],
+                    lambda own=own: own,
                     tree.at[step],
                     rows,
                     send_sem,
@@ -1078,18 +1277,17 @@
     for total in (down_sum, gate_sum, up_sum):
         by_rows(units, lambda at, total=total: total.__setitem__((at, slice(None)), jnp.zeros((at.size, width), jnp.float32)))
     greet(plane.near())
-    for gather in gathers[0]:
-        gather.begin()
-    for step in range(others):
-        mid_gather, back_gather = gathers[step]
+    gathers[0] = gathers[0][1:]
+    gathers[0][0].begin()
+    for step, pair in enumerate(gathers):
         base = step * blocks
-        event(base + half_blocks - 2, mid_gather.forward)
-        event(base + half_blocks, back_gather.forward)
+        event(base + half_blocks - 2, pair[0].forward)
+        event(base + half_blocks, *[gather.forward for gather in pair[1:]])
         if step + 1 < others:
             event(base + half_blocks, *[gather.begin for gather in gathers[step + 1]])
-        event(base + blocks - 1, mid_gather.near_rows, back_gather.near_rows)
-        event(base + blocks, mid_gather.turned, back_gather.turned)
-        event(base + blocks + half_blocks - 1, mid_gather.far_rows, back_gather.far_rows)
+        event(base + blocks - 1, *[gather.near_rows for gather in pair])
+        event(base + blocks, *[gather.turned for gather in pair])
+        event(base + blocks + half_blocks - 1, *[gather.far_rows for gather in pair])
 
     def body(block, carry):
         slot = lax.rem(block, 2)
@@ -1170,9 +1368,21 @@
 
 
 def feedforward_grads(
-    mid_every, back_every, mid_tree, back_tree, hidden, gate_back, up_back, gate_w, up_w, down_w
+    mid_near,
+    mid_far,
+    back_every,
+    mid_tree,
+    back_tree,
+    hidden,
+    gate_back,
+    up_back,
+    gate_w,
+    up_w,
+    down_w,
+    mid_begun,
 ):
-    replicas, rows, width = mid_every.shape
+    replicas = lax.axis_size("replica")
+    width = mid_tree.shape[1]
     tree_rows = mid_tree.shape[0]
     units = gate_w.shape[0]
     size = tree_rows // 6
@@ -1183,8 +1393,9 @@
     return pl.pallas_call(
         functools.partial(grads_kernel, replicas),
         out_shape=(grad, grad, grad, gathered, gathered),
-        in_specs=any_specs(10),
+        in_specs=any_specs(12),
         out_specs=tuple(any_specs(5)),
+        input_output_aliases={11: 3},
         scratch_shapes=[pltpu.VMEM((units, width), full)] * 3
         + [pltpu.VMEM((units, width), low)] * 3
         + [pltpu.VMEM((2, size, width), low)] * 2
@@ -1203,7 +1414,20 @@
             bytes_accessed=200 * 2**20,
             transcendentals=0,
         ),
-    )(mid_every, back_every, mid_tree, back_tree, hidden, gate_back, up_back, gate_w, up_w, down_w)[:3]
+    )(
+        mid_near,
+        mid_far,
+        back_every,
+        mid_tree,
+        back_tree,
+        hidden,
+        gate_back,
+        up_back,
+        gate_w,
+        up_w,
+        down_w,
+        mid_begun,
+    )[:3]
 
 
 def turn(values, cos, sin):
@@ -1236,6 +1460,9 @@
     key_own,
     value_own,
     output_w,
+    post_gain,
+    next_gain,
+    valid,
     tree_out,
     query_out,
     key_out,
@@ -1243,6 +1470,9 @@
     attended_out,
     mass_out,
     total,
+    middle_out,
+    next_out,
+    sums_out,
     own,
     tree,
     key_w,
@@ -1327,13 +1557,37 @@
         return dot_nn(attended_out[block_at(chip * block, block), :], output_w[:, columns])
 
     scatter_sum(wires, plane, scratch, product, total, attend)
+    sums_out[...] = jnp.zeros_like(sums_out)
+
+    def finish(at):
+        value = stream[at, :].astype(full)
+        branch = norm_rows(total[at, :], post_gain[...])
+        middle = value + branch
+        middle_out[at, :] = middle
+        next_out[at, :] = norm_rows(middle, next_gain[...]).astype(low)
+        add_row(sums_out, 0, valid[at, :] * value * value)
+        add_row(sums_out, 1, valid[at, :] * branch * branch)
+
+    by_rows(rows, finish)
     for copy in gathered:
         copy.wait_send()
     store.wait()
 
 
 def attention_forward(
-    stream, gain, cos, sin, query_bits, key_bits, query_weight, key_weight, value_weight, output_weight
+    stream,
+    gain,
+    cos,
+    sin,
+    query_bits,
+    key_bits,
+    query_weight,
+    key_weight,
+    value_weight,
+    output_weight,
+    post_gain,
+    next_gain,
+    valid,
 ):
     rows, width = stream.shape
     head = query_weight.shape[0]
@@ -1351,9 +1605,12 @@
             heads,
             jax.ShapeDtypeStruct((tree_rows, 128), full),
             jax.ShapeDtypeStruct((rows, width), full),
+            jax.ShapeDtypeStruct((rows, width), full),
+            jax.ShapeDtypeStruct((rows, width), low),
+            jax.ShapeDtypeStruct((8, width), full),
         ),
-        in_specs=vmem_specs(10),
-        out_specs=tuple(any_specs(1) + vmem_specs(6)),
+        in_specs=vmem_specs(13),
+        out_specs=tuple(any_specs(1) + vmem_specs(9)),
         scratch_shapes=[
             pltpu.VMEM((rows, width), low),
             pltpu.VMEM((tree_rows, width), low),
@@ -1380,10 +1637,14 @@
         key_weight,
         value_weight,
         output_weight,
+        post_gain[None],
+        next_gain[None],
+        valid,
     )
 
 
 def attention_backward_kernel(
+    replicas,
     own,
     cos_ref,
     sin_ref,
@@ -1396,10 +1657,22 @@
     values,
     attended,
     mass,
+    stream,
+    gain,
+    middle_back,
+    normed_hbm,
+    mid_near,
+    ffn_own,
     tree_out,
+    mid_rows,
+    every_out,
     back_out,
+    grads_out,
+    input_out,
+    sums_out,
     total,
     tree,
+    normed,
     attended_back,
     query_sum,
     key_sum,
@@ -1409,6 +1682,8 @@
     send_sem,
     recv_sem,
     local_sem,
+    mid_send_sem,
+    mid_recv_sem,
     *scratch,
 ):
     plane = Plane()
@@ -1418,12 +1693,30 @@
     block = 2 * rows
     low, full = jnp.bfloat16, jnp.float32
     wires = Wires(send_sem, recv_sem)
-    greet(plane.near())
+    normed_load = load(normed_hbm, normed, local_sem.at[1])
+    mid_gather = PlaneGather(
+        plane,
+        lambda: mid_near.at[0],
+        mid_rows.at[0],
+        rows,
+        mid_send_sem,
+        mid_recv_sem,
+        local_sem.at[2],
+        0,
+    )
+    steps = list(range(1, replicas))
+    greet(plane.near() + [replica_device(replicas, step) for step in steps])
+    over = send_over(wires, ffn_own, every_out, replicas, steps)
     tree[block_at(plane.me * rows, rows), :] = own[...]
     key_sum[...] = jnp.zeros_like(key_sum)
     value_sum[...] = jnp.zeros_like(value_sum)
 
+    seen = []
+
     def use(chip):
+        seen.append(chip)
+        if len(seen) == 3:
+            mid_gather.begin()
         there = block_at(chip * block, block)
         attended_back[there, :] = dot_nt(tree[there, :], output_w[...]).astype(low)
         inner = jnp.sum(
@@ -1479,30 +1772,70 @@
     def product(chip, columns):
         return dot_nn(back_out[block_at(chip * block, block), :], weights[:, columns])
 
-    scatter_sum(wires, plane, scratch, product, total)
+    def projection_grads():
+        mid_gather.forward()
+        normed_load.wait()
+
+        def tile(columns):
+            grads_out[: 2 * head, columns] = dot_tn(back_out[...], normed[:, columns]).astype(low)
+
+        by_columns(width, tile)
+
+    def output_grads():
+        mid_gather.turned()
+
+        def tile(columns):
+            grads_out[2 * head :, columns] = dot_tn(attended[...], tree[:, columns]).astype(low)
+
+        by_columns(width, tile)
+
+    scatter_sum(
+        wires, plane, scratch, product, total, meanwhile=(projection_grads, output_grads)
+    )
+    sums_out[...] = jnp.zeros_like(sums_out)
+
+    def input_rows(at):
+        back, gain_terms = norm_back(stream[at, :].astype(full), gain[...], total[at, :])
+        input_out[at, :] = middle_back[at, :] + back
+        add_row(sums_out, 0, gain_terms)
+
+    by_rows(rows, input_rows)
+    mid_gather.near_rows()
+    mid_gather.far_rows()
+    mid_gather.finish()
+    for copy in over:
+        copy.wait_recv()
     for copy in gathered:
         copy.wait_send()
     store.wait()
 
 
 def attention_backward(
-    own, cos, sin, query_bits, key_bits, weights, output_weight, queries, keys, values, attended, mass
+    own, cos, sin, query_bits, key_bits, weights, output_weight, queries, keys, values, attended, mass,
+    stream, gain, middle_back, normed, mid_near, ffn_own,
 ):
     rows, width = own.shape
     head = output_weight.shape[0]
     tree_rows = cos.shape[0]
+    replicas = lax.axis_size("replica")
     low, full = jnp.bfloat16, jnp.float32
-    copies = GATHER_COPIES + SCATTER_COPIES + 1
+    copies = GATHER_COPIES + SCATTER_COPIES + replicas
     return pl.pallas_call(
-        attention_backward_kernel,
+        functools.partial(attention_backward_kernel, replicas),
         out_shape=(
             jax.ShapeDtypeStruct((tree_rows, width), low),
+            jax.ShapeDtypeStruct((replicas - 1, tree_rows, width), low),
+            jax.ShapeDtypeStruct((replicas - 1, rows, width), low),
             jax.ShapeDtypeStruct((tree_rows, 2 * head), low),
+            jax.ShapeDtypeStruct((3 * head, width), low),
             jax.ShapeDtypeStruct((rows, width), full),
+            jax.ShapeDtypeStruct((8, width), full),
         ),
-        in_specs=vmem_specs(12),
-        out_specs=tuple(any_specs(1) + vmem_specs(2)),
+        in_specs=vmem_specs(15) + any_specs(3),
+        out_specs=tuple(any_specs(3) + vmem_specs(4)),
         scratch_shapes=[
+            pltpu.VMEM((rows, width), full),
+            pltpu.VMEM((tree_rows, width), low),
             pltpu.VMEM((tree_rows, width), low),
             pltpu.VMEM((tree_rows, head), low),
             pltpu.VMEM((tree_rows, head), low),
@@ -1512,14 +1845,16 @@
             pltpu.VMEM((tree_rows, head), full),
             pltpu.SemaphoreType.DMA((copies,)),
             pltpu.SemaphoreType.DMA((copies,)),
-            pltpu.SemaphoreType.DMA((1,)),
+            pltpu.SemaphoreType.DMA((3,)),
+            pltpu.SemaphoreType.DMA((GATHER_COPIES,)),
+            pltpu.SemaphoreType.DMA((GATHER_COPIES,)),
         ]
         + scatter_scratch(rows, width),
         compiler_params=remote_params(4),
         cost_estimate=pl.CostEstimate(
             flops=10 * tree_rows * head * width, bytes_accessed=20 * 2**20, transcendentals=0
         ),
-    )(own, cos, sin, query_bits, key_bits, weights, output_weight, queries, keys, values, attended, mass)
+    )(own, cos, sin, query_bits, key_bits, weights, output_weight, queries, keys, values, attended, mass, stream, gain[None], middle_back, normed, mid_near, ffn_own)
 
 
 def shards_heads(
@@ -1540,7 +1875,6 @@
     feedforward_gain,
     feedforward_post_gain,
 ):
-    low = jnp.bfloat16
     row_count, model_width = hidden_in.shape
     shard = lax.axis_index("shard")
     row_start = shard * row_count
@@ -1549,9 +1883,20 @@
     query_bits = ((1 << token_segment) | (1 << parent_tok) | (1 << grand_tok))[:, None]
     cos_table, sin_table = rope_tables(position, HEAD)
     cos_table, sin_table = cos_table[:, 0, : HEAD // 2], sin_table[:, 0, : HEAD // 2]
-    valid_rows = lax.dynamic_slice_in_dim(token_valid, row_start, row_count).astype(jnp.float32)
-    stream = hidden_in.astype(jnp.float32)
-    normed_in, queries, keys, values, attended, mass, attention_pre = attention_forward(
+    valid_rows = lax.dynamic_slice_in_dim(token_valid, row_start, row_count)
+    valid_rows = valid_rows.astype(jnp.float32)[:, None]
+    (
+        normed_in,
+        queries,
+        keys,
+        values,
+        attended,
+        mass,
+        attention_pre,
+        middle,
+        normed_mid,
+        first_sums,
+    ) = attention_forward(
         hidden_in,
         attention_gain,
         cos_table,
@@ -1562,33 +1907,49 @@
         key_weight,
         value_weight,
         output_weight,
-    )
-    attention_branch = norm_rows(attention_pre, attention_post_gain)
-    middle = stream + attention_branch
-    normed_mid = norm_rows(middle, feedforward_gain).astype(low)
-    mid_tree, hidden, mix, gelu_value, mid_every, feedforward_pre = feedforward_forward(
-        normed_mid, gate_weight, up_weight, down_weight
-    )
-    feedforward_branch = norm_rows(feedforward_pre, feedforward_post_gain)
-    result = middle + feedforward_branch
-    squares = jnp.stack(
-        [
-            jnp.sum(valid_rows[:, None] * summand * summand)
-            for summand in (stream, attention_branch, feedforward_branch, result)
-        ]
-    )
-    valid_total = jnp.sum(valid_rows) * model_width
-    seed_grad = cotangent.astype(jnp.float32) * valid_rows[:, None]
-    ffpre_back, grad_four = norm_back(feedforward_pre, feedforward_post_gain, seed_grad)
-    ffpre_low = ffpre_back.astype(low)
-    ffpre_tree, gate_back, up_back, ffpre_every, mid_back = feedforward_backward(
-        ffpre_low, gate_weight, up_weight, down_weight, mix, gelu_value
-    )
-    middle_part, grad_three = norm_back(middle, feedforward_gain, mid_back)
-    middle_back = seed_grad + middle_part
-    attention_pre_back, grad_two = norm_back(attention_pre, attention_post_gain, middle_back)
-    pre_tree, projection_back, normed_back = attention_backward(
-        attention_pre_back.astype(low),
+        attention_post_gain,
+        feedforward_gain,
+        valid_rows,
+    )
+    mid_tree, hidden, mix, gelu_value, mid_near, block_out, ffpre_low, second_sums = (
+        feedforward_forward(
+            normed_mid,
+            middle,
+            cotangent,
+            valid_rows,
+            feedforward_post_gain,
+            gate_weight,
+            up_weight,
+            down_weight,
+        )
+    )
+    ffpre_tree, gate_back, up_back, mid_far, middle_back, pre_low, third_sums = (
+        feedforward_backward(
+            ffpre_low,
+            middle,
+            attention_pre,
+            cotangent,
+            valid_rows,
+            feedforward_gain,
+            attention_post_gain,
+            normed_mid,
+            gate_weight,
+            up_weight,
+            down_weight,
+            mix,
+            gelu_value,
+        )
+    )
+    (
+        pre_tree,
+        mid_begun,
+        ffpre_every,
+        projection_back,
+        attention_grads,
+        input_grad,
+        fourth_sums,
+    ) = attention_backward(
+        pre_low,
         cos_table,
         sin_table,
         query_bits,
@@ -1600,22 +1961,21 @@
         values,
         attended,
         mass,
-    )
-    stream_part, grad_one = norm_back(stream, attention_gain, normed_back)
-    input_grad = middle_back + stream_part
-    attention_grads = jnp.concatenate(
-        [
-            dot_tn(projection_back, normed_in),
-            dot_tn(attended, pre_tree),
-        ]
-    ).astype(low)
+        hidden_in,
+        attention_gain,
+        middle_back,
+        normed_in,
+        mid_near,
+        ffpre_low,
+    )
     attention_grads = lax.psum(attention_grads, "replica").astype(jnp.float32)
     sizes = [query_weight.shape[0], key_weight.shape[0], value_weight.shape[0]]
     query_sum, key_sum, value_sum, output_sum = jnp.split(
         attention_grads, [sizes[0], sizes[0] + sizes[1], sum(sizes)]
     )
     gate_sum, up_sum, down_sum = feedforward_grads(
-        mid_every,
+        mid_near,
+        mid_far,
         ffpre_every,
         mid_tree,
         ffpre_tree,
@@ -1625,15 +1985,20 @@
         gate_weight,
         up_weight,
         down_weight,
-    )
-    extras = jnp.pad(jnp.append(squares, valid_total), (0, model_width - 5))
-    smalls = jnp.stack([grad_one, grad_two, grad_three, grad_four, extras])
+        mid_begun,
+    )
+    valid_total = jnp.full((1, model_width), jnp.sum(valid_rows))
+    smalls = jnp.concatenate(
+        [fourth_sums[:1], third_sums[:2], second_sums[:3], first_sums[:2], valid_total]
+    )
     smalls = jnp.sum(lax.all_gather(smalls, ("replica", "shard")), axis=0)
-    gain_one, gain_two, gain_three, gain_four = smalls[0], smalls[1], smalls[2], smalls[3]
-    squares_all, valid_all = smalls[4, :4], smalls[4, 4]
+    gain_one, gain_three, gain_two, gain_four = smalls[0], smalls[1], smalls[2], smalls[3]
+    totals = jnp.sum(smalls[4:], axis=1)
+    squares_all = jnp.stack([totals[2], totals[3], totals[0], totals[1]])
+    valid_all = totals[4]
     stream_rms = jnp.sqrt(squares_all / valid_all)
     return (
-        result.astype(low),
+        block_out,
         input_grad,
         query_sum,
         key_sum,
@@ -1651,7 +2016,7 @@
 
 
 def solution(mesh):
-    heads_fit = mesh.shape["shard"] == HEADS
+    heads_fit = mesh.shape["shard"] == HEADS and mesh.shape["replica"] > 2
     return jax.shard_map(
         shards_heads if heads_fit else shards_generic,
         mesh=mesh,

time: 725 us -> 692 us (0.954)
  other arithmetic: 45.4 us -> 15.9 us
  matrix products: 12.5 us -> 0 us
    reduce_sum x8 -> x2, other arithmetic: 19.8 us -> 1.51 us  [the longest x1 1.37 us: shards_heads(): valid_total = jnp.full((1, model_width), jnp.sum(valid_rows))]
    pallas_call x1, Pallas kernels: 84.5 us -> 100 us  [attention_backward(): pl.pallas_call(functools.partial(attention_backward_kernel, replicas), ou...]
    pallas_call x1, Pallas kernels: 268 us -> 252 us  [feedforward_grads(): pl.pallas_call(functools.partial(grads_kernel, replicas), out_shape=(grad...]
    dot_general x2 -> x0, matrix products: 12.5 us -> none  [dot_tn(): lax.dot_general(left, right, (((0,), (0,)), ((), ())), preferred_element_...]
    unnamed x51 -> x33, local copies, waits for them, and re-layouts: 22.6 us -> 24.4 us
  transfers between devices with their start and end apart: 2 -> 2, of which waited for: 0 -> 0; matrix products, arithmetic and copies ran while one was open for 3% -> 1% of each run, Pallas kernels for 37% -> 37%
where the time goes in v4:
time: 692 us; the launch traced here: 684 us
  Pallas kernels  611 us (88%)
  local copies, waits for them, and re-layouts  40.8 us (6%)
  between operations  16.1 us (2%)
  other arithmetic  15.9 us (2%)
    pallas_call x1, Pallas kernels, feedforward_grads(): pl.pallas_call(functools.partial(grads_kernel, replicas), out_shape=(grad...  252 us
    pallas_call x1, Pallas kernels, attention_backward(): pl.pallas_call(functools.partial(attention_backward_kernel, replicas), ou...  100 us
    pallas_call x1, Pallas kernels, feedforward_forward(): pl.pallas_call(functools.partial(forward_kernel, replicas), out_shape=(ja...  87.9 us
    pallas_call x1, Pallas kernels, attention_forward(): pl.pallas_call(attention_forward_kernel, out_shape=(jax.ShapeDtypeStruct(...  85.3 us
    pallas_call x1, Pallas kernels, feedforward_backward(): pl.pallas_call(functools.partial(backward_kernel, replicas), out_shape=(j...  85.2 us
    unnamed x33, local copies, waits for them, and re-layouts  24.4 us
  transfers between devices with their start and end apart: 2, of which 0 were waited for; matrix products, arithmetic and copies ran while one was open for 1% of the time, Pallas kernels for 37%

profile of v4, /device:TPU:0, one launch (start us, length us, event | category | flops | bytes accessed | tf_op | source)
XLA Modules:
  0.0 684.1 jit_solution(10328794422499228876)
XLA Ops:
  8.0 0.0 copy-start.7
  8.0 0.0 copy-start.8
  8.0 0.0 copy-start.9
  8.0 0.0 copy-start.10
  8.1 0.0 copy-start.2
  8.1 0.0 copy-start.4
  8.1 0.0 copy-start.5
  8.1 0.0 all-reduce.2.cloned.1.call-start
  8.2 1.0 select_reduce_fusion.5
  9.2 1.0 select_reduce_fusion.1
  10.1 0.8 select_reduce_fusion.6
  10.9 0.7 fusion.8
  11.6 0.8 select_reduce_fusion.2
  12.4 0.3 multiply_bitcast_fusion
  12.7 3.6 fusion.4
  16.3 0.7 compare_select_fusion
  17.0 1.1 broadcast_in_dim.61.query_bits
  18.1 0.6 broadcast_in_dim.29.key_bits
  18.7 1.4 fusion.9
  20.1 0.8 copy.42.valid
  20.9 0.0 copy-done.7
  20.9 0.6 broadcast_in_dim.25.gain
  21.5 0.0 copy-done.8
  21.5 0.6 broadcast_in_dim.56.post_gain
  22.1 0.0 copy-done.9
  22.1 0.6 broadcast_in_dim.57.next_gain.gain
  22.7 0.0 copy-done.10
  22.7 0.6 broadcast_in_dim.59.gain
  23.3 0.0 copy-done.2
  23.3 0.0 copy-done.4
  23.3 0.0 copy-done.5
  23.3 1.6 pad_maximum_fusion.weights
  24.9 85.3 %shard_map.263 = (bf16[1536,2304]{1,0:T(8,128)(2,1)}, bf16[1536,256]{1,0:T(8,128)(2,1)}, bf16[1536,256]{1,0:T(8,128)(2,1)}, bf16[1536,256]{1,0:T(8,128)(2,1)}, b...) custom-call(bf16[192,2304]{1,0:T(8,128)(2,1)} %stream.3, ...), custom_call_target="tpu_custom_call" | custom-call | flops 9059696640 | bytes 20971520 | tf_op jit(solution)/shard_map/pallas_call | solution.py:1598
  110.2 87.9 %shard_map.264 = (bf16[1536,2304]{1,0:T(8,128)(2,1)}, bf16[1536,1152]{1,0:T(8,128)(2,1)}, bf16[1536,1152]{1,0:T(8,128)(2,1)}, bf16[1536,1152]{1,0:T(8,128)(2,1)}...) custom-call(bf16[192,2304]{1,0:T(8,128)(2,1)} %get-tuple-element.47., ...), custom_call_target="tpu_custom_call" | custom-call | flops 24461180928 | bytes 41943040 | tf_op jit(solution)/shard_map/pallas_call | solution.py:839
  198.1 85.2 %shard_map.265 = (bf16[1536,2304]{1,0:T(8,128)(2,1)}, bf16[1536,1152]{1,0:T(8,128)(2,1)}, bf16[1536,1152]{1,0:T(8,128)(2,1)}, bf16[1,192,2304]{2,1,0:T(8,128)(2,...) custom-call(bf16[192,2304]{1,0:T(8,128)(2,1)} %get-tuple-element.50.own.ffn_own, ...), custom_call_target="tpu_custom_call" | custom-call | flops 24461180928 | bytes 41943040 | tf_op jit(solution)/shard_map/pallas_call | solution.py:1011
  283.3 100.5 %shard_map.266 = (bf16[1536,2304]{1,0:T(8,128)(2,1)}, bf16[3,1536,2304]{2,1,0:T(8,128)(2,1)}, bf16[3,192,2304]{2,1,0:T(8,128)(2,1)}, bf16[1536,512]{1,0:T(8,128)...) custom-call(bf16[192,2304]{1,0:T(8,128)(2,1)} %get-tuple-element.54.own, ...), custom_call_target="tpu_custom_call" | custom-call | flops 9059696640 | bytes 20971520 | tf_op jit(solution)/shard_map/pallas_call | solution.py:1823
  383.8 0.0 copy-start.6
  383.8 0.0 all-reduce.2.cloned.1.call-update
  383.9 0.0 all-gather.4.cloned.1.call-start
  383.9 0.9 slice.48
  384.8 0.9 slice.49
  385.7 0.0 copy-done.6
  385.7 0.9 slice.51
  386.6 0.7 broadcast_in_dim.60
  387.3 1.3 concatenate.28
  388.6 0.0 all-gather.4.cloned.1.call-update
  388.6 252.3 %shard_map.267 = (f32[1152,2304]{1,0:T(8,128)}, f32[1152,2304]{1,0:T(8,128)}, f32[1152,2304]{1,0:T(8,128)}, bf16[3,1536,2304]{2,1,0:T(8,128)(2,1)}, bf16[3,1536,2304]{2,1,0:T(8,128)(2,1)}) custom-call(bf16[2,192,2304]{2,1,0:T(8,128)(2,1)} %get-tuple-element.62.mid_near, ...), custom_call_target="tpu_custom_call", output_to_operand_aliasing={{3}: (11, {})} | custom-call | flops 171228266496 | bytes 209715200 | tf_op jit(solution)/shard_map/pallas_call | solution.py:1393
  640.9 0.0 all-reduce.2.cloned.1.call-done
  640.9 0.0 copy-start
  640.9 2.9 fusion.11
  643.9 0.0 copy-done
  643.9 2.5 fusion.10
  646.4 2.7 reduce_sum.120
  649.2 0.1 slice_reduce_fusion
  649.3 0.1 fusion.12
  649.4 0.6 slice.59
  650.0 0.7 slice_reduce_fusion.1
  650.6 1.2 fusion.7
  651.9 0.9 copy.53
  652.8 1.2 copy.54
  654.0 9.1 %copy.55 = f32[1152,2304]{1,0:T(8,128)} copy(f32[1152,2304]{1,0:T(8,128)} %get-tuple-element.122) | data formatting | bytes 21233664
  663.1 9.0 %copy.56 = f32[1152,2304]{1,0:T(8,128)} copy(f32[1152,2304]{1,0:T(8,128)} %get-tuple-element.123) | data formatting | bytes 21233664
  672.1 0.0 slice-done.1
  672.1 4.1 copy.57
  (14 shorter events, 0.0 us)
Async XLA Ops:
  8.0 12.9 %copy-start.7 = (f32[2304]{0:T(1024)S(1)}, f32[2304]{0:T(1024)}, u32[]{:S(2)}) copy-start(f32[2304]{0:T(1024)} %param.28) | copy-start | bytes 27652
  8.0 13.5 %copy-start.8 = (f32[2304]{0:T(1024)S(1)}, f32[2304]{0:T(1024)}, u32[]{:S(2)}) copy-start(f32[2304]{0:T(1024)} %param.29) | copy-start | bytes 27652
  8.0 14.1 %copy-start.9 = (f32[2304]{0:T(1024)S(1)}, f32[2304]{0:T(1024)}, u32[]{:S(2)}) copy-start(f32[2304]{0:T(1024)} %param.30) | copy-start | bytes 27652
  8.0 14.7 %copy-start.10 = (f32[2304]{0:T(1024)S(1)}, f32[2304]{0:T(1024)}, u32[]{:S(2)}) copy-start(f32[2304]{0:T(1024)} %param.31) | copy-start | bytes 27652
  8.1 15.3 %copy-start.2 = (bf16[256,2304]{1,0:T(8,128)(2,1)S(1)}, bf16[256,2304]{1,0:T(8,128)(2,1)}, u32[]{:S(2)}) copy-start(bf16[256,2304]{1,0:T(8,128)(2,1)} %query_w.1) | copy-start | bytes 3538948
  8.1 15.3 %copy-start.4 = (bf16[128,2304]{1,0:T(8,128)(2,1)S(1)}, bf16[128,2304]{1,0:T(8,128)(2,1)}, u32[]{:S(2)}) copy-start(bf16[128,2304]{1,0:T(8,128)(2,1)} %key_own.1) | copy-start | bytes 1769476
  8.1 15.3 %copy-start.5 = (bf16[128,2304]{1,0:T(8,128)(2,1)S(1)}, bf16[128,2304]{1,0:T(8,128)(2,1)}, u32[]{:S(2)}) copy-start(bf16[128,2304]{1,0:T(8,128)(2,1)} %value_own.1) | copy-start | bytes 1769476
  8.1 632.8 %all-reduce.2.cloned.1.call-start = ((), (), s32[]{:S(2)}) async-start(), calls=%async_computation | async-start | bytes 7077888 | tf_op jit(solution)/shard_map/psum | solution.py:1971
  383.8 1.9 copy-start.6
  383.9 262.5 %all-gather.4.cloned.1.call-start = ((), (), s32[]{:S(2)}) async-start(), calls=%async_computation.1 | async-start | bytes 4866048 | tf_op jit(solution)/shard_map/all_gather | solution.py:1994
  640.9 3.0 copy-start
  646.4 5.5 copy-start.3
  646.4 6.4 copy-start.1
  654.0 18.1 %slice-start = ((s8[10616832]{0:T(1024)(128)(4,1)}), s8[4194304]{0:T(1024)(128)(4,1)S(1)}, s32[]{:S(2)}) async-start(s8[10616832]{0:T(1024)(128)(4,1)} %bitcast.28), calls=%async_computation.2 | async-start | bytes 8388608
  654.0 18.1 %slice-start.1 = ((s8[10616832]{0:T(1024)(128)(4,1)}), s8[4194304]{0:T(1024)(128)(4,1)S(1)}, s32[]{:S(2)}) async-start(s8[10616832]{0:T(1024)(128)(4,1)} %bitcast.28), calls=%async_computation.3 | async-start | bytes 8388608
  663.1 9.0 %slice-start.2 = ((s8[10616832]{0:T(1024)(128)(4,1)}), s8[2228224]{0:T(1024)(128)(4,1)S(1)}, s32[]{:S(2)}) async-start(s8[10616832]{0:T(1024)(128)(4,1)} %bitcast.28), calls=%async_computation.4 | async-start | bytes 4456448
Sparse Core Ops, SparseCore 0:
  384.0 140.1 all-reduce.1
Sparse Core Ops, SparseCore 1:
  388.7 155.0 all-gather.3

commit v5 on v4

--- a/solution.py
+++ b/solution.py
@@ -1123,11 +1123,13 @@
             copy.start()
         self.local().start()
 
-    def forward(self):
+    def turn(self):
         self.first_x.wait_recv()
         self.turn_y.start()
         self.first_y.wait_recv()
         self.turn_x.start()
+
+    def to_mates(self):
         self.rest_x.wait_recv()
         self.mate_x.start()
         self.rest_y.wait_recv()
@@ -1201,7 +1203,7 @@
     low = jnp.bfloat16
     y = lax.div(plane.me, 4)
     others = replicas - 1
-    last = (others + 1) * blocks - 1
+    last = others * blocks + half_blocks - 1
     weights = [
         pltpu.make_async_copy(source, target, weight_sem.at[at])
         for at, (source, target) in enumerate(
@@ -1259,11 +1261,15 @@
             for at, (source, target) in enumerate(((mid_rows, mid), (back_rows, back)))
         ]
 
-    def add(total, dot, lhs, rhs, slot):
-        def tile(columns):
-            total[:, columns] += dot(lhs, rhs[slot, :, columns])
-
-        by_columns(width, tile)
+    def add(total, dot, lhs, rhs, slot, first=False):
+        def part(at):
+            left = lhs[:, at] if dot is dot_tn else lhs[at, :]
+            if first:
+                total[at, :] = dot(left, rhs[slot])
+            else:
+                total[at, :] += dot(left, rhs[slot])
+
+        by_rows(units, part, 384)
 
     events = {}
 
@@ -1274,20 +1280,24 @@
         copy.start()
     for copy in own_loads(0, 0):
         copy.start()
-    for total in (down_sum, gate_sum, up_sum):
-        by_rows(units, lambda at, total=total: total.__setitem__((at, slice(None)), jnp.zeros((at.size, width), jnp.float32)))
     greet(plane.near())
     gathers[0] = gathers[0][1:]
     gathers[0][0].begin()
     for step, pair in enumerate(gathers):
         base = step * blocks
-        event(base + half_blocks - 2, pair[0].forward)
-        event(base + half_blocks, *[gather.forward for gather in pair[1:]])
+        if len(pair) == 1:
+            event(base + 2, pair[0].turn)
+            event(base + 4, pair[0].to_mates)
+        else:
+            event(base + 1, pair[0].turn)
+            event(base + 2, pair[0].to_mates)
+            event(base + 3, pair[1].turn)
+            event(base + 4, pair[1].to_mates)
         if step + 1 < others:
-            event(base + half_blocks, *[gather.begin for gather in gathers[step + 1]])
-        event(base + blocks - 1, *[gather.near_rows for gather in pair])
-        event(base + blocks, *[gather.turned for gather in pair])
-        event(base + blocks + half_blocks - 1, *[gather.far_rows for gather in pair])
+            event(base + 4, *[gather.begin for gather in gathers[step + 1]])
+        event(base + 5, *[gather.near_rows for gather in pair])
+        event(base + 6 + (len(pair) > 1), *[gather.turned for gather in pair])
+        event(base + 8, *[gather.far_rows for gather in pair])
 
     def body(block, carry):
         slot = lax.rem(block, 2)
@@ -1307,8 +1317,8 @@
         def _():
             for copy in other_loads(block, slot):
                 copy.wait()
-            tile = max(t for t in (384, 256, 128) if units % t == 0)
-            for at in range(units // tile):
+            tile = units // 2
+            for at in range(2):
                 there = pl.ds(at * tile, tile)
                 gelu_value, slope = gelu_parts(dot_nt(gate_w[there, :], mid[slot]))
                 up_lin = dot_nt(up_w[there, :], mid[slot])
@@ -1334,11 +1344,13 @@
             for copy in other_loads(block + 1, 1 - slot):
                 copy.start()
 
-        @pl.when(is_own)
-        def _():
-            add(down_sum, dot_tn, own_hidden[slot], back, slot)
-            add(gate_sum, dot_tn, own_gate[slot], mid, slot)
-            add(up_sum, dot_tn, own_up[slot], mid, slot)
+        for first in (True, False):
+
+            @pl.when(block == 0 if first else (block > 0) & is_own)
+            def _(first=first):
+                add(down_sum, dot_tn, own_hidden.at[slot], back, slot, first)
+                add(gate_sum, dot_tn, own_gate.at[slot], mid, slot, first)
+                add(up_sum, dot_tn, own_up.at[slot], mid, slot, first)
 
         @pl.when(block >= blocks)
         def _():
@@ -1350,7 +1362,7 @@
                     (up_sum, up_back, mid, up_out),
                 )
             ):
-                add(total, dot_nn, lhs[...], rhs, slot)
+                add(total, dot_nn, lhs, rhs, slot)
                 stores.append(pltpu.make_async_copy(total, out, weight_sem.at[3 + at]))
                 pl.when(block == last)(stores[-1].start)
 
@@ -1427,7 +1439,120 @@
         up_w,
         down_w,
         mid_begun,
-    )[:3]
+    )
+
+
+def last_kernel(
+    start_ref,
+    mid_ref,
+    back_ref,
+    gate_hbm,
+    up_hbm,
+    down_hbm,
+    gate_so_far,
+    up_so_far,
+    down_so_far,
+    gate_out,
+    up_out,
+    down_out,
+    gate_sum,
+    up_sum,
+    down_sum,
+    gate_w,
+    up_w,
+    down_w,
+    hidden,
+    gate_back,
+    up_back,
+    sems,
+):
+    step = pl.program_id(0)
+    final = step == pl.num_programs(0) - 1
+    units = gate_w.shape[0]
+    low = jnp.bfloat16
+    weights = [
+        pltpu.make_async_copy(source, target, sems.at[at])
+        for at, (source, target) in enumerate(
+            ((gate_hbm, gate_w), (up_hbm, up_w), (down_hbm, down_w))
+        )
+    ]
+    sums = [
+        pltpu.make_async_copy(source, target, sems.at[3 + at])
+        for at, (source, target) in enumerate(
+            ((down_so_far, down_sum), (gate_so_far, gate_sum), (up_so_far, up_sum))
+        )
+    ]
+
+    @pl.when(step == 0)
+    def _():
+        for copy in weights:
+            copy.start()
+        for copy in weights:
+            copy.wait()
+        for copy in sums:
+            copy.start()
+
+    tile = units // 2
+    for at in range(2):
+        there = pl.ds(at * tile, tile)
+        gelu_value, slope = gelu_parts(dot_nt(gate_w[there, :], mid_ref[...]))
+        up_lin = dot_nt(up_w[there, :], mid_ref[...])
+        hidden_back = dot_nt(down_w[there, :], back_ref[...]).astype(low).astype(jnp.float32)
+        hidden[there, :] = (gelu_value * up_lin).astype(low)
+        gate_back[there, :] = (hidden_back * up_lin * slope).astype(low)
+        up_back[there, :] = (hidden_back * gelu_value).astype(low)
+    stores = []
+    for at, (total, lhs, rhs, out) in enumerate(
+        (
+            (down_sum, hidden, back_ref, down_out),
+            (gate_sum, gate_back, mid_ref, gate_out),
+            (up_sum, up_back, mid_ref, up_out),
+        )
+    ):
+        pl.when(step == 0)(sums[at].wait)
+
+        def part(at, total=total, lhs=lhs, rhs=rhs):
+            total[at, :] += dot_nn(lhs[at, :], rhs[...])
+
+        by_rows(units, part, 384)
+        stores.append(pltpu.make_async_copy(total, out, sems.at[6 + at]))
+        pl.when(final)(stores[-1].start)
+
+    @pl.when(final)
+    def _():
+        for copy in stores:
+            copy.wait()
+
+
+def last_grads(gate_sum, up_sum, down_sum, mid_rows, back_rows, gate_w, up_w, down_w):
+    trees, tree_rows, width = mid_rows.shape
+    units = gate_w.shape[0]
+    size = tree_rows // 6
+    low, full = jnp.bfloat16, jnp.float32
+    start = (3 * (1 - lax.axis_index("shard") // 4)).reshape(1)
+
+    def block(step, start_ref):
+        return trees - 1, start_ref[0] + step, 0
+
+    grad = jax.ShapeDtypeStruct((units, width), full)
+    return pl.pallas_call(
+        last_kernel,
+        grid_spec=pltpu.PrefetchScalarGridSpec(
+            num_scalar_prefetch=1,
+            grid=(3,),
+            in_specs=[pl.BlockSpec((None, size, width), block)] * 2 + any_specs(6),
+            out_specs=tuple(any_specs(3)),
+            scratch_shapes=[pltpu.VMEM((units, width), full)] * 3
+            + [pltpu.VMEM((units, width), low)] * 3
+            + [pltpu.VMEM((units, size), low)] * 3
+            + [pltpu.SemaphoreType.DMA((9,))],
+        ),
+        out_shape=(grad, grad, grad),
+        compiler_params=pltpu.CompilerParams(vmem_limit_bytes=VMEM_BYTES),
+        cost_estimate=pl.CostEstimate(
+            flops=6 * tree_rows * units * width, bytes_accessed=90 * 2**20, transcendentals=0
+        ),
+    )(start, mid_rows, back_rows, gate_w, up_w, down_w, gate_sum, up_sum, down_sum)
 
 
 def turn(values, cos, sin):
@@ -1657,9 +1782,13 @@
     values,
     attended,
     mass,
-    stream,
     gain,
-    middle_back,
+    valid,
+    first_sums,
+    second_sums,
+    third_sums,
+    stream_hbm,
+    middle_back_hbm,
     normed_hbm,
     mid_near,
     ffn_own,
@@ -1773,7 +1902,8 @@
         return dot_nn(back_out[block_at(chip * block, block), :], weights[:, columns])
 
     def projection_grads():
-        mid_gather.forward()
+        mid_gather.turn()
+        mid_gather.to_mates()
         normed_load.wait()
 
         def tile(columns):
@@ -1793,6 +1923,14 @@
         wires, plane, scratch, product, total, meanwhile=(projection_grads, output_grads)
     )
     sums_out[...] = jnp.zeros_like(sums_out)
+
+    stream, middle_back = scratch[2].at[0], scratch[0].at[1]
+    late = [
+        load(stream_hbm, stream, local_sem.at[3]),
+        load(middle_back_hbm, middle_back, local_sem.at[4]),
+    ]
+    for copy in late:
+        copy.wait()
 
     def input_rows(at):
         back, gain_terms = norm_back(stream[at, :].astype(full), gain[...], total[at, :])
@@ -1800,6 +1938,10 @@
         add_row(sums_out, 0, gain_terms)
 
     by_rows(rows, input_rows)
+    sums_out[1:3, :] = third_sums[0:2, :]
+    sums_out[3:6, :] = second_sums[0:3, :]
+    sums_out[6:8, :] = first_sums[0:2, :]
+    sums_out[8:9, :] = jnp.broadcast_to(jnp.sum(valid[...], axis=0, keepdims=True), (1, width))
     mid_gather.near_rows()
     mid_gather.far_rows()
     mid_gather.finish()
@@ -1812,7 +1954,7 @@
 
 def attention_backward(
     own, cos, sin, query_bits, key_bits, weights, output_weight, queries, keys, values, attended, mass,
-    stream, gain, middle_back, normed, mid_near, ffn_own,
+    stream, gain, middle_back, valid, sums, normed, mid_near, ffn_own,
 ):
     rows, width = own.shape
     head = output_weight.shape[0]
@@ -1829,9 +1971,9 @@
             jax.ShapeDtypeStruct((tree_rows, 2 * head), low),
             jax.ShapeDtypeStruct((3 * head, width), low),
             jax.ShapeDtypeStruct((rows, width), full),
-            jax.ShapeDtypeStruct((8, width), full),
+            jax.ShapeDtypeStruct((16, width), full),
         ),
-        in_specs=vmem_specs(15) + any_specs(3),
+        in_specs=vmem_specs(17) + any_specs(5),
         out_specs=tuple(any_specs(3) + vmem_specs(4)),
         scratch_shapes=[
             pltpu.VMEM((rows, width), full),
@@ -1845,7 +1987,7 @@
             pltpu.VMEM((tree_rows, head), full),
             pltpu.SemaphoreType.DMA((copies,)),
             pltpu.SemaphoreType.DMA((copies,)),
-            pltpu.SemaphoreType.DMA((3,)),
+            pltpu.SemaphoreType.DMA((5,)),
             pltpu.SemaphoreType.DMA((GATHER_COPIES,)),
             pltpu.SemaphoreType.DMA((GATHER_COPIES,)),
         ]
@@ -1854,7 +1996,7 @@
         cost_estimate=pl.CostEstimate(
             flops=10 * tree_rows * head * width, bytes_accessed=20 * 2**20, transcendentals=0
         ),
-    )(own, cos, sin, query_bits, key_bits, weights, output_weight, queries, keys, values, attended, mass, stream, gain[None], middle_back, normed, mid_near, ffn_own)
+    )(own, cos, sin, query_bits, key_bits, weights, output_weight, queries, keys, values, attended, mass, gain[None], valid, *sums, stream, middle_back, normed, mid_near, ffn_own)
 
 
 def shards_heads(
@@ -1947,7 +2089,7 @@
         projection_back,
         attention_grads,
         input_grad,
-        fourth_sums,
+        sums,
     ) = attention_backward(
         pre_low,
         cos_table,
@@ -1964,6 +2106,8 @@
         hidden_in,
         attention_gain,
         middle_back,
+        valid_rows,
+        (first_sums, second_sums, third_sums),
         normed_in,
         mid_near,
         ffpre_low,
@@ -1973,7 +2117,7 @@
     query_sum, key_sum, value_sum, output_sum = jnp.split(
         attention_grads, [sizes[0], sizes[0] + sizes[1], sum(sizes)]
     )
-    gate_sum, up_sum, down_sum = feedforward_grads(
+    gate_sum, up_sum, down_sum, mid_rows, back_rows = feedforward_grads(
         mid_near,
         mid_far,
         ffpre_every,
@@ -1987,11 +2131,10 @@
         down_weight,
         mid_begun,
     )
-    valid_total = jnp.full((1, model_width), jnp.sum(valid_rows))
-    smalls = jnp.concatenate(
-        [fourth_sums[:1], third_sums[:2], second_sums[:3], first_sums[:2], valid_total]
-    )
-    smalls = jnp.sum(lax.all_gather(smalls, ("replica", "shard")), axis=0)
+    gate_sum, up_sum, down_sum = last_grads(
+        gate_sum, up_sum, down_sum, mid_rows, back_rows, gate_weight, up_weight, down_weight
+    )
+    smalls = jnp.sum(lax.all_gather(sums, ("replica", "shard")), axis=0)
     gain_one, gain_three, gain_two, gain_four = smalls[0], smalls[1], smalls[2], smalls[3]
     totals = jnp.sum(smalls[4:], axis=1)
     squares_all = jnp.stack([totals[2], totals[3], totals[0], totals[1]])

time: 692 us -> 669 us (0.967)
  local copies, waits for them, and re-layouts: 40.8 us -> 13.9 us
    pallas_call x0 -> x1, Pallas kernels: none -> 46.9 us  [last_grads(): pl.pallas_call(last_kernel, grid_spec=pltpu.PrefetchScalarGridSpec(num_sc...]
    pallas_call x1, Pallas kernels: 252 us -> 208 us  [feedforward_grads(): pl.pallas_call(functools.partial(grads_kernel, replicas), out_shape=(grad...]
    unnamed x33 -> x22, local copies, waits for them, and re-layouts: 24.4 us -> 2.17 us
  transfers between devices with their start and end apart: 2 -> 2, of which waited for: 0 -> 0; matrix products, arithmetic and copies ran while one was open for 1% -> 1% of each run, Pallas kernels for 37% -> 39%
where the time goes in v5:
time: 669 us; the launch traced here: 661 us
  Pallas kernels  615 us (92%)
  between operations  16.1 us (2%)
  other arithmetic  15.3 us (2%)
  local copies, waits for them, and re-layouts  13.9 us (2%)
    pallas_call x1, Pallas kernels, feedforward_grads(): pl.pallas_call(functools.partial(grads_kernel, replicas), out_shape=(grad...  208 us
    pallas_call x1, Pallas kernels, attention_backward(): pl.pallas_call(functools.partial(attention_backward_kernel, replicas), ou...  102 us
    pallas_call x1, Pallas kernels, feedforward_forward(): pl.pallas_call(functools.partial(forward_kernel, replicas), out_shape=(ja...  87.9 us
    pallas_call x1, Pallas kernels, attention_forward(): pl.pallas_call(attention_forward_kernel, out_shape=(jax.ShapeDtypeStruct(...  85.3 us
    pallas_call x1, Pallas kernels, feedforward_backward(): pl.pallas_call(functools.partial(backward_kernel, replicas), out_shape=(j...  85.2 us
    pallas_call x1, Pallas kernels, last_grads(): pl.pallas_call(last_kernel, grid_spec=pltpu.PrefetchScalarGridSpec(num_sc...  46.9 us
  transfers between devices with their start and end apart: 2, of which 0 were waited for; matrix products, arithmetic and copies ran while one was open for 1% of the time, Pallas kernels for 39%

profile of v5, /device:TPU:0, one launch (start us, length us, event | category | flops | bytes accessed | tf_op | source)
XLA Modules:
  0.0 661.0 jit_solution(6462783606563275802)
XLA Ops:
  8.0 0.0 copy-start.6
  8.0 0.0 copy-start.7
  8.0 0.0 copy-start.8
  8.0 0.0 copy-start.9
  8.1 0.0 copy-start.2
  8.1 0.0 copy-start.4
  8.1 0.0 copy-start.5
  8.1 0.0 all-reduce.2.cloned.1.call-start
  8.2 1.0 select_reduce_fusion.5
  9.2 1.0 select_reduce_fusion.1
  10.1 0.8 select_reduce_fusion.6
  10.9 0.7 fusion.8
  11.6 0.8 select_reduce_fusion.2
  12.4 0.3 multiply_bitcast_fusion
  12.7 3.6 fusion.4
  16.3 0.8 dynamic-slice_convert_fusion
  17.0 0.8 copy.38.valid
  17.8 0.7 compare_select_fusion
  18.5 1.1 broadcast_in_dim.57.query_bits
  19.7 0.6 broadcast_in_dim.27.key_bits
  20.3 0.0 copy-done.6
  20.3 0.6 broadcast_in_dim.23.gain
  20.9 0.0 copy-done.7
  20.9 0.6 broadcast_in_dim.28.post_gain
  21.5 0.0 copy-done.8
  21.5 0.6 broadcast_in_dim.54.next_gain.gain
  22.1 0.0 copy-done.9
  22.1 0.6 broadcast_in_dim.56.gain
  22.7 0.0 copy-done.2
  22.7 0.0 copy-done.4
  22.7 0.0 copy-done.5
  22.7 1.6 pad_maximum_fusion.weights
  24.3 85.3 %shard_map.263 = (bf16[1536,2304]{1,0:T(8,128)(2,1)}, bf16[1536,256]{1,0:T(8,128)(2,1)}, bf16[1536,256]{1,0:T(8,128)(2,1)}, bf16[1536,256]{1,0:T(8,128)(2,1)}, b...) custom-call(bf16[192,2304]{1,0:T(8,128)(2,1)} %stream_hbm.1, ...), custom_call_target="tpu_custom_call" | custom-call | flops 9059696640 | bytes 20971520 | tf_op jit(solution)/shard_map/pallas_call | solution.py:1723
  109.6 87.9 %shard_map.264 = (bf16[1536,2304]{1,0:T(8,128)(2,1)}, bf16[1536,1152]{1,0:T(8,128)(2,1)}, bf16[1536,1152]{1,0:T(8,128)(2,1)}, bf16[1536,1152]{1,0:T(8,128)(2,1)}...) custom-call(bf16[192,2304]{1,0:T(8,128)(2,1)} %get-tuple-element.52., ...), custom_call_target="tpu_custom_call" | custom-call | flops 24461180928 | bytes 41943040 | tf_op jit(solution)/shard_map/pallas_call | solution.py:839
  197.6 85.2 %shard_map.265 = (bf16[1536,2304]{1,0:T(8,128)(2,1)}, bf16[1536,1152]{1,0:T(8,128)(2,1)}, bf16[1536,1152]{1,0:T(8,128)(2,1)}, bf16[1,192,2304]{2,1,0:T(8,128)(2,...) custom-call(bf16[192,2304]{1,0:T(8,128)(2,1)} %get-tuple-element.55.own.ffn_own, ...), custom_call_target="tpu_custom_call" | custom-call | flops 24461180928 | bytes 41943040 | tf_op jit(solution)/shard_map/pallas_call | solution.py:1011
  282.8 101.5 %shard_map.266 = (bf16[1536,2304]{1,0:T(8,128)(2,1)}, bf16[3,1536,2304]{2,1,0:T(8,128)(2,1)}, bf16[3,192,2304]{2,1,0:T(8,128)(2,1)}, bf16[1536,512]{1,0:T(8,128)...) custom-call(bf16[192,2304]{1,0:T(8,128)(2,1)} %get-tuple-element.59.own, ...), custom_call_target="tpu_custom_call" | custom-call | flops 9059696640 | bytes 20971520 | tf_op jit(solution)/shard_map/pallas_call | solution.py:1965
  384.3 0.0 all-reduce.2.cloned.1.call-update
  384.3 0.0 all-gather.3.cloned.1.call-start
  384.4 0.5 all-gather.3.cloned.1.call-update
  384.9 208.2 %shard_map.267 = (f32[1152,2304]{1,0:T(8,128)}, f32[1152,2304]{1,0:T(8,128)}, f32[1152,2304]{1,0:T(8,128)}, bf16[3,1536,2304]{2,1,0:T(8,128)(2,1)}, bf16[3,1536,2304]{2,1,0:T(8,128)(2,1)}) custom-call(bf16[2,192,2304]{2,1,0:T(8,128)(2,1)} %get-tuple-element.70.mid_near, ...), custom_call_target="tpu_custom_call", output_to_operand_aliasing={{3}: (11, {})} | custom-call | flops 171228266496 | bytes 209715200 | tf_op jit(solution)/shard_map/pallas_call | solution.py:1405
  593.1 46.9 %shard_map.268 = (f32[1152,2304]{1,0:T(8,128)}, f32[1152,2304]{1,0:T(8,128)}, f32[1152,2304]{1,0:T(8,128)}) custom-call(s32[1]{0:T(128)} %bitcast.10.start_ref, bf16[3,1536,2304]{2,1,0:T(8,128)(2,1)} %get-tuple-element.81.mid_ref, bf16[3,1536,2304]{2,1,0:T(8,128)(2,1)} %get-tuple-element.82.back_ref, bf16[1152,2304]{1,0:T(8,128)(2,1)} %gate_hbm.7, ...), custom_call_target="tpu_custom_call" | custom-call | flops 24461180928 | bytes 94371840 | tf_op jit(solution)/shard_map/pallas_call | solution.py:1538
  640.1 0.0 all-reduce.2.cloned.1.call-done
  640.1 0.0 copy-start
  640.1 2.9 fusion.10
  643.0 0.0 copy-done
  643.0 2.5 fusion.9
  645.6 0.0 copy-start.3
  645.6 0.0 copy-start.1
  645.6 0.0 all-gather.3.cloned.1.call-done
  645.6 2.7 reduce_sum.110
  648.3 0.1 slice_reduce_fusion
  648.4 0.1 fusion.11
  648.5 0.6 slice.43
  649.1 0.7 slice_reduce_fusion.1
  649.8 1.2 fusion.7
  651.0 0.0 copy-done.3
  651.0 0.9 copy.47
  651.9 0.0 copy-done.1
  651.9 1.2 copy.48
  (2 shorter events, 0.0 us)
Async XLA Ops:
  8.0 12.3 %copy-start.6 = (f32[2304]{0:T(1024)S(1)}, f32[2304]{0:T(1024)}, u32[]{:S(2)}) copy-start(f32[2304]{0:T(1024)} %param.28) | copy-start | bytes 27652
  8.0 12.9 %copy-start.7 = (f32[2304]{0:T(1024)S(1)}, f32[2304]{0:T(1024)}, u32[]{:S(2)}) copy-start(f32[2304]{0:T(1024)} %param.29) | copy-start | bytes 27652
  8.0 13.5 %copy-start.8 = (f32[2304]{0:T(1024)S(1)}, f32[2304]{0:T(1024)}, u32[]{:S(2)}) copy-start(f32[2304]{0:T(1024)} %param.30) | copy-start | bytes 27652
  8.0 14.1 %copy-start.9 = (f32[2304]{0:T(1024)S(1)}, f32[2304]{0:T(1024)}, u32[]{:S(2)}) copy-start(f32[2304]{0:T(1024)} %param.31) | copy-start | bytes 27652
  8.1 14.7 %copy-start.2 = (bf16[256,2304]{1,0:T(8,128)(2,1)S(1)}, bf16[256,2304]{1,0:T(8,128)(2,1)}, u32[]{:S(2)}) copy-start(bf16[256,2304]{1,0:T(8,128)(2,1)} %query_w.1) | copy-start | bytes 3538948
  8.1 14.7 %copy-start.4 = (bf16[128,2304]{1,0:T(8,128)(2,1)S(1)}, bf16[128,2304]{1,0:T(8,128)(2,1)}, u32[]{:S(2)}) copy-start(bf16[128,2304]{1,0:T(8,128)(2,1)} %key_own.1) | copy-start | bytes 1769476
  8.1 14.7 %copy-start.5 = (bf16[128,2304]{1,0:T(8,128)(2,1)S(1)}, bf16[128,2304]{1,0:T(8,128)(2,1)}, u32[]{:S(2)}) copy-start(bf16[128,2304]{1,0:T(8,128)(2,1)} %value_own.1) | copy-start | bytes 1769476
  8.1 632.0 %all-reduce.2.cloned.1.call-start = ((), (), s32[]{:S(2)}) async-start(), calls=%async_computation | async-start | bytes 7077888 | tf_op jit(solution)/shard_map/psum | solution.py:2115
  384.3 261.2 %all-gather.3.cloned.1.call-start = ((), (), s32[]{:S(2)}) async-start(), calls=%async_computation.1 | async-start | bytes 4866048 | tf_op jit(solution)/shard_map/all_gather | solution.py:2137
  640.1 3.0 copy-start
  645.6 5.5 copy-start.3
  645.6 6.4 copy-start.1
Sparse Core Ops, SparseCore 0:
  384.5 140.1 all-reduce.1
Sparse Core Ops, SparseCore 1:
  387.7 156.0 all-gather.2

commit v6 on v5

--- a/solution.py
+++ b/solution.py
@@ -1269,7 +1269,7 @@
             else:
                 total[at, :] += dot(left, rhs[slot])
 
-        by_rows(units, part, 384)
+        by_rows(units, part, 384 if dot is dot_tn else units // 2)
 
     events = {}
 
@@ -1514,7 +1514,7 @@
         def part(at, total=total, lhs=lhs, rhs=rhs):
             total[at, :] += dot_nn(lhs[at, :], rhs[...])
 
-        by_rows(units, part, 384)
+        by_rows(units, part, units // 2)
         stores.append(pltpu.make_async_copy(total, out, sems.at[6 + at]))
         pl.when(final)(stores[-1].start)
 

time: 669 us -> 660 us (0.987)
  Pallas kernels: 615 us -> 606 us
    pallas_call x1, Pallas kernels: 208 us -> 200 us  [feedforward_grads(): pl.pallas_call(functools.partial(grads_kernel, replicas), out_shape=(grad...]
  transfers between devices with their start and end apart: 2 -> 2, of which waited for: 0 -> 0; matrix products, arithmetic and copies ran while one was open for 1% -> 1% of each run, Pallas kernels for 39% -> 38%
where the time goes in v6:
time: 660 us; the launch traced here: 652 us
  Pallas kernels  606 us (92%)
  between operations  16.1 us (2%)
  other arithmetic  15.3 us (2%)
  local copies, waits for them, and re-layouts  13.9 us (2%)
    pallas_call x1, Pallas kernels, feedforward_grads(): pl.pallas_call(functools.partial(grads_kernel, replicas), out_shape=(grad...  200 us
    pallas_call x1, Pallas kernels, attention_backward(): pl.pallas_call(functools.partial(attention_backward_kernel, replicas), ou...  102 us
    pallas_call x1, Pallas kernels, feedforward_forward(): pl.pallas_call(functools.partial(forward_kernel, replicas), out_shape=(ja...  87.9 us
    pallas_call x1, Pallas kernels, attention_forward(): pl.pallas_call(attention_forward_kernel, out_shape=(jax.ShapeDtypeStruct(...  85.3 us
    pallas_call x1, Pallas kernels, feedforward_backward(): pl.pallas_call(functools.partial(backward_kernel, replicas), out_shape=(j...  85.2 us
    pallas_call x1, Pallas kernels, last_grads(): pl.pallas_call(last_kernel, grid_spec=pltpu.PrefetchScalarGridSpec(num_sc...  46 us
  transfers between devices with their start and end apart: 2, of which 0 were waited for; matrix products, arithmetic and copies ran while one was open for 1% of the time, Pallas kernels for 38%

profile of v6, /device:TPU:0, one launch (start us, length us, event | category | flops | bytes accessed | tf_op | source)
XLA Modules:
  0.0 651.6 jit_solution(3211417428458373352)
XLA Ops:
  8.0 0.0 copy-start.6
  8.0 0.0 copy-start.7
  8.0 0.0 copy-start.8
  8.0 0.0 copy-start.9
  8.1 0.0 copy-start.2
  8.1 0.0 copy-start.4
  8.1 0.0 copy-start.5
  8.1 0.0 all-reduce.2.cloned.1.call-start
  8.2 1.0 select_reduce_fusion.5
  9.2 1.0 select_reduce_fusion.1
  10.1 0.8 select_reduce_fusion.6
  10.9 0.7 fusion.8
  11.6 0.8 select_reduce_fusion.2
  12.4 0.3 multiply_bitcast_fusion
  12.7 3.6 fusion.4
  16.3 0.8 dynamic-slice_convert_fusion
  17.0 0.8 copy.38.valid
  17.8 0.7 compare_select_fusion
  18.5 1.1 broadcast_in_dim.57.query_bits
  19.7 0.6 broadcast_in_dim.27.key_bits
  20.3 0.0 copy-done.6
  20.3 0.6 broadcast_in_dim.23.gain
  20.9 0.0 copy-done.7
  20.9 0.6 broadcast_in_dim.28.post_gain
  21.5 0.0 copy-done.8
  21.5 0.6 broadcast_in_dim.54.next_gain.gain
  22.1 0.0 copy-done.9
  22.1 0.6 broadcast_in_dim.56.gain
  22.7 0.0 copy-done.2
  22.7 0.0 copy-done.4
  22.7 0.0 copy-done.5
  22.7 1.6 pad_maximum_fusion.weights
  24.3 85.3 %shard_map.263 = (bf16[1536,2304]{1,0:T(8,128)(2,1)}, bf16[1536,256]{1,0:T(8,128)(2,1)}, bf16[1536,256]{1,0:T(8,128)(2,1)}, bf16[1536,256]{1,0:T(8,128)(2,1)}, b...) custom-call(bf16[192,2304]{1,0:T(8,128)(2,1)} %stream_hbm.1, ...), custom_call_target="tpu_custom_call" | custom-call | flops 9059696640 | bytes 20971520 | tf_op jit(solution)/shard_map/pallas_call | solution.py:1723
  109.6 87.9 %shard_map.264 = (bf16[1536,2304]{1,0:T(8,128)(2,1)}, bf16[1536,1152]{1,0:T(8,128)(2,1)}, bf16[1536,1152]{1,0:T(8,128)(2,1)}, bf16[1536,1152]{1,0:T(8,128)(2,1)}...) custom-call(bf16[192,2304]{1,0:T(8,128)(2,1)} %get-tuple-element.52., ...), custom_call_target="tpu_custom_call" | custom-call | flops 24461180928 | bytes 41943040 | tf_op jit(solution)/shard_map/pallas_call | solution.py:839
  197.6 85.2 %shard_map.265 = (bf16[1536,2304]{1,0:T(8,128)(2,1)}, bf16[1536,1152]{1,0:T(8,128)(2,1)}, bf16[1536,1152]{1,0:T(8,128)(2,1)}, bf16[1,192,2304]{2,1,0:T(8,128)(2,...) custom-call(bf16[192,2304]{1,0:T(8,128)(2,1)} %get-tuple-element.55.own.ffn_own, ...), custom_call_target="tpu_custom_call" | custom-call | flops 24461180928 | bytes 41943040 | tf_op jit(solution)/shard_map/pallas_call | solution.py:1011
  282.8 101.5 %shard_map.266 = (bf16[1536,2304]{1,0:T(8,128)(2,1)}, bf16[3,1536,2304]{2,1,0:T(8,128)(2,1)}, bf16[3,192,2304]{2,1,0:T(8,128)(2,1)}, bf16[1536,512]{1,0:T(8,128)...) custom-call(bf16[192,2304]{1,0:T(8,128)(2,1)} %get-tuple-element.59.own, ...), custom_call_target="tpu_custom_call" | custom-call | flops 9059696640 | bytes 20971520 | tf_op jit(solution)/shard_map/pallas_call | solution.py:1965
  384.3 0.0 all-reduce.2.cloned.1.call-update
  384.3 0.0 all-gather.3.cloned.1.call-start
  384.4 0.5 all-gather.3.cloned.1.call-update
  384.9 199.8 %shard_map.267 = (f32[1152,2304]{1,0:T(8,128)}, f32[1152,2304]{1,0:T(8,128)}, f32[1152,2304]{1,0:T(8,128)}, bf16[3,1536,2304]{2,1,0:T(8,128)(2,1)}, bf16[3,1536,2304]{2,1,0:T(8,128)(2,1)}) custom-call(bf16[2,192,2304]{2,1,0:T(8,128)(2,1)} %get-tuple-element.70.mid_near, ...), custom_call_target="tpu_custom_call", output_to_operand_aliasing={{3}: (11, {})} | custom-call | flops 171228266496 | bytes 209715200 | tf_op jit(solution)/shard_map/pallas_call | solution.py:1405
  584.7 46.0 %shard_map.268 = (f32[1152,2304]{1,0:T(8,128)}, f32[1152,2304]{1,0:T(8,128)}, f32[1152,2304]{1,0:T(8,128)}) custom-call(s32[1]{0:T(128)} %bitcast.10.start_ref, bf16[3,1536,2304]{2,1,0:T(8,128)(2,1)} %get-tuple-element.81.mid_ref, bf16[3,1536,2304]{2,1,0:T(8,128)(2,1)} %get-tuple-element.82.back_ref, bf16[1152,2304]{1,0:T(8,128)(2,1)} %gate_hbm.7, ...), custom_call_target="tpu_custom_call" | custom-call | flops 24461180928 | bytes 94371840 | tf_op jit(solution)/shard_map/pallas_call | solution.py:1538
  630.7 0.0 all-reduce.2.cloned.1.call-done
  630.7 0.0 copy-start
  630.7 2.9 fusion.10
  633.6 0.0 copy-done
  633.7 2.5 fusion.9
  636.2 0.0 copy-start.3
  636.2 0.0 copy-start.1
  636.2 0.0 all-gather.3.cloned.1.call-done
  636.2 2.7 reduce_sum.110
  638.9 0.1 slice_reduce_fusion
  639.0 0.1 fusion.11
  639.1 0.6 slice.43
  639.7 0.7 slice_reduce_fusion.1
  640.4 1.2 fusion.7
  641.6 0.0 copy-done.3
  641.6 0.9 copy.47
  642.5 0.0 copy-done.1
  642.5 1.2 copy.48
  (2 shorter events, 0.0 us)
Async XLA Ops:
  8.0 12.3 %copy-start.6 = (f32[2304]{0:T(1024)S(1)}, f32[2304]{0:T(1024)}, u32[]{:S(2)}) copy-start(f32[2304]{0:T(1024)} %param.28) | copy-start | bytes 27652
  8.0 12.9 %copy-start.7 = (f32[2304]{0:T(1024)S(1)}, f32[2304]{0:T(1024)}, u32[]{:S(2)}) copy-start(f32[2304]{0:T(1024)} %param.29) | copy-start | bytes 27652
  8.0 13.5 %copy-start.8 = (f32[2304]{0:T(1024)S(1)}, f32[2304]{0:T(1024)}, u32[]{:S(2)}) copy-start(f32[2304]{0:T(1024)} %param.30) | copy-start | bytes 27652
  8.0 14.1 %copy-start.9 = (f32[2304]{0:T(1024)S(1)}, f32[2304]{0:T(1024)}, u32[]{:S(2)}) copy-start(f32[2304]{0:T(1024)} %param.31) | copy-start | bytes 27652
  8.1 14.7 %copy-start.2 = (bf16[256,2304]{1,0:T(8,128)(2,1)S(1)}, bf16[256,2304]{1,0:T(8,128)(2,1)}, u32[]{:S(2)}) copy-start(bf16[256,2304]{1,0:T(8,128)(2,1)} %query_w.1) | copy-start | bytes 3538948
  8.1 14.7 %copy-start.4 = (bf16[128,2304]{1,0:T(8,128)(2,1)S(1)}, bf16[128,2304]{1,0:T(8,128)(2,1)}, u32[]{:S(2)}) copy-start(bf16[128,2304]{1,0:T(8,128)(2,1)} %key_own.1) | copy-start | bytes 1769476
  8.1 14.7 %copy-start.5 = (bf16[128,2304]{1,0:T(8,128)(2,1)S(1)}, bf16[128,2304]{1,0:T(8,128)(2,1)}, u32[]{:S(2)}) copy-start(bf16[128,2304]{1,0:T(8,128)(2,1)} %value_own.1) | copy-start | bytes 1769476
  8.1 622.6 %all-reduce.2.cloned.1.call-start = ((), (), s32[]{:S(2)}) async-start(), calls=%async_computation | async-start | bytes 7077888 | tf_op jit(solution)/shard_map/psum | solution.py:2115
  384.3 251.8 %all-gather.3.cloned.1.call-start = ((), (), s32[]{:S(2)}) async-start(), calls=%async_computation.1 | async-start | bytes 4866048 | tf_op jit(solution)/shard_map/all_gather | solution.py:2137
  630.7 3.0 copy-start
  636.2 5.5 copy-start.3
  636.2 6.4 copy-start.1
Sparse Core Ops, SparseCore 0:
  384.5 140.2 all-reduce.1
Sparse Core Ops, SparseCore 1:
  387.7 156.5 all-gather.2
